TPU v7x, 128 devices: a whole 4x4x4 slice. The times are simulated.
128 devices in a mesh: seq: 8 (over z, x_hi), shard: 16 (over y, x_lo, core).
Axes of the slice: x: 4 (x_hi: 2, x_lo: 2; x = x_hi * 2 + x_lo), y: 4, z: 4, core: 2. Of those that a mesh axis runs over, the one named last changes fastest.
Arguments:
- layer_input: bfloat16 [16384, 1024], P(('seq', 'shard')), may hold values from -6 to 6
- attn_gain: bfloat16 [1024], P(('seq', 'shard')), may hold values from 0.5 to 1.5
- moe_gain: bfloat16 [1024], P(('seq', 'shard')), may hold values from 0.5 to 1.5
- w_qkv: bfloat16 [1024, 2048], P(('seq', 'shard')), may hold values from -0.1875 to 0.1875
- w_out: bfloat16 [1024, 1024], P(('seq', 'shard')), may hold values from -4 to 4
- w_gate: bfloat16 [32, 1024, 512], P('shard', 'seq'), may hold values from -0.1875 to 0.1875
- w_up: bfloat16 [32, 1024, 512], P('shard', 'seq'), may hold values from -0.1875 to 0.1875
- w_down: bfloat16 [32, 512, 1024], P('shard', 'seq'), may hold values from -0.5 to 0.5
- routes: int32 [16384, 8], P(('seq', 'shard')), may hold values from 0 to 31, all different within a row; in each aligned block of 128 rows (0 to 127, 128 to 255, ...) at most 40 rows name the same one
- route_weights: float32 [16384, 8], P(('seq', 'shard')), may hold values from 0.05 to 0.4
- cotangent: bfloat16 [16384, 1024], P(('seq', 'shard')), may hold values from -6 to 6
Outputs:
- block_out: bfloat16 [16384, 1024], P(('seq', 'shard'))
- input_grad: bfloat16 [16384, 1024], P(('seq', 'shard'))
- attn_gain_grad: float32 [1024], P(('seq', 'shard'))
- moe_gain_grad: float32 [1024], P(('seq', 'shard'))
- w_qkv_grad: float32 [1024, 2048], P(('seq', 'shard'))
- w_out_grad: float32 [1024, 1024], P(('seq', 'shard'))
- w_gate_grad: float32 [32, 1024, 512], P('shard', 'seq')
- w_up_grad: float32 [32, 1024, 512], P('shard', 'seq')
- w_down_grad: float32 [32, 512, 1024], P('shard', 'seq')
Inputs may be any that keep to these rules, and one draw needn't show every extreme that they name: `routes`: each row names 8 different experts. In the rows of one device no expert is named more than 40 times, and in every draw some expert is named exactly 40 times in some device's rows.
All inputs are finite; a program needn't handle non-finite values.
Results may differ from a plain program's by a relative error of at most 0.029.
Values may be sent and summed in bfloat16 or wider, within the bound.
A program may use at most 128 MiB of HBM per device.

v0:
```python
import math

import jax
import jax.numpy as jnp
from jax import lax
from jax.sharding import PartitionSpec as P

HEADS = 16
KV = 8
HEAD = 64
EXPERTS = 32
TOPK = 8
TOK_DEV = 128
CAP = 40


epsilon = 1e-06
rope_base = 10000.0


def rope_tables(start_pos, position_count):
    half_width = HEAD // 2
    frequency = jnp.exp(
        jnp.arange(half_width, dtype=jnp.float32) * jnp.float32(-2.0 * math.log(rope_base) / HEAD)
    )
    position = (start_pos + jnp.arange(position_count, dtype=jnp.int32)).astype(jnp.float32)
    angles = position[:, None] * frequency[None, :]
    return (jnp.cos(angles)[:, None, :], jnp.sin(angles)[:, None, :])


def rotate(values, cosine_table, sine_table):
    half_width = values.shape[-1] // 2
    first_half = values[..., :half_width]
    second_half = values[..., half_width:]
    return jnp.concatenate(
        [
            first_half * cosine_table - second_half * sine_table,
            second_half * cosine_table + first_half * sine_table,
        ],
        axis=-1,
    )


def stretch_positions(source, head_rows, shard_count):
    within = jnp.arange(head_rows, dtype=jnp.int32)
    return (within // TOK_DEV * shard_count + source) * TOK_DEV + within % TOK_DEV


def tile_plan(seq_count, head_rows):
    for candidate in (4, 2):
        if seq_count % candidate == 0 and head_rows // candidate >= 512:
            return candidate
    return 1


def tile_scores(query_tile, key_tile, query_pos, key_pos, masked, score_scale):
    scores = (
        jnp.einsum("qagd,kad->agqk", query_tile, key_tile, preferred_element_type=jnp.float32)
        * score_scale
    )
    if masked:
        scores = jnp.where(query_pos[:, None] >= key_pos[None, :], scores, -1e30)
    return scores


def norm_back(values, inverse, gain_vector, upstream):
    scaled = upstream * gain_vector
    gain_grad = jnp.sum(upstream * values * inverse, axis=0)
    input_part = inverse * scaled - values * inverse**3 * jnp.mean(
        values * scaled, axis=1, keepdims=True
    )
    return (input_part, gain_grad)


def on_device(
    layer_input,
    attn_gain,
    moe_gain,
    w_qkv,
    w_out,
    w_gate,
    w_up,
    w_down,
    routes,
    route_weights,
    cotangent,
):
    seq_count = lax.axis_size("seq")
    shard_count = lax.axis_size("shard")
    shard_index = lax.axis_index("shard")
    stretch_index = lax.axis_index("seq") * shard_count + shard_index
    width_model = layer_input.shape[1]
    group_size = HEADS // KV
    local_kv = KV // seq_count
    local_q = HEADS // seq_count
    width_q = HEADS * HEAD
    width_kv = KV * HEAD
    key_cols = local_kv * HEAD
    head_rows = TOK_DEV * seq_count
    tile_count = tile_plan(seq_count, head_rows)
    tile_rows = head_rows // tile_count
    score_scale = 1.0 / math.sqrt(HEAD)

    def gather_attention():
        return (
            lax.all_gather(attn_gain, ("seq", "shard"), axis=0, tiled=True),
            lax.all_gather(moe_gain, ("seq", "shard"), axis=0, tiled=True),
            lax.all_gather(w_qkv, ("seq", "shard"), axis=0, tiled=True),
            lax.all_gather(w_out, ("seq", "shard"), axis=0, tiled=True),
        )

    def gather_keys(local_rows):
        return lax.all_gather(local_rows, "shard", axis=0, tiled=True)

    def gather_experts():
        return (
            lax.all_gather(w_gate, "seq", axis=1, tiled=True),
            lax.all_gather(w_up, "seq", axis=1, tiled=True),
            lax.all_gather(w_down, "seq", axis=1, tiled=True),
        )

    def expert_front(rows_in, gate_matrix, up_matrix):
        gate_pre = jnp.einsum(
            "erd,edf->erf", rows_in, gate_matrix, preferred_element_type=jnp.float32
        )
        up_pre = jnp.einsum("erd,edf->erf", rows_in, up_matrix, preferred_element_type=jnp.float32)
        hidden_units = (jax.nn.silu(gate_pre) * up_pre).astype(jnp.bfloat16)
        return (gate_pre, up_pre, hidden_units)

    def split_block(all_rows, source):
        key_block = lax.dynamic_slice_in_dim(all_rows, source * head_rows, head_rows, 0)
        key_heads = key_block[:, :key_cols].reshape(head_rows, local_kv, HEAD)
        value_heads = key_block[:, key_cols:].reshape(head_rows, local_kv, HEAD)
        return (key_heads, value_heads, stretch_positions(source, head_rows, shard_count))

    query_pos = stretch_positions(shard_index, head_rows, shard_count)
    x_wide = layer_input.astype(jnp.float32)
    gain_attn, gain_moe, qkv_weight, out_weight = gather_attention()
    inverse_one = lax.rsqrt(jnp.mean(x_wide * x_wide, axis=1, keepdims=True) + epsilon)
    normed = (x_wide * inverse_one * gain_attn.astype(jnp.float32)).astype(jnp.bfloat16)
    projected = jnp.dot(normed, qkv_weight, preferred_element_type=jnp.float32)
    cosine_table, sine_table = rope_tables(stretch_index * TOK_DEV, TOK_DEV)
    query_rot = rotate(
        projected[:, :width_q].reshape(TOK_DEV, HEADS, HEAD), cosine_table, sine_table
    )
    key_rot = rotate(
        projected[:, width_q : width_q + width_kv].reshape(TOK_DEV, KV, HEAD),
        cosine_table,
        sine_table,
    )
    value_new = projected[:, width_q + width_kv :]
    query_send = query_rot.reshape(TOK_DEV, width_q).astype(jnp.bfloat16)
    memory_send = jnp.concatenate(
        [key_rot, value_new.reshape(TOK_DEV, seq_count, key_cols)], axis=2
    )
    memory_send = memory_send.reshape(TOK_DEV, 2 * width_kv).astype(jnp.bfloat16)
    query_heads, memory_heads = (
        lax.all_to_all(query_send, "seq", split_axis=1, concat_axis=0, tiled=True),
        lax.all_to_all(memory_send, "seq", split_axis=1, concat_axis=0, tiled=True),
    )
    key_rows = gather_keys(memory_heads)
    query_tiles = query_heads.reshape(head_rows, local_kv, group_size, HEAD)

    def peak_pass(source, state_pair):
        row_peak, row_total = state_pair
        key_heads, value_heads, key_pos = split_block(key_rows, source)
        for query_part in range(tile_count):
            query_span = slice(query_part * tile_rows, (query_part + 1) * tile_rows)
            running = row_peak[:, :, query_span]
            summed = row_total[:, :, query_span]
            for key_index in range(query_part + 1):
                key_span = slice(key_index * tile_rows, (key_index + 1) * tile_rows)
                scores = tile_scores(
                    query_tiles[query_span],
                    key_heads[key_span],
                    query_pos[query_span],
                    key_pos[key_span],
                    key_index == query_part,
                    score_scale,
                )
                newest = jnp.maximum(running, jnp.max(scores, axis=-1))
                summed = summed * jnp.exp(running - newest) + jnp.sum(
                    jnp.exp(scores - newest[..., None]), axis=-1
                )
                running = newest
            row_peak = row_peak.at[:, :, query_span].set(running)
            row_total = row_total.at[:, :, query_span].set(summed)
        return (row_peak, row_total)

    start_peak = jnp.full((local_kv, group_size, head_rows), -1e30, jnp.float32)
    start_total = jnp.zeros((local_kv, group_size, head_rows), jnp.float32)
    row_peak, row_total = lax.fori_loop(0, shard_count, peak_pass, (start_peak, start_total))
    log_total = row_peak + jnp.log(row_total)

    def value_pass(source, value_acc):
        key_heads, value_heads, key_pos = split_block(key_rows, source)
        for query_part in range(tile_count):
            query_span = slice(query_part * tile_rows, (query_part + 1) * tile_rows)
            lse_now = log_total[:, :, query_span]
            for key_index in range(query_part + 1):
                key_span = slice(key_index * tile_rows, (key_index + 1) * tile_rows)
                scores = tile_scores(
                    query_tiles[query_span],
                    key_heads[key_span],
                    query_pos[query_span],
                    key_pos[key_span],
                    key_index == query_part,
                    score_scale,
                )
                softmax_weights = jnp.exp(scores - lse_now[..., None]).astype(jnp.bfloat16)
                value_acc = value_acc.at[query_span].add(
                    jnp.einsum(
                        "agqk,kad->qagd",
                        softmax_weights,
                        value_heads[key_span],
                        preferred_element_type=jnp.float32,
                    )
                )
        return value_acc

    value_acc = lax.fori_loop(
        0, shard_count, value_pass, jnp.zeros((head_rows, local_kv, group_size, HEAD), jnp.float32)
    )
    attended_wide = value_acc.reshape(head_rows, local_q * HEAD)
    attended_full = lax.all_to_all(
        attended_wide.astype(jnp.bfloat16), "seq", split_axis=0, concat_axis=1, tiled=True
    )
    residual = x_wide + jnp.dot(attended_full, out_weight, preferred_element_type=jnp.float32)
    inverse_two = lax.rsqrt(jnp.mean(residual * residual, axis=1, keepdims=True) + epsilon)
    gain_moe_wide = gain_moe.astype(jnp.float32)
    normed_moe = (residual * inverse_two * gain_moe_wide).astype(jnp.bfloat16)
    flat_routes = routes.reshape(TOK_DEV * TOPK)
    onehot = (flat_routes[:, None] == jnp.arange(EXPERTS, dtype=jnp.int32)[None, :]).astype(
        jnp.int32
    )
    slot_index = jnp.sum((jnp.cumsum(onehot, axis=0) - 1) * onehot, axis=1)
    slot_place = flat_routes * CAP + slot_index
    route_token = jnp.arange(TOK_DEV * TOPK, dtype=jnp.int32) // TOPK
    send_rows = (
        jnp.zeros((EXPERTS * CAP, width_model), jnp.bfloat16)
        .at[slot_place]
        .set(normed_moe[route_token])
    )
    expert_rows = lax.all_to_all(
        send_rows.reshape(EXPERTS, CAP, width_model),
        "shard",
        split_axis=0,
        concat_axis=1,
        tiled=True,
    )
    gate_weight, up_weight, down_weight = gather_experts()
    gate_pre, up_pre, hidden_units = expert_front(expert_rows, gate_weight, up_weight)
    expert_out = jnp.einsum(
        "erf,efd->erd", hidden_units, down_weight, preferred_element_type=jnp.float32
    ).astype(jnp.bfloat16)
    came_back = lax.all_to_all(expert_out, "shard", split_axis=1, concat_axis=0, tiled=True)
    route_out = came_back.reshape(EXPERTS * CAP, width_model)[slot_place].reshape(
        TOK_DEV, TOPK, width_model
    )
    moe_sum = jnp.sum(route_weights[:, :, None] * route_out.astype(jnp.float32), axis=1)
    block_out = (residual + moe_sum).astype(jnp.bfloat16)
    out_grad = cotangent.astype(jnp.float32)
    route_grad = (
        (route_weights[:, :, None] * out_grad[:, None, :])
        .astype(jnp.bfloat16)
        .reshape(TOK_DEV * TOPK, width_model)
    )
    grad_send = jnp.zeros((EXPERTS * CAP, width_model), jnp.bfloat16).at[slot_place].set(route_grad)
    grad_rows = lax.all_to_all(
        grad_send.reshape(EXPERTS, CAP, width_model),
        "shard",
        split_axis=0,
        concat_axis=1,
        tiled=True,
    )
    gain_attn, gain_moe, qkv_weight, out_weight = gather_attention()
    gain_moe_wide = gain_moe.astype(jnp.float32)
    key_rows = gather_keys(memory_heads)
    gate_weight, up_weight, down_weight = gather_experts()
    gate_pre, up_pre, hidden_units = expert_front(expert_rows, gate_weight, up_weight)
    units_grad = jnp.einsum(
        "erd,efd->erf", grad_rows, down_weight, preferred_element_type=jnp.float32
    )
    down_grad = jnp.einsum(
        "erf,erd->efd", hidden_units, grad_rows, preferred_element_type=jnp.float32
    )
    sigmoid_gate = jax.nn.sigmoid(gate_pre)
    gate_grad = (
        units_grad * up_pre * sigmoid_gate * (1.0 + gate_pre * (1.0 - sigmoid_gate))
    ).astype(jnp.bfloat16)
    up_grad = (units_grad * gate_pre * sigmoid_gate).astype(jnp.bfloat16)
    rows_grad = (
        jnp.einsum("erf,edf->erd", gate_grad, gate_weight, preferred_element_type=jnp.float32)
        + jnp.einsum("erf,edf->erd", up_grad, up_weight, preferred_element_type=jnp.float32)
    ).astype(jnp.bfloat16)
    gate_w_grad = jnp.einsum(
        "erd,erf->edf", expert_rows, gate_grad, preferred_element_type=jnp.float32
    )
    up_w_grad = jnp.einsum("erd,erf->edf", expert_rows, up_grad, preferred_element_type=jnp.float32)
    returned = lax.all_to_all(rows_grad, "shard", split_axis=1, concat_axis=0, tiled=True)
    expert_sums = (
        lax.psum_scatter(
            gate_w_grad.astype(jnp.bfloat16), "seq", scatter_dimension=1, tiled=True
        ).astype(jnp.float32),
        lax.psum_scatter(
            up_w_grad.astype(jnp.bfloat16), "seq", scatter_dimension=1, tiled=True
        ).astype(jnp.float32),
        lax.psum_scatter(
            down_grad.astype(jnp.bfloat16), "seq", scatter_dimension=1, tiled=True
        ).astype(jnp.float32),
    )
    route_back = returned.reshape(EXPERTS * CAP, width_model)[slot_place].reshape(
        TOK_DEV, TOPK, width_model
    )
    moe_in_grad = jnp.sum(route_back.astype(jnp.float32), axis=1)
    moe_part, moe_gain_grad = norm_back(residual, inverse_two, gain_moe_wide, moe_in_grad)
    residual_grad = out_grad + moe_part
    branch_grad = residual_grad.astype(jnp.bfloat16)
    out_proj_grad = jnp.einsum(
        "tc,td->cd", attended_full, branch_grad, preferred_element_type=jnp.float32
    )
    attended_grad = jnp.einsum(
        "td,cd->tc", branch_grad, out_weight, preferred_element_type=jnp.float32
    ).astype(jnp.bfloat16)
    grad_heads = lax.all_to_all(attended_grad, "seq", split_axis=1, concat_axis=0, tiled=True)
    grad_tiles = grad_heads.reshape(head_rows, local_kv, group_size, HEAD)
    row_delta = jnp.sum(grad_tiles.astype(jnp.float32) * value_acc, axis=-1).transpose(1, 2, 0)

    def grad_pass(source, state_pair):
        query_grad, memory_grad = state_pair
        key_heads, value_heads, key_pos = split_block(key_rows, source)
        key_grad = jnp.zeros((head_rows, local_kv, HEAD), jnp.float32)
        value_grad = jnp.zeros((head_rows, local_kv, HEAD), jnp.float32)
        for query_part in range(tile_count):
            query_span = slice(query_part * tile_rows, (query_part + 1) * tile_rows)
            query_now = query_tiles[query_span]
            grad_now = grad_tiles[query_span]
            lse_now = log_total[:, :, query_span]
            delta_now = row_delta[:, :, query_span]
            for key_index in range(query_part + 1):
                key_span = slice(key_index * tile_rows, (key_index + 1) * tile_rows)
                scores = tile_scores(
                    query_now,
                    key_heads[key_span],
                    query_pos[query_span],
                    key_pos[key_span],
                    key_index == query_part,
                    score_scale,
                )
                softmax_weights = jnp.exp(scores - lse_now[..., None])
                value_grad = value_grad.at[key_span].add(
                    jnp.einsum(
                        "agqk,qagd->kad",
                        softmax_weights.astype(jnp.bfloat16),
                        grad_now,
                        preferred_element_type=jnp.float32,
                    )
                )
                weight_grad = jnp.einsum(
                    "qagd,kad->agqk",
                    grad_now,
                    value_heads[key_span],
                    preferred_element_type=jnp.float32,
                )
                score_grad = (softmax_weights * (weight_grad - delta_now[..., None])).astype(
                    jnp.bfloat16
                )
                query_grad = query_grad.at[query_span].add(
                    jnp.einsum(
                        "agqk,kad->qagd",
                        score_grad,
                        key_heads[key_span],
                        preferred_element_type=jnp.float32,
                    )
                    * score_scale
                )
                key_grad = key_grad.at[key_span].add(
                    jnp.einsum(
                        "agqk,qagd->kad", score_grad, query_now, preferred_element_type=jnp.float32
                    )
                    * score_scale
                )
        update = jnp.concatenate(
            [key_grad.reshape(head_rows, key_cols), value_grad.reshape(head_rows, key_cols)], axis=1
        )
        memory_grad = lax.dynamic_update_slice_in_dim(memory_grad, update, source * head_rows, 0)
        return (query_grad, memory_grad)

    start_query = jnp.zeros((head_rows, local_kv, group_size, HEAD), jnp.float32)
    start_memory = jnp.zeros((shard_count * head_rows, 2 * key_cols), jnp.float32)
    query_grad, memory_grad = lax.fori_loop(0, shard_count, grad_pass, (start_query, start_memory))
    memory_sum = lax.psum_scatter(
        memory_grad.astype(jnp.bfloat16), "shard", scatter_dimension=0, tiled=True
    )
    query_back, memory_back = (
        lax.all_to_all(
            query_grad.reshape(head_rows, local_q * HEAD).astype(jnp.bfloat16),
            "seq",
            split_axis=0,
            concat_axis=1,
            tiled=True,
        ),
        lax.all_to_all(memory_sum, "seq", split_axis=0, concat_axis=1, tiled=True),
    )
    memory_back = memory_back.reshape(TOK_DEV, seq_count, 2, key_cols)
    key_back = memory_back[:, :, 0]
    value_back = memory_back[:, :, 1].reshape(TOK_DEV, width_kv)
    query_pre = rotate(
        query_back.astype(jnp.float32).reshape(TOK_DEV, HEADS, HEAD), cosine_table, -sine_table
    )
    key_pre = rotate(key_back.astype(jnp.float32), cosine_table, -sine_table)
    projected_grad = jnp.concatenate(
        [
            query_pre.reshape(TOK_DEV, width_q),
            key_pre.reshape(TOK_DEV, width_kv),
            value_back.astype(jnp.float32),
        ],
        axis=1,
    ).astype(jnp.bfloat16)
    qkv_grad = jnp.einsum("td,tc->dc", normed, projected_grad, preferred_element_type=jnp.float32)
    normed_grad = jnp.einsum(
        "tc,dc->td", projected_grad, qkv_weight, preferred_element_type=jnp.float32
    )
    attn_part, attn_gain_grad = norm_back(
        x_wide, inverse_one, gain_attn.astype(jnp.float32), normed_grad
    )
    input_grad = (residual_grad + attn_part).astype(jnp.bfloat16)
    weight_sums = (
        lax.psum_scatter(attn_gain_grad, ("seq", "shard"), scatter_dimension=0, tiled=True),
        lax.psum_scatter(moe_gain_grad, ("seq", "shard"), scatter_dimension=0, tiled=True),
        lax.psum_scatter(qkv_grad, ("seq", "shard"), scatter_dimension=0, tiled=True),
        lax.psum_scatter(out_proj_grad, ("seq", "shard"), scatter_dimension=0, tiled=True),
    )
    return (
        block_out,
        input_grad,
        weight_sums[0],
        weight_sums[1],
        weight_sums[2],
        weight_sums[3],
        expert_sums[0],
        expert_sums[1],
        expert_sums[2],
    )


def solution(mesh):
    placed = (
        P(("seq", "shard"), None),
        P(("seq", "shard")),
        P(("seq", "shard")),
        P(("seq", "shard"), None),
        P(("seq", "shard"), None),
        P("shard", "seq", None),
        P("shard", "seq", None),
        P("shard", "seq", None),
        P(("seq", "shard"), None),
        P(("seq", "shard"), None),
        P(("seq", "shard"), None),
    )
    return jax.shard_map(
        on_device,
        mesh=mesh,
        in_specs=placed,
        out_specs=(
            P(("seq", "shard"), None),
            P(("seq", "shard"), None),
            P(("seq", "shard")),
            P(("seq", "shard")),
            P(("seq", "shard"), None),
            P(("seq", "shard"), None),
            P("shard", "seq", None),
            P("shard", "seq", None),
            P("shard", "seq", None),
        ),
        check_vma=False,
    )
```

profile of v0, /device:TPU:1, one launch (start us, length us, event | category | flops | bytes accessed | tf_op | source)
XLA Modules:
  0.0 2622.0 jit_solution(6523673316892186500)
XLA Ops:
  9.7 68.8 %all-reduce.7 = (bf16[1024]{0:T(1024)(128)(2,1)S(1)}, bf16[1024]{0:T(1024)(128)(2,1)S(1)}) all-reduce(bf16[1024]{0:T(1024)(128)(2,1)S(1)} %dynamic-update-slice.165, bf16[1024]{0:T(1024)(128)(2,1)S(1)} %dynamic-update-slice.166), channel_id=1, replica_groups=mesh['seq'=8,'shard'=16] {'seq','shard'}, use_global_device_ids=true, to_apply=%add.2 | all-reduce | flops 2048 | bytes 8192
  80.8 129.8 %all-gather.7.cloned.1.call-done = bf16[1024,2048]{1,0:T(8,128)(2,1)} async-done(((bf16[8,2048]{1,0:T(8,128)(2,1)}), bf16[1024,2048]{1,0:T(8,128)(2,1)}) %all-gather.7.cloned.1.call-update) | async-done | bytes 4194320 | tf_op jit(solution)/shard_map/all_gather | solution.py:108
  214.1 12.0 all_to_all.153
  229.2 9.0 reduce-window.6
  243.2 10.3 all-to-all-done.1
  253.8 11.3 all-gather.9.cloned.1.call-done
  265.1 6.4 copy.175
  271.5 96.6 %while.66 = (s32[]{:T(128)}, f32[1,2,1024]{2,1,0:T(2,128)S(1)}, f32[1,2,1024]{2,1,0:T(2,128)S(1)}, s32[1024]{0:T(1024)S(1)}, bf16[16384,128]{0,1:T(8,128)(2,1)},...) while((s32[]{:T(128)}, f32[1,2,1024]{2,1,0:T(2,128)S(1)}, ...), condition=%wide.region_8.9_spmd, body=%wide.region_1.8_spmd.sunk | while | flops 211836928 | bytes 14901439 | solution.py:192
  368.2 89.9 %while.67 = (s32[]{:T(128)}, f32[1024,1,2,64]{0,3,2,1:T(8,128)S(1)}, bf16[16384,128]{0,1:T(8,128)(2,1)}, s32[1024]{0:T(1024)S(1)}, bf16[1024,1,2,64]{0,3,2,1:T(8...) while((s32[]{:T(128)}, ...), condition=%wide.region_10.11_spmd, body=%wide.region_9.10_spmd.sunk | while | flops 409157632 | bytes 3994311 | solution.py:221
  459.0 6.5 all-to-all-start.2
  466.0 7.5 scatter_custom_fusion.1
  474.2 5.2 all-to-all-start.5
  483.1 16.8 scatter_custom_fusion
  499.9 23.4 all-to-all-done.5
  523.4 5.1 all-to-all-start.3
  530.3 34.0 %all-to-all-done.3 = bf16[32,40,1024]{2,1,0:T(8,128)(2,1)} async-done(((bf16[32,40,1024]{2,1,0:T(8,128)(2,1)}), bf16[32,40,1024]{2,1,0:T(8,128)(2,1)}, u32[]{:S(2)}, u32[]{:S(2)}) %all-to-all-start.3) | async-done | bytes 2621472 | tf_op jit(solution)/shard_map/all_to_all | solution.py:244
  566.4 5.6 fusion.240
  572.0 12.0 all-gather.13.cloned.1.call-done
  584.0 4.6 fusion.239
  588.5 49.6 %all-gather.17.cloned.1.call-done = bf16[2,512,1024]{2,1,0:T(8,128)(2,1)} async-done(((bf16[2,64,1024]{2,1,0:T(8,128)(2,1)}), bf16[2,512,1024]{2,1,0:T(8,128)(2,1)}) %all-gather.17.cloned.1.call-update) | async-done | bytes 2097168 | tf_op jit(solution)/shard_map/all_gather | solution.py:119
  638.1 8.1 multiply_convert_fusion
  648.8 4.2 copy.184
  653.1 5.6 all-to-all-start.4
  664.0 4.2 copy.188
  668.2 23.1 all-to-all-done.4
  692.9 5.1 all-to-all-start.6
  700.5 30.4 %all-to-all-done.6 = bf16[2,640,1024]{2,0,1:T(2,128)(2,1)} async-done(((bf16[2,640,1024]{2,0,1:T(2,128)(2,1)}), bf16[2,640,1024]{2,0,1:T(2,128)(2,1)}, u32[]{:S(2)}, u32[]{:S(2)}) %all-to-all-start.6) | async-done | bytes 2621472 | tf_op jit(solution)/shard_map/all_to_all | solution.py:300
  730.9 4.1 copy.189
  735.0 5.4 gather_fusion
  740.4 8.2 gather_fusion.1
  748.6 4.9 convert_reduce_fusion
  756.9 4.0 all-to-all-start.7
  761.1 7.4 all-to-all-done.7
  771.1 258.2 %while.68 = (s32[]{:T(128)}, f32[1024,1,2,64]{0,3,2,1:T(8,128)S(1)}, bf16[16384,128]{1,0:T(8,128)(2,1)}, bf16[16384,128]{0,1:T(8,128)(2,1)}, s32[1024]{0:T(1024)...) while((s32[]{:T(128)}, ...), condition=%wide.region_22.23_spmd, body=%wide.region_21.22_spmd.sunk | while | flops 1019854848 | bytes 38691108 | solution.py:391
  1030.6 4.9 convolution_convert_fusion.1
  1036.8 5.0 convolution_convert_fusion.2
  1043.0 5.0 convolution_convert_fusion.3
  1051.9 11.2 all_to_all.154
  1063.2 32.5 %reduce-scatter.7.cloned.1.call-done = bf16[1024,128]{1,0:T(8,128)(2,1)} async-done(((bf16[16384,128]{1,0:T(8,128)(2,1)}), bf16[1024,128]{1,0:T(8,128)(2,1)}) %reduce-scatter.7.cloned.1.call-update) | async-done | bytes 262160 | tf_op jit(solution)/shard_map/reduce_scatter | solution.py:392
  1095.7 5.7 all-to-all-start.9
  1101.5 7.6 all-to-all-done.9
  1109.4 4.8 fusion.207
  1114.2 59.6 %reduce-scatter.17.cloned.1.call-done = bf16[2,64,1024]{2,1,0:T(8,128)(2,1)} async-done(((bf16[2,512,1024]{2,1,0:T(8,128)(2,1)}), bf16[2,64,1024]{2,1,0:T(8,128)(2,1)}) %reduce-scatter.17.cloned.1.call-update) | async-done | bytes 262160 | tf_op jit(solution)/shard_map/reduce_scatter | solution.py:308
  1175.7 75.8 %reduce-scatter.15.cloned.1.call-done = bf16[2,128,512]{2,1,0:T(8,128)(2,1)} async-done(((bf16[2,1024,512]{2,1,0:T(8,128)(2,1)}), bf16[2,128,512]{2,1,0:T(8,128)(2,1)}) %reduce-scatter.15.cloned.1.call-update) | async-done | bytes 262160 | tf_op jit(solution)/shard_map/reduce_scatter | solution.py:305
  1253.3 75.7 %reduce-scatter.13.cloned.1.call-done = bf16[2,128,512]{2,1,0:T(8,128)(2,1)} async-done(((bf16[2,1024,512]{2,1,0:T(8,128)(2,1)}), bf16[2,128,512]{2,1,0:T(8,128)(2,1)}) %reduce-scatter.13.cloned.1.call-update) | async-done | bytes 262160 | tf_op jit(solution)/shard_map/reduce_scatter | solution.py:302
  1334.6 65.9 %all-reduce.6 = (f32[1024]{0:T(1024)S(1)}, f32[1024]{0:T(1024)S(1)}) all-reduce(f32[1024]{0:T(1024)S(1)} %get-tuple-element.1021, f32[1024]{0:T(1024)S(1)} %get-tuple-element.1019), channel_id=3, replica_groups=mesh['seq'=8,'shard'=16] {'seq','shard'}, use_global_device_ids=true, to_apply=%region_26.27.clone | all-reduce | flops 2048 | bytes 16384
  1402.6 565.4 %reduce-scatter.11.cloned.1.call-done = f32[8,1024]{1,0:T(8,128)} async-done(((f32[1024,1024]{1,0:T(8,128)}), f32[8,1024]{1,0:T(8,128)}) %reduce-scatter.11.cloned.1.call-update) | async-done | bytes 32784 | tf_op jit(solution)/shard_map/reduce_scatter | solution.py:432
  1968.0 646.8 %reduce-scatter.9.cloned.1.call-done = f32[8,2048]{1,0:T(8,128)} async-done(((f32[1024,2048]{1,0:T(8,128)}), f32[8,2048]{1,0:T(8,128)}) %reduce-scatter.9.cloned.1.call-update) | async-done | bytes 65552 | tf_op jit(solution)/shard_map/reduce_scatter | solution.py:431
  (992 shorter events, 503.6 us)
Async XLA Ops:
  7.2 203.5 %all-gather.7.cloned.1.call-start = ((), (), s32[]{:S(2)}) async-start(), calls=%async_computation.16 | async-start | bytes 4227072 | tf_op jit(solution)/shard_map/all_gather | solution.py:108
  7.9 257.2 %all-gather.9.cloned.1.call-start = ((), (), s32[]{:S(2)}) async-start(), calls=%async_computation.17 | async-start | bytes 4456448 | tf_op jit(solution)/shard_map/all_gather | solution.py:113
  78.4 135.3 %copy-start.17 = (f32[1024]{0:T(1024)}, f32[1024]{0:T(1024)S(1)}, u32[]{:S(2)}) copy-start(f32[1024]{0:T(1024)S(1)} %convert_element_type.247) | copy-start | bytes 12292
  80.1 133.7 %copy-start.21 = (f32[128]{0:T(128)}, f32[128]{0:T(128)S(1)}, u32[]{:S(2)}) copy-start(f32[128]{0:T(128)S(1)} %get-tuple-element.1126) | copy-start | bytes 1540
  80.8 158.1 %copy-start.15 = (f32[128,32]{0,1:T(8,128)}, f32[128,32]{0,1:T(8,128)S(1)}, u32[]{:S(2)}) copy-start(f32[128,32]{0,1:T(8,128)S(1)} %get-tuple-element.1124) | copy-start | bytes 49156
  213.7 15.2 copy-start.20
  227.0 253.0 %all-gather.11.cloned.1.call-start = ((), (), s32[]{:S(2)}) async-start(), calls=%async_computation.18 | async-start | bytes 2113536 | tf_op jit(solution)/shard_map/all_gather | solution.py:109
  227.7 338.7 %all-gather.15.cloned.1.call-start = ((), (), s32[]{:S(2)}) async-start(), calls=%async_computation.20 | async-start | bytes 2359296 | tf_op jit(solution)/shard_map/all_gather | solution.py:118
  228.3 355.6 %all-gather.13.cloned.1.call-start = ((), (), s32[]{:S(2)}) async-start(), calls=%async_computation.19 | async-start | bytes 2359296 | tf_op jit(solution)/shard_map/all_gather | solution.py:117
  239.7 13.8 all-to-all-start.1
  458.1 15.4 copy-start.4
  458.1 7.6 copy-start.23
  458.1 7.8 copy-start.13
  459.0 14.6 all-to-all-start.2
  473.5 0.7 copy-start.7
  474.2 49.1 %all-to-all-start.5 = ((bf16[32,40,1024]{2,1,0:T(8,128)(2,1)}), bf16[32,40,1024]{2,1,0:T(8,128)(2,1)S(1)}, u32[]{:S(2)}, u32[]{:S(2)}) async-start(bf16[32,40,1024]{2,1,0:T(8,128)(2,1)} %bitcast.795), calls=%async_computation.5 | async-start | bytes 5242880 | tf_op jit(solution)/shard_map/all_to_all | solution.py:269
  479.4 158.7 %all-gather.17.cloned.1.call-start = ((), (), s32[]{:S(2)}) async-start(), calls=%async_computation.21 | async-start | bytes 2359296 | tf_op jit(solution)/shard_map/all_gather | solution.py:119
  523.4 41.0 %all-to-all-start.3 = ((bf16[32,40,1024]{2,1,0:T(8,128)(2,1)}), bf16[32,40,1024]{2,1,0:T(8,128)(2,1)}, u32[]{:S(2)}, u32[]{:S(2)}) async-start(bf16[32,40,1024]{2,1,0:T(8,128)(2,1)} %bitcast.797), calls=%async_computation.3 | async-start | bytes 5242880 | tf_op jit(solution)/shard_map/all_to_all | solution.py:244
  566.4 17.6 copy-start.6
  638.1 9.2 copy-start.25
  646.2 1.1 copy-start.26
  653.1 38.3 %all-to-all-start.4 = ((bf16[2,640,1024]{2,0,1:T(2,128)(2,1)}), bf16[2,640,1024]{2,0,1:T(2,128)(2,1)S(1)}, u32[]{:S(2)}, u32[]{:S(2)}) async-start(bf16[2,640,1024]{2,0,1:T(2,128)(2,1)} %copy.184), calls=%async_computation.4 | async-start | bytes 5242880 | tf_op jit(solution)/shard_map/all_to_all | solution.py:256
  658.7 3.7 copy-start.9
  658.7 3.7 copy-start.11
  691.3 1.6 copy-start
  692.9 38.0 %all-to-all-start.6 = ((bf16[2,640,1024]{2,0,1:T(2,128)(2,1)}), bf16[2,640,1024]{2,0,1:T(2,128)(2,1)}, u32[]{:S(2)}, u32[]{:S(2)}) async-start(bf16[2,640,1024]{2,0,1:T(2,128)(2,1)} %copy.188), calls=%async_computation.6 | async-start | bytes 5242880 | tf_op jit(solution)/shard_map/all_to_all | solution.py:300
  740.4 8.2 copy-start.2
  748.6 5.1 copy-start.14
  753.6 1.7 copy-start.1
  755.3 13.5 copy-start.5
  756.9 11.6 all-to-all-start.7
  760.8 334.9 %reduce-scatter.7.cloned.1.call-start = ((), (), s32[]{:S(2)}) async-start(), calls=%async_computation.22 | async-start | bytes 4456448 | tf_op jit(solution)/shard_map/reduce_scatter | solution.py:392
  1029.2 1.3 copy-start.27
  1029.3 144.6 %reduce-scatter.17.cloned.1.call-start = ((), (), s32[]{:S(2)}) async-start(), calls=%async_computation.27 | async-start | bytes 2359296 | tf_op jit(solution)/shard_map/reduce_scatter | solution.py:308
  1035.4 1.3 copy-start.12
  1035.5 216.1 %reduce-scatter.15.cloned.1.call-start = ((), (), s32[]{:S(2)}) async-start(), calls=%async_computation.26 | async-start | bytes 2359296 | tf_op jit(solution)/shard_map/reduce_scatter | solution.py:305
  1041.7 1.3 copy-start.10
  1041.7 287.3 %reduce-scatter.13.cloned.1.call-start = ((), (), s32[]{:S(2)}) async-start(), calls=%async_computation.25 | async-start | bytes 2359296 | tf_op jit(solution)/shard_map/reduce_scatter | solution.py:302
  1048.1 0.9 copy-start.8
  1048.1 919.9 %reduce-scatter.11.cloned.1.call-start = ((), (), s32[]{:S(2)}) async-start(), calls=%async_computation.24 | async-start | bytes 4227072 | tf_op jit(solution)/shard_map/reduce_scatter | solution.py:432
  1051.8 49.6 %copy-start.16 = (f32[128,32]{0,1:T(8,128)S(1)}, f32[128,32]{0,1:T(8,128)}, u32[]{:S(2)}) copy-start(f32[128,32]{0,1:T(8,128)} %copy-done.15) | copy-start | bytes 49156
  1051.8 49.6 %copy-start.19 = (f32[128,32]{0,1:T(8,128)S(1)}, f32[128,32]{0,1:T(8,128)}, u32[]{:S(2)}) copy-start(f32[128,32]{0,1:T(8,128)} %get-tuple-element.1122) | copy-start | bytes 49156
  1063.1 46.3 %copy-start.3 = (bf16[128,1024]{1,0:T(8,128)(2,1)S(1)}, bf16[128,1024]{1,0:T(8,128)(2,1)}, u32[]{:S(2)}) copy-start(bf16[128,1024]{1,0:T(8,128)(2,1)} %param.49) | copy-start | bytes 786436
  1063.1 46.3 %copy-start.18 = (f32[1024]{0:T(1024)S(1)}, f32[1024]{0:T(1024)}, u32[]{:S(2)}) copy-start(f32[1024]{0:T(1024)} %copy-done.17) | copy-start | bytes 12292
  1063.1 46.3 %copy-start.22 = (f32[128]{0:T(128)S(1)}, f32[128]{0:T(128)}, u32[]{:S(2)}) copy-start(f32[128]{0:T(128)} %copy-done.21) | copy-start | bytes 1540
  1095.7 13.4 all-to-all-start.9
  1101.4 1513.4 %reduce-scatter.9.cloned.1.call-start = ((), (), s32[]{:S(2)}) async-start(), calls=%async_computation.23 | async-start | bytes 8454144 | tf_op jit(solution)/shard_map/reduce_scatter | solution.py:431
  1330.8 70.9 %copy-start.24 = (f32[128]{0:T(128)S(1)}, f32[128]{0:T(128)}, u32[]{:S(2)}) copy-start(f32[128]{0:T(128)} %get-tuple-element.1125) | copy-start | bytes 1540
Sparse Core Ops, SparseCore 0:
  9.7 200.8 all-gather.6
  227.1 37.9 all-gather.8
  266.8 193.9 all-gather.10
  463.0 64.3 all-gather.14
  529.5 54.4 all-gather.12
  586.1 51.9 all-gather.16
  1029.4 66.2 reduce-scatter.6
  1099.4 74.4 reduce-scatter.16
  1177.6 73.8 reduce-scatter.14
  1255.1 73.8 reduce-scatter.12
  1331.9 635.9 reduce-scatter.10
  1970.9 643.7 reduce-scatter.8
where the time goes:
time: 2650 us; the launch traced here: 2620 us
  waiting for transfers between devices  1800 us (68%)
  matrix products  440 us (17%)
  blocking collectives  158 us (6%)
  local copies, waits for them, and re-layouts  91 us (3%)
  other arithmetic  74.6 us (3%)
  starting transfers between devices  41.2 us (2%)
    reduce_scatter x1, waiting for transfers between devices, on_device(): lax.psum_scatter(qkv_grad, ('seq', 'shard'), scatter_dimension=0, tiled=T...  647 us
    reduce_scatter x1, waiting for transfers between devices, on_device(): lax.psum_scatter(out_proj_grad, ('seq', 'shard'), scatter_dimension=0, ti...  565 us
    dot_general x96, matrix products, tile_scores(): jnp.einsum('qagd,kad->agqk', query_tile, key_tile, preferred_element_type...  138 us
    unnamed x2, blocking collectives  135 us
    all_gather x1, waiting for transfers between devices, gather_attention(): lax.all_gather(w_qkv, ('seq', 'shard'), axis=0, tiled=True)  130 us
    dot_general x48, matrix products, value_pass(): jnp.einsum('agqk,kad->qagd', softmax_weights, value_heads[key_span], pref...  82.4 us
    reduce_scatter x1, waiting for transfers between devices, on_device(): lax.psum_scatter(up_w_grad.astype(jnp.bfloat16), 'seq', scatter_dimension...  75.8 us
    reduce_scatter x1, waiting for transfers between devices, on_device(): lax.psum_scatter(gate_w_grad.astype(jnp.bfloat16), 'seq', scatter_dimensi...  75.7 us
  transfers between devices with their start and end apart: 20, of which 17 were waited for; matrix products, arithmetic and copies ran while one was open for 11% of the time, Pallas kernels for 0%

commit v1 on v0

v1 whole, which is shorter than its diff:
```python
import functools
import math

import jax
import jax.numpy as jnp
from jax import lax
from jax.experimental import pallas as pl
from jax.experimental.pallas import tpu as pltpu
from jax.sharding import PartitionSpec as P

HEADS = 16
KV = 8
HEAD = 64
EXPERTS = 32
TOPK = 8
TOK_DEV = 128
CAP = 40
WIDTH = 1024
FF = 512
N_SEQ = 8
N_SHARD = 16
HEAD_ROWS = TOK_DEV * N_SEQ
TOKENS = TOK_DEV * N_SEQ * N_SHARD
LOCAL_EXPERTS = EXPERTS // N_SHARD
EXPERT_ROWS = N_SHARD * CAP
COLS = 256
FWD_TILE = 2048
BWD_TILE = 1024

epsilon = 1e-06
rope_base = 10000.0

f32 = jnp.float32
bf16 = jnp.bfloat16
MESH = pl.DeviceIdType.MESH
ANY = pl.BlockSpec(memory_space=pl.ANY)
NT = (((1,), (1,)), ((), ()))
NN = (((1,), (0,)), ((), ()))
TN = (((0,), (0,)), ((), ()))


def dot(left, right, dims):
    return lax.dot_general(left, right, dims, preferred_element_type=f32)


def greet(peers):
    barrier = pltpu.get_barrier_semaphore()
    for axis, peer in peers:
        pl.semaphore_signal(barrier, inc=1, device_id={axis: peer}, device_id_type=MESH)
    pl.semaphore_wait(barrier, len(peers))


def remote(source, target, send, recv, axis, peer):
    copy = pltpu.make_async_remote_copy(
        src_ref=source,
        dst_ref=target,
        send_sem=send,
        recv_sem=recv,
        device_id={axis: peer},
        device_id_type=MESH,
    )
    copy.start()
    return copy


def exchange_kernel(axis, count, dim, x_ref, o_ref, send, recv, own):
    def block(ref, index):
        return ref.at[:, index] if dim == 1 else ref.at[index]

    me = lax.axis_index(axis)
    greet([(axis, lax.rem(me + k, count)) for k in range(1, count)])
    mine = pltpu.make_async_copy(block(x_ref, me), block(o_ref, me), own)
    mine.start()
    copies = []
    for k in range(1, count):
        peer = lax.rem(me + k, count)
        copies.append(
            remote(block(x_ref, peer), block(o_ref, me), send.at[k - 1], recv.at[k - 1], axis, peer)
        )
    mine.wait()
    for copy in copies:
        copy.wait()


def exchange(x, axis, count, ident, dim=0):
    return pl.pallas_call(
        functools.partial(exchange_kernel, axis, count, dim),
        out_shape=jax.ShapeDtypeStruct(x.shape, x.dtype),
        in_specs=[ANY],
        out_specs=ANY,
        scratch_shapes=[
            pltpu.SemaphoreType.DMA((count - 1,)),
            pltpu.SemaphoreType.DMA((count - 1,)),
            pltpu.SemaphoreType.DMA,
        ],
        compiler_params=pltpu.CompilerParams(collective_id=ident, has_side_effects=True),
        name="exchange_" + axis,
    )(x)


def staged(axis, share, x_ref, place, sem_send, sem_recv, own):
    me = lax.axis_index(axis)
    cores = 2 if axis == "shard" else 1
    core = lax.rem(me, cores)
    pair = lax.rem(me // cores, 2)
    ring = me // (2 * cores)

    def at(r, p, c):
        return (r * 2 + p) * cores + c

    ring_peer = [at(lax.rem(ring + k, 4), pair, core) for k in (1, 2, 3)]
    ring_from = [lax.rem(ring + 4 - k, 4) for k in (1, 2, 3)]
    pair_peer = at(ring, 1 - pair, core)
    core_peer = at(ring, pair, 1 - core)
    mine = pltpu.make_async_copy(x_ref, place(me, 0, 8), own)
    mine.start()
    sends = []

    def go(source, index, low, high, peer):
        n = len(sends)
        sends.append(
            remote(source, place(index, low, high), sem_send.at[n], sem_recv.at[n], axis, peer)
        )
        return sends[-1]

    to_pair = go(x_ref, me, 0, 8, pair_peer)
    to_ring = [go(x_ref, me, 0, 8, peer) for peer in ring_peer]
    landed = []
    if cores == 2:
        landed.append(go(x_ref, me, 0, 8, core_peer))

    def pass_core(index, low, high):
        if cores == 2:
            landed.append(go(place(index, low, high), index, low, high, core_peer))

    to_pair.wait_recv()
    fwd_ring = [
        go(place(pair_peer, 0, share), pair_peer, 0, share, peer) for peer in ring_peer
    ]
    pass_core(pair_peer, 0, 8)
    fwd_pair = []
    for k in (0, 2, 1):
        to_ring[k].wait_recv()
        source = at(ring_from[k], pair, core)
        fwd_pair.append((k, go(place(source, share, 8), source, share, 8, pair_peer)))
        pass_core(source, 0, 8)
    for k in (0, 2, 1):
        fwd_ring[k].wait_recv()
        pass_core(at(ring_from[k], 1 - pair, core), 0, share)
    for k, copy in fwd_pair:
        copy.wait_recv()
        pass_core(at(ring_from[k], 1 - pair, core), share, 8)
    for copy in landed:
        copy.wait_recv()
    mine.wait()
    for copy in sends:
        copy.wait_send()


def staged_peers(axis):
    me = lax.axis_index(axis)
    cores = 2 if axis == "shard" else 1
    core = lax.rem(me, cores)
    pair = lax.rem(me // cores, 2)
    ring = me // (2 * cores)
    peers = [(lax.rem(ring + k, 4) * 2 + pair) * cores + core for k in (1, 2, 3)]
    peers.append((ring * 2 + 1 - pair) * cores + core)
    if cores == 2:
        peers.append((ring * 2 + pair) * cores + 1 - core)
    return [(axis, peer) for peer in peers]


def gather_memory_kernel(x_ref, o_ref, send, recv, own):
    greet(staged_peers("shard"))
    staged("shard", 4, x_ref, lambda j, low, high: o_ref.at[low:high, j], send, recv, own)


def gather_memory(x, ident):
    return pl.pallas_call(
        gather_memory_kernel,
        out_shape=jax.ShapeDtypeStruct((N_SEQ, N_SHARD, TOK_DEV, 2 * HEAD), x.dtype),
        in_specs=[ANY],
        out_specs=ANY,
        scratch_shapes=[
            pltpu.SemaphoreType.DMA((24,)),
            pltpu.SemaphoreType.DMA((24,)),
            pltpu.SemaphoreType.DMA,
        ],
        compiler_params=pltpu.CompilerParams(collective_id=ident, has_side_effects=True),
        name="gather_memory",
    )(x)


def first_kernel(x_ref, w_ref, xo_ref, wo_ref, w_mid, send, recv, own, wsend, wrecv, wown):
    seq = lax.axis_index("seq")
    shard = lax.axis_index("shard")
    greet(
        [("seq", lax.rem(seq + k, N_SEQ)) for k in range(1, N_SEQ)]
        + [("shard", lax.rem(shard + k, N_SHARD)) for k in range(1, N_SHARD)]
    )
    mine = pltpu.make_async_copy(w_ref.at[seq], w_mid.at[seq], wown)
    mine.start()
    pieces = []
    for k in range(1, N_SEQ):
        peer = lax.rem(seq + k, N_SEQ)
        pieces.append(
            remote(w_ref.at[peer], w_mid.at[seq], wsend.at[k - 1], wrecv.at[k - 1], "seq", peer)
        )
    mine.wait()
    for piece in pieces:
        piece.wait()
    mine = pltpu.make_async_copy(w_mid, wo_ref.at[shard], wown)
    mine.start()
    pieces = []
    for k in range(1, N_SHARD):
        peer = lax.rem(shard + k, N_SHARD)
        n = N_SEQ - 2 + k
        pieces.append(
            remote(w_mid, wo_ref.at[shard], wsend.at[n], wrecv.at[n], "shard", peer)
        )
    staged("seq", 4, x_ref, lambda s, low, high: xo_ref.at[s, low:high], send, recv, own)
    mine.wait()
    for piece in pieces:
        piece.wait()


def first_gather(x, pieces, ident):
    return pl.pallas_call(
        first_kernel,
        out_shape=[
            jax.ShapeDtypeStruct((N_SEQ, 8, TOK_DEV // 8, WIDTH), bf16),
            jax.ShapeDtypeStruct((N_SHARD,) + pieces.shape, bf16),
        ],
        in_specs=[ANY, ANY],
        out_specs=[ANY, ANY],
        scratch_shapes=[
            pltpu.VMEM(pieces.shape, bf16),
            pltpu.SemaphoreType.DMA((12,)),
            pltpu.SemaphoreType.DMA((12,)),
            pltpu.SemaphoreType.DMA,
            pltpu.SemaphoreType.DMA((N_SEQ + N_SHARD,)),
            pltpu.SemaphoreType.DMA((N_SEQ + N_SHARD,)),
            pltpu.SemaphoreType.DMA,
        ],
        compiler_params=pltpu.CompilerParams(collective_id=ident, has_side_effects=True),
        name="gather_tokens",
    )(x, pieces)


def attention_kernel(j_ref, q_ref, kv_ref, o_ref, wide_ref, lse_ref, vt):
    i = pl.program_id(0)
    j = j_ref[0]

    @pl.when(i == 0)
    def _():
        def turn(t, carry):
            rows = pl.ds(pl.multiple_of(t * 512, 512), 512)
            vt[:, rows] = kv_ref[rows, :].T
            return carry

        lax.fori_loop(0, TOKENS // 512, turn, 0)

    queries = spread(q_ref[0], False)
    first = (i * N_SHARD + j) * TOK_DEV
    full = first // FWD_TILE

    def tile(t, carry, masked):
        peak, total, acc = carry
        rows = pl.ds(pl.multiple_of(t * FWD_TILE, FWD_TILE), FWD_TILE)
        scores = dot(kv_ref[rows, :], queries, NT)
        if masked:
            key_pos = t * FWD_TILE + lax.broadcasted_iota(jnp.int32, scores.shape, 0)
            query_pos = first + (lax.broadcasted_iota(jnp.int32, scores.shape, 1) & (TOK_DEV - 1))
            scores = jnp.where(query_pos >= key_pos, scores, -1e30)
        newest = jnp.maximum(peak, jnp.max(scores, axis=0, keepdims=True))
        weights = jnp.exp(scores - newest)
        shrink = jnp.exp(peak - newest)
        total = total * shrink + jnp.sum(weights, axis=0, keepdims=True)
        acc = acc * shrink + dot(vt[HEAD:, rows], weights.astype(bf16), NN)
        return newest, total, acc

    start = (
        jnp.full((1, 2 * TOK_DEV), -1e30, f32),
        jnp.zeros((1, 2 * TOK_DEV), f32),
        jnp.zeros((HEAD, 2 * TOK_DEV), f32),
    )
    carry = lax.fori_loop(0, full, lambda t, c: tile(t, c, False), start)
    peak, total, acc = tile(full, carry, True)
    acc = acc / total
    stacked = jnp.concatenate([acc[:, :TOK_DEV], acc[:, TOK_DEV:]], axis=0)
    wide_ref[0] = stacked
    o_ref[0] = stacked.T.astype(bf16)
    lse_ref[0] = peak + jnp.log(total)


def spread(rows, right):
    zeros = jnp.zeros((TOK_DEV, HEAD), rows.dtype)
    parts = [rows[:, :HEAD], rows[:, HEAD:]]
    if right:
        parts = [jnp.concatenate([zeros, part], axis=1) for part in parts]
    else:
        parts = [jnp.concatenate([part, zeros], axis=1) for part in parts]
    return jnp.concatenate(parts, axis=0)


def attention(shard, queries, memory):
    return pl.pallas_call(
        attention_kernel,
        grid_spec=pltpu.PrefetchScalarGridSpec(
            num_scalar_prefetch=1,
            grid=(N_SEQ,),
            in_specs=[
                pl.BlockSpec((1, TOK_DEV, 2 * HEAD), lambda i, j: (i, 0, 0)),
                pl.BlockSpec((TOKENS, 2 * HEAD), lambda i, j: (0, 0)),
            ],
            out_specs=[
                pl.BlockSpec((1, TOK_DEV, 2 * HEAD), lambda i, j: (i, 0, 0)),
                pl.BlockSpec((1, 2 * HEAD, TOK_DEV), lambda i, j: (i, 0, 0)),
                pl.BlockSpec((1, 1, 2 * TOK_DEV), lambda i, j: (i, 0, 0)),
            ],
            scratch_shapes=[pltpu.VMEM((2 * HEAD, TOKENS), bf16)],
        ),
        out_shape=[
            jax.ShapeDtypeStruct((N_SEQ, TOK_DEV, 2 * HEAD), bf16),
            jax.ShapeDtypeStruct((N_SEQ, 2 * HEAD, TOK_DEV), f32),
            jax.ShapeDtypeStruct((N_SEQ, 1, 2 * TOK_DEV), f32),
        ],
        compiler_params=pltpu.CompilerParams(vmem_limit_bytes=48 << 20),
        cost_estimate=pl.CostEstimate(
            flops=9_000_000_000, bytes_accessed=6 << 20, transcendentals=18_000_000
        ),
        name="attention_forward",
    )(shard, queries, memory)


def attention_back_kernel(
    j_ref, q_ref, g_ref, wide_ref, lse_ref, kv_ref, dq_ref, dkv_ref, kt, acc
):
    i = pl.program_id(0)
    j = j_ref[0]

    @pl.when(i == 0)
    def _():
        def turn(t, carry):
            rows = pl.ds(pl.multiple_of(t * 512, 512), 512)
            kt[:, rows] = kv_ref[rows, :].T[:HEAD]
            acc[rows, :] = jnp.zeros((512, 2 * HEAD), f32)
            return carry

        lax.fori_loop(0, TOKENS // 512, turn, 0)

    queries = spread(q_ref[0], False)
    upstream = spread(g_ref[0], True)
    lse = lse_ref[0]
    product = wide_ref[0] * g_ref[0].astype(f32).T
    delta = jnp.concatenate(
        [
            jnp.sum(product[:HEAD], axis=0, keepdims=True),
            jnp.sum(product[HEAD:], axis=0, keepdims=True),
        ],
        axis=1,
    )
    first = (i * N_SHARD + j) * TOK_DEV
    full = first // BWD_TILE

    def tile(t, query_grad, masked):
        rows = pl.ds(pl.multiple_of(t * BWD_TILE, BWD_TILE), BWD_TILE)
        memory = kv_ref[rows, :]
        scores = dot(memory, queries, NT)
        weights = jnp.exp(scores - lse)
        if masked:
            key_pos = t * BWD_TILE + lax.broadcasted_iota(jnp.int32, scores.shape, 0)
            query_pos = first + (lax.broadcasted_iota(jnp.int32, scores.shape, 1) & (TOK_DEV - 1))
            weights = jnp.where(query_pos >= key_pos, weights, 0.0)
        weight_grad = dot(memory, upstream, NT)
        score_grad = (weights * (weight_grad - delta)).astype(bf16)
        acc[rows, :] += dot(weights.astype(bf16), upstream, NN) + dot(score_grad, queries, NN)
        return query_grad + dot(kt[:, rows], score_grad, NN)

    start = jnp.zeros((HEAD, 2 * TOK_DEV), f32)
    query_grad = lax.fori_loop(0, full, lambda t, c: tile(t, c, False), start)
    query_grad = tile(full, query_grad, True) * (1.0 / math.sqrt(HEAD))
    stacked = jnp.concatenate([query_grad[:, :TOK_DEV], query_grad[:, TOK_DEV:]], axis=0)
    dq_ref[0] = stacked.T.astype(bf16)

    @pl.when(i == N_SEQ - 1)
    def _():
        def put(t, carry):
            rows = pl.ds(pl.multiple_of(t * 512, 512), 512)
            dkv_ref[rows, :] = acc[rows, :].astype(bf16)
            return carry

        lax.fori_loop(0, TOKENS // 512, put, 0)


def attention_back(shard, queries, upstream, wide, lse, memory):
    return pl.pallas_call(
        attention_back_kernel,
        grid_spec=pltpu.PrefetchScalarGridSpec(
            num_scalar_prefetch=1,
            grid=(N_SEQ,),
            in_specs=[
                pl.BlockSpec((1, TOK_DEV, 2 * HEAD), lambda i, j: (i, 0, 0)),
                pl.BlockSpec((1, TOK_DEV, 2 * HEAD), lambda i, j: (i, 0, 0)),
                pl.BlockSpec((1, 2 * HEAD, TOK_DEV), lambda i, j: (i, 0, 0)),
                pl.BlockSpec((1, 1, 2 * TOK_DEV), lambda i, j: (i, 0, 0)),
                pl.BlockSpec((TOKENS, 2 * HEAD), lambda i, j: (0, 0)),
            ],
            out_specs=[
                pl.BlockSpec((1, TOK_DEV, 2 * HEAD), lambda i, j: (i, 0, 0)),
                pl.BlockSpec((TOKENS, 2 * HEAD), lambda i, j: (0, 0)),
            ],
            scratch_shapes=[
                pltpu.VMEM((HEAD, TOKENS), bf16),
                pltpu.VMEM((TOKENS, 2 * HEAD), f32),
            ],
        ),
        out_shape=[
            jax.ShapeDtypeStruct((N_SEQ, TOK_DEV, 2 * HEAD), bf16),
            jax.ShapeDtypeStruct((TOKENS, 2 * HEAD), bf16),
        ],
        compiler_params=pltpu.CompilerParams(vmem_limit_bytes=56 << 20),
        cost_estimate=pl.CostEstimate(
            flops=23_000_000_000, bytes_accessed=12 << 20, transcendentals=18_000_000
        ),
        name="attention_backward",
    )(shard, queries, upstream, wide, lse, memory)


def expert_kernel(x_ref, g_ref, w_ref, out_ref, back_ref, wg_ref, gu, down, xt, ht, both):
    gu[...] = w_ref[0, :, :128, :].reshape(WIDTH, 2 * FF)
    down[...] = w_ref[0, :, 128:, :].reshape(FF, WIDTH)

    def rows_step(t, carry):
        rows = pl.ds(pl.multiple_of(t * 128, 128), 128)
        x = x_ref[0, rows, :]
        pre = dot(x, gu[...], NN)
        gate, up = pre[:, :FF], pre[:, FF:]
        sigmoid = jax.nn.sigmoid(gate)
        act = gate * sigmoid
        hidden = (act * up).astype(bf16)
        out_ref[0, rows, :] = dot(hidden, down[...], NN).astype(bf16)
        units = dot(g_ref[0, rows, :], down[...], NT)
        gate_grad = (units * up * sigmoid * (1.0 + gate * (1.0 - sigmoid))).astype(bf16)
        up_grad = (units * act).astype(bf16)
        pair = jnp.concatenate([gate_grad, up_grad], axis=1)
        back_ref[0, rows, :] = dot(pair, gu[...], NT).astype(bf16)
        both[rows, :] = pair
        xt[:, rows] = x.T
        ht[:, rows] = hidden.T
        return carry

    lax.fori_loop(0, EXPERT_ROWS // 128, rows_step, 0)

    def grad_step(s, carry):
        features = pl.ds(pl.multiple_of(s * 128, 128), 128)
        units = pl.ds(pl.multiple_of(s * 64, 64), 64)
        wg_ref[s, 0, :128, :] = dot(xt[features, :], both[...], NN).astype(bf16)
        wg_ref[s, 0, 128:, :] = dot(ht[units, :], g_ref[0], NN).astype(bf16)
        return carry

    lax.fori_loop(0, N_SEQ, grad_step, 0)


def experts(x, g, w):
    rows = pl.BlockSpec((1, EXPERT_ROWS, WIDTH), lambda e: (e, 0, 0))
    shape = jax.ShapeDtypeStruct((LOCAL_EXPERTS, EXPERT_ROWS, WIDTH), bf16)
    return pl.pallas_call(
        expert_kernel,
        grid=(LOCAL_EXPERTS,),
        in_specs=[rows, rows, pl.BlockSpec((1, N_SEQ, 192, WIDTH), lambda e: (e, 0, 0, 0))],
        out_specs=[rows, rows, pl.BlockSpec((N_SEQ, 1, 192, WIDTH), lambda e: (0, e, 0, 0))],
        out_shape=[
            shape,
            shape,
            jax.ShapeDtypeStruct((N_SEQ, LOCAL_EXPERTS, 192, WIDTH), bf16),
        ],
        scratch_shapes=[
            pltpu.VMEM((WIDTH, 2 * FF), bf16),
            pltpu.VMEM((FF, WIDTH), bf16),
            pltpu.VMEM((WIDTH, EXPERT_ROWS), bf16),
            pltpu.VMEM((FF, EXPERT_ROWS), bf16),
            pltpu.VMEM((EXPERT_ROWS, 2 * FF), bf16),
        ],
        compiler_params=pltpu.CompilerParams(vmem_limit_bytes=56 << 20),
        cost_estimate=pl.CostEstimate(
            flops=12_000_000_000, bytes_accessed=24 << 20, transcendentals=1_000_000
        ),
        name="experts",
    )(x, g, w)


def group_columns(rows):
    lead = rows.shape[:-1]
    queries = rows[..., : HEADS * HEAD].reshape(lead + (N_SEQ, 2 * HEAD))
    keys = rows[..., HEADS * HEAD : (HEADS + KV) * HEAD].reshape(lead + (N_SEQ, HEAD))
    values = rows[..., (HEADS + KV) * HEAD :].reshape(lead + (N_SEQ, HEAD))
    return jnp.concatenate([queries, keys, values], axis=-1)


def ungroup_columns(groups):
    rows = groups.shape[0]
    return jnp.concatenate(
        [
            groups[:, :, : 2 * HEAD].reshape(rows, HEADS * HEAD),
            groups[:, :, 2 * HEAD : 3 * HEAD].reshape(rows, KV * HEAD),
            groups[:, :, 3 * HEAD :].reshape(rows, KV * HEAD),
        ],
        axis=1,
    )


def rope_pair(shard):
    half = HEAD // 2
    frequency = jnp.exp(
        jnp.arange(half, dtype=f32) * jnp.float32(-2.0 * math.log(rope_base) / HEAD)
    )
    chunk = jnp.arange(N_SEQ, dtype=jnp.int32)[:, None] * N_SHARD + shard
    position = chunk * TOK_DEV + jnp.arange(TOK_DEV, dtype=jnp.int32)[None, :]
    angles = position.reshape(HEAD_ROWS, 1).astype(f32) * frequency[None, :]
    return jnp.tile(jnp.cos(angles), (1, 6)), jnp.tile(jnp.sin(angles), (1, 6))


def turn_matrix():
    row = jnp.arange(3 * HEAD, dtype=jnp.int32)[:, None]
    col = jnp.arange(3 * HEAD, dtype=jnp.int32)[None, :]
    half = HEAD // 2
    low = col % HEAD < half
    minus = low & (row == col + half)
    plus = (~low) & (row == col - half)
    return (plus.astype(f32) - minus.astype(f32)).astype(bf16)


def on_device(
    layer_input,
    attn_gain,
    moe_gain,
    w_qkv,
    w_out,
    w_gate,
    w_up,
    w_down,
    routes,
    route_weights,
    cotangent,
):
    shard = lax.axis_index("shard")
    shard_array = shard.astype(jnp.int32).reshape(1)

    expert_pack = jnp.concatenate(
        [jnp.concatenate([w_gate, w_up], axis=2), w_down], axis=1
    )
    grouped = group_columns(w_qkv)
    projections = jnp.concatenate([w_out, grouped.reshape(8, 2 * WIDTH)], axis=1)
    projections = lax.all_gather(projections, "shard", axis=0, tiled=True)
    expert_weights = lax.all_gather(expert_pack, "seq", axis=1)
    pieces = grouped.transpose(1, 0, 2).reshape(N_SEQ, 8, 2, 128).transpose(0, 2, 1, 3)
    gains = jnp.concatenate([attn_gain, moe_gain, jnp.zeros((112,), bf16)])
    gains = jnp.broadcast_to(gains[None, None, :], (N_SEQ, 16, 128))
    pieces = jnp.concatenate([pieces.reshape(N_SEQ, 16, 128), gains], axis=1)
    tokens, columns = first_gather(
        layer_input.reshape(8, TOK_DEV // 8, WIDTH), pieces, 1
    )
    gain_rows = columns[:, :, 16, :16].transpose(1, 0, 2)
    gain_attn = gain_rows[:, :, :8].reshape(WIDTH).astype(f32)
    gain_moe = gain_rows[:, :, 8:].reshape(WIDTH).astype(f32)
    columns = columns[:, :, :16].reshape(N_SHARD, N_SEQ, 2, 8, 128)
    columns = columns.transpose(1, 0, 3, 2, 4).reshape(WIDTH, COLS)

    wide = tokens.reshape(HEAD_ROWS, WIDTH).astype(f32)
    inverse = lax.rsqrt(jnp.mean(wide * wide, axis=1, keepdims=True) + epsilon)
    normed = (wide * inverse * gain_attn).astype(bf16)
    cosine, sine = rope_pair(shard)
    turn = turn_matrix()
    turned = dot(columns[:, : 3 * HEAD], turn, NN).astype(bf16)
    projected = dot(normed, jnp.concatenate([columns, turned], axis=1), NN)
    rotated = projected[:, : 3 * HEAD] * cosine + projected[:, COLS:] * sine
    queries = rotated[:, : 2 * HEAD].astype(bf16) * jnp.bfloat16(1.0 / math.sqrt(HEAD))
    queries = queries.reshape(N_SEQ, TOK_DEV, 2 * HEAD)
    memory = jnp.concatenate(
        [rotated[:, 2 * HEAD :], projected[:, 3 * HEAD : COLS]], axis=1
    ).astype(bf16)
    memory = gather_memory(memory.reshape(N_SEQ, TOK_DEV, 2 * HEAD), 2)
    memory = memory.reshape(TOKENS, 2 * HEAD)

    flat_routes = routes.reshape(TOK_DEV * TOPK)
    onehot = (flat_routes[:, None] == jnp.arange(EXPERTS, dtype=jnp.int32)[None, :]).astype(
        jnp.int32
    )
    slot_index = jnp.sum((jnp.cumsum(onehot, axis=0) - 1) * onehot, axis=1)
    slot_row = flat_routes % LOCAL_EXPERTS * N_SHARD + flat_routes // LOCAL_EXPERTS
    slot_place = (slot_row * CAP + slot_index).reshape(TOK_DEV, TOPK)
    here = slot_place[:, :, None] == jnp.arange(EXPERTS * CAP, dtype=jnp.int32)[None, None, :]
    pick = jnp.sum(here.astype(f32), axis=1)
    scale = jnp.sum(jnp.where(here, route_weights[:, :, None], 0.0), axis=1)
    pick = pick.astype(bf16)
    scale_high = scale.astype(bf16)
    scale_low = (scale - scale_high.astype(f32)).astype(bf16)
    slot_scale = jnp.sum(scale, axis=0)[:, None]
    out_grad = cotangent.astype(f32)
    slots = (LOCAL_EXPERTS, N_SHARD, CAP, WIDTH)
    grad_send = (slot_scale * dot(pick, cotangent, TN)).astype(bf16).reshape(slots)
    grad_rows = [
        lax.all_to_all(grad_send[e], "shard", 0, 0).reshape(EXPERT_ROWS, WIDTH)
        for e in range(LOCAL_EXPERTS)
    ]
    grad_rows = jnp.stack(grad_rows)

    attended, attended_wide, lse = attention(shard_array, queries, memory)
    out_weight = lax.all_to_all(
        jnp.broadcast_to(projections[None, :, :WIDTH], (N_SEQ, 128, WIDTH)), "seq", 0, 0
    ).reshape(WIDTH, WIDTH)

    attended_full = exchange(attended, "seq", N_SEQ, 3)
    attended_full = attended_full.transpose(1, 0, 2).reshape(TOK_DEV, WIDTH)
    x_wide = layer_input.astype(f32)
    residual = x_wide + dot(attended_full, out_weight, NN)
    inverse_two = lax.rsqrt(jnp.mean(residual * residual, axis=1, keepdims=True) + epsilon)
    normed_moe = (residual * inverse_two * gain_moe).astype(bf16)

    send_rows = dot(pick, normed_moe, TN).astype(bf16).reshape(slots)
    expert_rows = exchange(send_rows, "shard", N_SHARD, 4, dim=1)
    expert_rows = expert_rows.reshape(LOCAL_EXPERTS, EXPERT_ROWS, WIDTH)
    expert_out, rows_grad, expert_grads = experts(expert_rows, grad_rows, expert_weights)
    returned = exchange(rows_grad.reshape(slots), "shard", N_SHARD, 5, dim=1)
    expert_out = expert_out.reshape(slots)
    came_back = [
        lax.all_to_all(expert_out[e], "shard", 0, 0).reshape(EXPERT_ROWS, WIDTH)
        for e in range(LOCAL_EXPERTS)
    ]
    came_back = jnp.concatenate(came_back, axis=0)
    moe_sum = dot(scale_high, came_back, NN) + dot(scale_low, came_back, NN)
    block_out = (residual + moe_sum).astype(bf16)
    expert_grads = lax.all_to_all(expert_grads, "seq", 0, 0)
    expert_sums = jnp.sum(expert_grads.astype(f32), axis=0)

    moe_in_grad = dot(pick, returned.reshape(EXPERTS * CAP, WIDTH), NN)
    scaled = moe_in_grad * gain_moe
    moe_part = inverse_two * scaled - residual * inverse_two**3 * jnp.mean(
        residual * scaled, axis=1, keepdims=True
    )
    residual_grad = out_grad + moe_part
    branch_grad = residual_grad.astype(bf16)
    attended_grad = dot(branch_grad, out_weight, NT).astype(bf16)
    attended_grad = attended_grad.reshape(TOK_DEV, N_SEQ, 2 * HEAD).transpose(1, 0, 2)
    attended_grad = exchange(attended_grad, "seq", N_SEQ, 6)
    branch_all = lax.all_to_all(
        jnp.broadcast_to(branch_grad[None], (N_SEQ, TOK_DEV, WIDTH)), "seq", 0, 0
    ).reshape(HEAD_ROWS, WIDTH)

    query_grad, memory_grad = attention_back(
        shard_array, queries, attended_grad, attended_wide, lse, memory
    )
    memory_grad = memory_grad.reshape(N_SEQ, N_SHARD, TOK_DEV, 2 * HEAD)
    memory_grad = exchange(memory_grad, "shard", N_SHARD, 7, dim=1)
    memory_grad = jnp.sum(memory_grad.astype(f32), axis=1).astype(bf16)
    memory_grad = memory_grad.reshape(HEAD_ROWS, 2 * HEAD)
    rotary = jnp.concatenate(
        [query_grad.reshape(HEAD_ROWS, 2 * HEAD), memory_grad[:, :HEAD]], axis=1
    )
    rotary = rotary.astype(f32) * cosine + dot(rotary, turn, NT) * sine
    projected_grad = jnp.concatenate([rotary.astype(bf16), memory_grad[:, HEAD:]], axis=1)
    token_grad = exchange(projected_grad.reshape(N_SEQ, TOK_DEV, COLS), "seq", N_SEQ, 8)

    qkv_part = dot(normed, projected_grad, TN)
    qkv_part = qkv_part.reshape(N_SEQ, N_SHARD, 8, COLS).transpose(1, 0, 2, 3)
    out_part = dot(attended.reshape(HEAD_ROWS, 2 * HEAD), branch_all, TN)
    out_part = out_part.reshape(N_SHARD, 8, WIDTH)
    pack = expert_pack.astype(f32)
    moe_gain_part = jnp.sum(
        pack[:, :128] * expert_sums[:, :128], axis=(0, 2)
    ) / lax.dynamic_slice_in_dim(gain_moe, lax.axis_index("seq") * 128, 128)
    moe_gain_part = moe_gain_part.reshape(N_SHARD, 1, 8)
    moe_gain_high = moe_gain_part.astype(bf16)
    moe_gain_low = (moe_gain_part - moe_gain_high.astype(f32)).astype(bf16)
    gain_part = jnp.concatenate([moe_gain_high, moe_gain_low], axis=1)
    gain_part = jnp.pad(gain_part, ((0, 0), (0, 14), (0, COLS - 8)))
    sums = jnp.concatenate(
        [
            qkv_part.reshape(N_SHARD, 64, COLS).astype(bf16),
            out_part.reshape(N_SHARD, 32, COLS).astype(bf16),
            gain_part,
        ],
        axis=1,
    )
    sums = jnp.sum(exchange(sums, "shard", N_SHARD, 9).astype(f32), axis=0)
    out_weight_grad = sums[64:96].reshape(8, WIDTH)
    moe_gain_grad = sums[96, :8] + sums[97, :8]
    qkv_groups = exchange(sums[:64].reshape(N_SEQ, 8, COLS), "seq", N_SEQ, 10).transpose(1, 0, 2)
    attn_gain_grad = jnp.sum(grouped.astype(f32) * qkv_groups, axis=(1, 2)) / attn_gain.astype(f32)
    qkv_weight_grad = ungroup_columns(qkv_groups)

    qkv_all = lax.all_gather(projections[:, WIDTH:], "seq", axis=0, tiled=True)
    token_grad = token_grad.transpose(1, 0, 2).reshape(TOK_DEV, N_SEQ * COLS)
    normed_grad = dot(token_grad, qkv_all, NT)
    inverse_one = lax.rsqrt(jnp.mean(x_wide * x_wide, axis=1, keepdims=True) + epsilon)
    scaled = normed_grad * gain_attn
    attn_part = inverse_one * scaled - x_wide * inverse_one**3 * jnp.mean(
        x_wide * scaled, axis=1, keepdims=True
    )
    input_grad = (residual_grad + attn_part).astype(bf16)
    return (
        block_out,
        input_grad,
        attn_gain_grad,
        moe_gain_grad,
        qkv_weight_grad,
        out_weight_grad,
        expert_sums[:, :128, :FF],
        expert_sums[:, :128, FF:],
        expert_sums[:, 128:],
    )


def solution(mesh):
    token = P(("seq", "shard"), None)
    vector = P(("seq", "shard"))
    expert = P("shard", "seq", None)
    return jax.shard_map(
        on_device,
        mesh=mesh,
        in_specs=(
            token,
            vector,
            vector,
            token,
            token,
            expert,
            expert,
            expert,
            token,
            token,
            token,
        ),
        out_specs=(token, token, vector, vector, token, token, expert, expert, expert),
        check_vma=False,
    )
```

time: 2650 us -> 760 us (0.29)
  waiting for transfers between devices: 1800 us -> 16.2 us
  Pallas kernels: 0 us -> 522 us
  matrix products: 440 us -> 22.1 us
  blocking collectives: 158 us -> 68.3 us
  local copies, waits for them, and re-layouts: 91 us -> 42.9 us
  other arithmetic: 74.6 us -> 39.7 us
    reduce_scatter x6 -> x0, waiting for transfers between devices: 1460 us -> none  [the longest x1 647 us: on_device(): lax.psum_scatter(qkv_grad, ('seq', 'shard'), scatter_dimension=0, tiled=T...]
    pallas_call x0 -> x13, Pallas kernels: none -> 522 us  [the longest x8 271 us: exchange(): pl.pallas_call(functools.partial(exchange_kernel, axis, count, dim), out_...]
    dot_general x351 -> x13, matrix products: 440 us -> 22.1 us  [dot(): return lax.dot_general(left, right, dims, preferred_element_type=f32)]
    all_gather x6 -> x2, waiting for transfers between devices: 203 us -> 0.04 us  [the longest x1 0.02 us: on_device(): qkv_all = lax.all_gather(projections[:, WIDTH:], 'seq', axis=0, tiled=True)]
    unnamed x2 -> x0, blocking collectives: 135 us -> none
    all_to_all x8 -> x6, waiting for transfers between devices: 136 us -> 16.2 us  [the longest x2 16.1 us: on_device(): lax.all_to_all(expert_out[e], 'shard', 0, 0).reshape(EXPERT_ROWS, WIDTH)]
    all_gather x0 -> x1, blocking collectives: none -> 34 us  [on_device(): projections = lax.all_gather(projections, 'shard', axis=0, tiled=True)]
  transfers between devices with their start and end apart: 20 -> 8, of which waited for: 17 -> 1; matrix products, arithmetic and copies ran while one was open for 11% -> 10% of each run, Pallas kernels for 0% -> 62%
where the time goes in v1:
time: 760 us; the launch traced here: 758 us
  Pallas kernels  522 us (69%)
  blocking collectives  68.3 us (9%)
  local copies, waits for them, and re-layouts  42.9 us (6%)
  other arithmetic  39.7 us (5%)
  starting transfers between devices  31.6 us (4%)
  matrix products  22.1 us (3%)
  waiting for transfers between devices  16.2 us (2%)
  between operations  15 us (2%)
    pallas_call x8, Pallas kernels, exchange(): pl.pallas_call(functools.partial(exchange_kernel, axis, count, dim), out_...  271 us
    pallas_call x1, Pallas kernels, first_gather(): pl.pallas_call(first_kernel, out_shape=[jax.ShapeDtypeStruct((N_SEQ, 8, T...  77.6 us
    pallas_call x1, Pallas kernels, attention_back(): pl.pallas_call(attention_back_kernel, grid_spec=pltpu.PrefetchScalarGridS...  60 us
    pallas_call x1, Pallas kernels, attention(): pl.pallas_call(attention_kernel, grid_spec=pltpu.PrefetchScalarGridSpec(n...  45.8 us
    pallas_call x1, Pallas kernels, gather_memory(): pl.pallas_call(gather_memory_kernel, out_shape=jax.ShapeDtypeStruct((N_SE...  35.3 us
    all_to_all x1, blocking collectives, on_device(): lax.all_to_all(jnp.broadcast_to(branch_grad[None], (N_SEQ, TOK_DEV, WIDTH...  34.3 us
    all_gather x1, blocking collectives, on_device(): projections = lax.all_gather(projections, 'shard', axis=0, tiled=True)  34 us
    pallas_call x1, Pallas kernels, experts(): pl.pallas_call(expert_kernel, grid=(LOCAL_EXPERTS,), in_specs=[rows, rows...  32.5 us
  transfers between devices with their start and end apart: 8, of which 1 were waited for; matrix products, arithmetic and copies ran while one was open for 10% of the time, Pallas kernels for 62%

profile of v1, /device:TPU:1, one launch (start us, length us, event | category | flops | bytes accessed | tf_op | source)
XLA Modules:
  0.0 758.3 jit_solution(7079949871532661070)
XLA Ops:
  10.0 1.9 pad_maximum_fusion.11
  12.3 9.0 %reduce-window.6 = s32[32,8,128]{2,1,0:T(8,128)S(1)} reduce-window(s32[32,8,128]{2,1,0:T(8,128)S(1)} %fusion.42, s32[]{:T(128)} %constant.77.clone.1), window={size=1x1x128 pad=0_0x0_0x127_0}, to_apply=%region_1.2 | reduce-window | flops 4161536 | bytes 262148 | tf_op jit(solution)/shard_map/reduce-window
  22.1 4.3 select_reduce_fusion.1
  27.3 1.7 fusion.63
  29.0 7.0 all-to-all-start.1
  37.1 77.6 %gather_tokens.1 = (bf16[8,8,16,1024]{3,2,1,0:T(8,128)(2,1)}, bf16[16,8,32,128]{3,2,1,0:T(8,128)(2,1)}) custom-call(bf16[8,16,1024]{2,1,0:T(8,128)(2,1)} %bitcast.138, bf16[8,32,128]{2,1,0:T(8,128)(2,1)} %pad_maximum_fusion.16.w_ref), custom_call_target="tpu_custom_call" | custom-call | tf_op jit(solution)/shard_map/gather_tokens/pallas_call | solution.py:228
  114.7 1.1 slice.116
  118.3 6.2 all-to-all-start.2
  125.0 34.0 %all_gather.12 = bf16[128,3072]{1,0:T(8,128)(2,1)S(1)} all-gather(bf16[8,3072]{1,0:T(8,128)(2,1)S(1)} %pad_maximum_fusion.18), channel_id=1, replica_groups=mesh['seq'=8,'shard'=16] {'shard'}, dimensions={0}, use_global_device_ids=true | all-gather | bytes 835584 | tf_op jit(solution)/shard_map/all_gather | solution.py:555
  160.5 1.4 copy-done.7
  161.8 2.4 fusion.13
  164.2 1.6 broadcast_in_dim.18
  165.8 4.0 all-to-all-start
  171.4 1.5 fusion.18
  175.6 1.8 pad_maximum_fusion.14.x_ref
  177.4 35.3 %gather_memory.1 = bf16[8,16,128,128]{3,2,1,0:T(8,128)(2,1)} custom-call(bf16[8,128,128]{2,1,0:T(8,128)(2,1)} %pad_maximum_fusion.14.x_ref), custom_call_target="tpu_custom_call" | custom-call | tf_op jit(solution)/shard_map/gather_memory/pallas_call | solution.py:179
  212.9 2.3 copy-done
  215.2 45.8 %attention_forward.1 = (bf16[8,128,128]{2,1,0:T(8,128)(2,1)S(1)}, f32[8,128,128]{2,1,0:T(8,128)S(1)}, f32[8,1,256]{2,1,0:T(1,128)S(1)}) custom-call(s32[1]{0:T(128)} %bitcast.j_ref, bf16[8,128,128]{2,1,0:T(8,128)(2,1)S(1)} %bitcast.128, bf16[16384,128]{1,0:T(8,128)(2,1)S(1)} %bitcast.127), custom_call_target="tpu_custom_call" | custom-call | flops 8999999488 | bytes 6291456 | tf_op jit(solution)/shard_map/attention_forward/pallas_call | solution.py:307
  263.1 10.4 %exchange_seq.4 = bf16[8,128,128]{2,1,0:T(8,128)(2,1)} custom-call(bf16[8,128,128]{2,1,0:T(8,128)(2,1)} %copy-done.1), custom_call_target="tpu_custom_call" | custom-call | tf_op jit(solution)/shard_map/exchange_seq/pallas_call | solution.py:86
  273.7 3.5 pad_maximum_fusion.g_ref
  277.3 1.5 multiply_reduce_fusion.2
  278.8 2.4 convolution_convert_fusion
  281.2 33.0 %exchange_shard.4 = bf16[2,16,40,1024]{3,2,1,0:T(8,128)(2,1)} custom-call(bf16[2,16,40,1024]{3,2,1,0:T(8,128)(2,1)} %bitcast.132), custom_call_target="tpu_custom_call" | custom-call | tf_op jit(solution)/shard_map/exchange_shard/pallas_call | solution.py:86
  314.2 32.5 %experts.1 = (bf16[2,640,1024]{2,1,0:T(8,128)(2,1)}, bf16[2,640,1024]{2,1,0:T(8,128)(2,1)}, bf16[8,2,192,1024]{3,2,1,0:T(8,128)(2,1)}) custom-call(bf16[2,640,1024]{2,1,0:T(8,128)(2,1)} %bitcast.141, bf16[2,640,1024]{2,1,0:T(8,128)(2,1)} %pad_maximum_fusion.g_ref, bf16[2,8,192,1024]{3,2,1,0:T(8,128)(2,1)} %bitcast.162), custom_call_target="tpu_custom_call" | custom-call | flops 12000000000 | bytes 25165824 | tf_op jit(solution)/shard_map/experts/pallas_call | solution.py:468
  346.7 3.5 fusion.62
  350.2 4.3 all-to-all-start.3
  354.6 1.9 slice.163
  356.5 16.1 %all-to-all-done.3 = bf16[16,40,1024]{2,1,0:T(8,128)(2,1)} async-done(((bf16[16,40,1024]{2,1,0:T(8,128)(2,1)}), bf16[16,40,1024]{2,1,0:T(8,128)(2,1)}, u32[]{:S(2)}, u32[]{:S(2)}) %all-to-all-start.3) | async-done | bytes 1310752 | tf_op jit(solution)/shard_map/all_to_all | solution.py:628
  372.6 5.0 all-to-all-start.4
  377.6 68.2 %exchange_shard.5 = bf16[2,16,40,1024]{3,2,1,0:T(8,128)(2,1)} custom-call(bf16[2,16,40,1024]{3,2,1,0:T(8,128)(2,1)} %bitcast.140), custom_call_target="tpu_custom_call" | custom-call | tf_op jit(solution)/shard_map/exchange_shard/pallas_call | solution.py:86
  445.9 2.4 multiply_reduce_fusion.1
  449.5 34.3 %all_to_all.35 = bf16[8,128,1024]{2,1,0:T(8,128)(2,1)} all-to-all(bf16[8,128,1024]{2,1,0:T(8,128)(2,1)S(1)} %broadcast_in_dim.25), channel_id=1, replica_groups=mesh['seq'=8,'shard'=16] {'seq'}, dimensions={0} | all-to-all | bytes 4194304 | tf_op jit(solution)/shard_map/all_to_all | solution.py:647
  483.8 5.0 all-to-all-start.6
  488.8 4.0 copy.152
  492.7 1.5 convolution_convert_fusion.3
  496.2 68.5 %exchange_seq.5.g_ref = bf16[8,128,128]{2,1,0:T(8,128)(2,1)} custom-call(bf16[8,128,128]{2,1,0:T(8,128)(2,1)} %bitcast.151), custom_call_target="tpu_custom_call" | custom-call | tf_op jit(solution)/shard_map/exchange_seq/pallas_call | solution.py:86
  564.7 60.0 %attention_backward.1 = (bf16[8,128,128]{2,1,0:T(8,128)(2,1)}, bf16[16384,128]{1,0:T(8,128)(2,1)}) custom-call(s32[1]{0:T(128)} %bitcast.j_ref, bf16[8,128,128]{2,1,0:T(8,128)(2,1)} %bitcast.129, bf16[8,128,128]{2,1,0:T(8,128)(2,1)} %exchange_seq.5.g_ref, f32[8,128,128]{2,1,0:T(8,128)} %copy-done.4, f32[8,1,256]{2,1,0:T(1,128)} %copy-done.5, ...), custom_call_target="tpu_custom_call" | custom-call | flops 23000000512 | bytes 12582912 | tf_op jit(solution)/shard_map/attention_backward/pallas_call | solution.py:397
  624.7 58.1 %exchange_shard.6 = bf16[8,16,128,128]{3,2,1,0:T(8,128)(2,1)} custom-call(bf16[8,16,128,128]{3,2,1,0:T(8,128)(2,1)} %bitcast.137), custom_call_target="tpu_custom_call" | custom-call | tf_op jit(solution)/shard_map/exchange_shard/pallas_call | solution.py:86
  682.9 2.9 reduce_sum.140
  690.7 10.9 %exchange_seq.6 = bf16[8,128,256]{2,1,0:T(8,128)(2,1)} custom-call(bf16[8,128,256]{2,1,0:T(8,128)(2,1)} %bitcast.145), custom_call_target="tpu_custom_call" | custom-call | tf_op jit(solution)/shard_map/exchange_seq/pallas_call | solution.py:86
  701.6 1.3 copy.151
  703.0 3.9 fusion.19
  707.8 2.2 fusion.2
  710.1 3.1 fusion.11
  713.9 4.4 convert_reduce_fusion
  720.4 14.7 %exchange_shard.7 = bf16[16,112,256]{2,1,0:T(8,128)(2,1)} custom-call(bf16[16,112,256]{2,1,0:T(8,128)(2,1)} %pad_maximum_fusion.10.x_ref), custom_call_target="tpu_custom_call" | custom-call | tf_op jit(solution)/shard_map/exchange_shard/pallas_call | solution.py:86
  735.0 1.3 convert_reduce_fusion.2
  737.0 7.4 exchange_seq.7
  (189 shorter events, 36.0 us)
Async XLA Ops:
  7.2 4.8 copy-start.30
  7.2 307.0 %all-gather.6.cloned.1.call-start = ((), (), s32[]{:S(2)}) async-start(), calls=%async_computation.8 | async-start | bytes 7077888 | tf_op jit(solution)/shard_map/all_gather | solution.py:556
  8.2 13.7 %copy-start.31 = (f32[128,8]{0,1:T(8,128)S(1)}, f32[128,8]{0,1:T(8,128)}, u32[]{:S(2)}) copy-start(f32[128,8]{0,1:T(8,128)} %param.20) | copy-start | bytes 12292
  9.2 0.8 copy-start.10
  11.9 14.5 %copy-start.16 = (bf16[128,1024]{1,0:T(8,128)(2,1)S(1)}, bf16[128,1024]{1,0:T(8,128)(2,1)}, u32[]{:S(2)}) copy-start(bf16[128,1024]{1,0:T(8,128)(2,1)} %param.21) | copy-start | bytes 786436
  29.0 7.1 copy-start.24
  29.0 7.3 copy-start.36
  29.0 7.3 copy-start.37
  29.0 89.3 %all-to-all-start.1 = ((bf16[16,40,1024]{2,1,0:T(8,128)(2,1)}), bf16[16,40,1024]{2,1,0:T(8,128)(2,1)}, u32[]{:S(2)}, u32[]{:S(2)}) async-start(bf16[16,40,1024]{2,1,0:T(8,128)(2,1)} %bitcast.29), calls=%async_computation.1 | async-start | bytes 2621440 | tf_op jit(solution)/shard_map/all_to_all | solution.py:604
  114.7 2.6 copy-start.8
  117.0 1.2 copy-start.25
  117.1 0.8 copy-start.19
  117.1 1.1 copy-start.26
  117.1 1.1 copy-start.28
  117.1 1.1 copy-start.32
  117.2 1.1 copy-start.34
  118.3 45.9 %all-to-all-start.2 = ((bf16[16,40,1024]{2,1,0:T(8,128)(2,1)}), bf16[16,40,1024]{2,1,0:T(8,128)(2,1)}, u32[]{:S(2)}, u32[]{:S(2)}) async-start(bf16[16,40,1024]{2,1,0:T(8,128)(2,1)} %bitcast.134), calls=%async_computation.2 | async-start | bytes 2621440 | tf_op jit(solution)/shard_map/all_to_all | solution.py:604
  124.7 35.8 %copy-start.22 = (f32[1024]{0:T(1024)}, f32[1024]{0:T(1024)S(1)}, u32[]{:S(2)}) copy-start(f32[1024]{0:T(1024)S(1)} %reshape.455) | copy-start | bytes 12292
  159.0 0.9 copy-start.12
  159.9 1.9 copy-start.20
  160.4 1.4 copy-start.7
  165.8 111.4 %all-to-all-start = ((bf16[8,128,1024]{2,1,0:T(8,128)(2,1)}), bf16[8,128,1024]{2,1,0:T(8,128)(2,1)S(1)}, u32[]{:S(2)}, u32[]{:S(2)}) async-start(bf16[8,128,1024]{2,1,0:T(8,128)(2,1)} %broadcast_in_dim.18), calls=%async_computation | async-start | bytes 4194304 | tf_op jit(solution)/shard_map/all_to_all | solution.py:610
  212.9 48.1 %copy-start.3 = (bf16[1024,128]{1,0:T(8,128)(2,1)}, bf16[1024,128]{1,0:T(8,128)(2,1)S(1)}, u32[]{:S(2)}) copy-start(bf16[1024,128]{1,0:T(8,128)(2,1)S(1)} %copy.133) | copy-start | bytes 786436
  212.9 2.3 copy-start
  261.1 0.7 copy-start.1
  261.7 0.8 copy-start.4
  262.5 0.6 copy-start.5
  273.7 3.5 copy-start.9
  350.2 22.4 %all-to-all-start.3 = ((bf16[16,40,1024]{2,1,0:T(8,128)(2,1)}), bf16[16,40,1024]{2,1,0:T(8,128)(2,1)}, u32[]{:S(2)}, u32[]{:S(2)}) async-start(bf16[16,40,1024]{2,1,0:T(8,128)(2,1)} %bitcast.136), calls=%async_computation.3 | async-start | bytes 2621440 | tf_op jit(solution)/shard_map/all_to_all | solution.py:628
  354.5 348.4 %all-gather.4.cloned.1.call-start = ((), (), s32[]{:S(2)}) async-start(), calls=%async_computation.7 | async-start | bytes 4718592 | tf_op jit(solution)/shard_map/all_gather | solution.py:693
  372.6 76.6 %all-to-all-start.4 = ((bf16[16,40,1024]{2,1,0:T(8,128)(2,1)}), bf16[16,40,1024]{2,1,0:T(8,128)(2,1)}, u32[]{:S(2)}, u32[]{:S(2)}) async-start(bf16[16,40,1024]{2,1,0:T(8,128)(2,1)} %bitcast.135), calls=%async_computation.4 | async-start | bytes 2621440 | tf_op jit(solution)/shard_map/all_to_all | solution.py:628
  445.8 2.4 copy-start.17
  483.8 230.1 %all-to-all-start.6 = ((bf16[8,2,192,1024]{3,2,1,0:T(8,128)(2,1)}), bf16[8,2,192,1024]{3,2,1,0:T(8,128)(2,1)}, u32[]{:S(2)}, u32[]{:S(2)}) async-start(bf16[8,2,192,1024]{3,2,1,0:T(8,128)(2,1)} %get-tuple-element.28), calls=%async_computation.6 | async-start | bytes 12582912 | tf_op jit(solution)/shard_map/all_to_all | solution.py:634
  682.8 3.3 copy-start.21
  685.8 0.8 copy-start.27
  685.8 0.8 copy-start.29
  685.8 0.8 copy-start.33
  685.8 0.8 copy-start.35
  686.4 1.6 copy-start.14
  689.6 13.3 %copy-start.23 = (f32[1024]{0:T(1024)S(1)}, f32[1024]{0:T(1024)}, u32[]{:S(2)}) copy-start(f32[1024]{0:T(1024)} %copy-done.22) | copy-start | bytes 12292
  703.0 3.9 copy-start.15
  703.0 4.9 copy-start.18
  710.1 3.1 copy-start.2
  710.1 3.1 copy-start.6
  713.8 4.4 copy-start.11
  718.3 1.0 copy-start.13
  736.4 13.3 %copy-start.38 = (bf16[8]{0:T(256)(128)(2,1)S(1)}, bf16[8]{0:T(256)(128)(2,1)}, u32[]{:S(2)}) copy-start(bf16[8]{0:T(256)(128)(2,1)} %param.12) | copy-start | bytes 52
Sparse Core Ops, SparseCore 0:
  12.1 117.5 all-gather.5
  358.3 94.2 all-gather.3

commit v2 on v1

v2 whole, which is shorter than its diff:
```python
import functools
import math

import jax
import jax.numpy as jnp
from jax import lax
from jax.experimental import pallas as pl
from jax.experimental.pallas import tpu as pltpu
from jax.sharding import PartitionSpec as P

HEADS = 16
KV = 8
HEAD = 64
EXPERTS = 32
TOPK = 8
TOK_DEV = 128
CAP = 40
WIDTH = 1024
FF = 512
N_SEQ = 8
N_SHARD = 16
HEAD_ROWS = TOK_DEV * N_SEQ
TOKENS = TOK_DEV * N_SEQ * N_SHARD
LOCAL_EXPERTS = EXPERTS // N_SHARD
EXPERT_ROWS = N_SHARD * CAP
COLS = 256
SUPER = TOK_DEV * N_SHARD
BWD_TILE = 1024

epsilon = 1e-06
rope_base = 10000.0

f32 = jnp.float32
bf16 = jnp.bfloat16
MESH = pl.DeviceIdType.MESH
ANY = pl.BlockSpec(memory_space=pl.ANY)
NT = (((1,), (1,)), ((), ()))
NN = (((1,), (0,)), ((), ()))
TN = (((0,), (0,)), ((), ()))


def dot(left, right, dims):
    return lax.dot_general(left, right, dims, preferred_element_type=f32)


def greet(peers):
    barrier = pltpu.get_barrier_semaphore()
    for axis, peer in peers:
        pl.semaphore_signal(barrier, inc=1, device_id={axis: peer}, device_id_type=MESH)
    pl.semaphore_wait(barrier, len(peers))


def remote(source, target, send, recv, axis, peer):
    copy = pltpu.make_async_remote_copy(
        src_ref=source,
        dst_ref=target,
        send_sem=send,
        recv_sem=recv,
        device_id={axis: peer},
        device_id_type=MESH,
    )
    copy.start()
    return copy


def exchange_kernel(axis, count, dim, x_ref, o_ref, send, recv, own):
    def block(ref, index):
        return ref.at[:, index] if dim == 1 else ref.at[index]

    me = lax.axis_index(axis)
    greet([(axis, lax.rem(me + k, count)) for k in range(1, count)])
    mine = pltpu.make_async_copy(block(x_ref, me), block(o_ref, me), own)
    mine.start()
    copies = []
    for k in range(1, count):
        peer = lax.rem(me + k, count)
        copies.append(
            remote(block(x_ref, peer), block(o_ref, me), send.at[k - 1], recv.at[k - 1], axis, peer)
        )
    mine.wait()
    for copy in copies:
        copy.wait()


def exchange(x, axis, count, ident, dim=0):
    return pl.pallas_call(
        functools.partial(exchange_kernel, axis, count, dim),
        out_shape=jax.ShapeDtypeStruct(x.shape, x.dtype),
        in_specs=[ANY],
        out_specs=ANY,
        scratch_shapes=[
            pltpu.SemaphoreType.DMA((count - 1,)),
            pltpu.SemaphoreType.DMA((count - 1,)),
            pltpu.SemaphoreType.DMA,
        ],
        compiler_params=pltpu.CompilerParams(collective_id=ident, has_side_effects=True),
        name="exchange_" + axis,
    )(x)


def staged(axis, units, share, x_ref, place, sem_send, sem_recv, own):
    me = lax.axis_index(axis)
    cores = 2 if axis == "shard" else 1
    core = lax.rem(me, cores)
    pair = lax.rem(me // cores, 2)
    ring = me // (2 * cores)

    def at(r, p, c):
        return (r * 2 + p) * cores + c

    ring_peer = [at(lax.rem(ring + k, 4), pair, core) for k in (1, 2, 3)]
    ring_from = [lax.rem(ring + 4 - k, 4) for k in (1, 2, 3)]
    pair_peer = at(ring, 1 - pair, core)
    core_peer = at(ring, pair, 1 - core)
    mine = pltpu.make_async_copy(x_ref, place(me, 0, units), own)
    mine.start()
    sends = []

    def go(source, index, low, high, peer):
        n = len(sends)
        sends.append(
            remote(source, place(index, low, high), sem_send.at[n], sem_recv.at[n], axis, peer)
        )
        return sends[-1]

    to_pair = go(x_ref, me, 0, units, pair_peer)
    to_ring = [go(x_ref, me, 0, units, peer) for peer in ring_peer]
    landed = []
    if cores == 2:
        landed.append(go(x_ref, me, 0, units, core_peer))

    def pass_core(index, low, high):
        if cores == 2:
            landed.append(go(place(index, low, high), index, low, high, core_peer))

    to_pair.wait_recv()
    fwd_ring = [
        go(place(pair_peer, 0, share), pair_peer, 0, share, peer) for peer in ring_peer
    ]
    pass_core(pair_peer, 0, units)
    fwd_pair = []
    for k in (0, 2, 1):
        to_ring[k].wait_recv()
        source = at(ring_from[k], pair, core)
        if share < units:
            fwd_pair.append((k, go(place(source, share, units), source, share, units, pair_peer)))
        pass_core(source, 0, units)
    for k in (0, 2, 1):
        fwd_ring[k].wait_recv()
        pass_core(at(ring_from[k], 1 - pair, core), 0, share)
    for k, copy in fwd_pair:
        copy.wait_recv()
        pass_core(at(ring_from[k], 1 - pair, core), share, units)
    for copy in landed:
        copy.wait_recv()
    mine.wait()
    for copy in sends:
        copy.wait_send()


def first_kernel(
    x_ref, w_ref, v_ref, xo_ref, wo_ref, vo_ref, w_mid, w_pack, send, recv, own, wsend, wrecv, wown, vown
):
    seq = lax.axis_index("seq")
    shard = lax.axis_index("shard")
    far = lax.rem(seq, 2)
    partner = seq + 1 - 2 * far
    greet(
        [("seq", lax.rem(seq + k, N_SEQ)) for k in range(1, N_SEQ)]
        + [("shard", lax.rem(shard + k, N_SHARD)) for k in range(1, N_SHARD)]
    )
    mine = pltpu.make_async_copy(w_ref.at[seq], w_mid.at[seq], wown)
    mine.start()
    slab = pltpu.make_async_copy(v_ref, vo_ref.at[far, shard], vown)
    slab.start()
    pieces = []
    for k in range(1, N_SEQ):
        peer = lax.rem(seq + k, N_SEQ)
        pieces.append(
            remote(w_ref.at[peer], w_mid.at[seq], wsend.at[k - 1], wrecv.at[k - 1], "seq", peer)
        )
    rows = []
    for k in range(1, N_SHARD):
        peer = lax.rem(shard + k, N_SHARD)
        n = 21 + k
        rows.append(
            remote(v_ref, vo_ref.at[far, shard], wsend.at[n], wrecv.at[n], "shard", peer)
        )
    mine.wait()
    for piece in pieces:
        piece.wait()
    packed = jnp.zeros((16, 128), f32)
    row = lax.broadcasted_iota(jnp.int32, (16, 128), 0)
    for s in range(N_SEQ):
        packed = jnp.where(row == s, w_mid[s, 16:].astype(f32), packed)
        w_pack[s] = w_mid[s, :16]
    w_pack[N_SEQ] = packed.astype(bf16)
    mine = pltpu.make_async_copy(w_pack, wo_ref.at[shard], wown)
    mine.start()
    pieces = []
    for k in range(1, N_SHARD):
        peer = lax.rem(shard + k, N_SHARD)
        n = 6 + k
        pieces.append(
            remote(w_pack, wo_ref.at[shard], wsend.at[n], wrecv.at[n], "shard", peer)
        )
    staged("seq", 8, 8, x_ref, lambda s, low, high: xo_ref.at[s, low:high], send, recv, own)
    slab.wait()
    for row in rows:
        row.wait()
    pair = remote(vo_ref.at[far], vo_ref.at[far], wsend.at[37], wrecv.at[37], "seq", partner)
    mine.wait()
    for piece in pieces:
        piece.wait()
    pair.wait()


def first_gather(x, pieces, rows, ident):
    return pl.pallas_call(
        first_kernel,
        out_shape=[
            jax.ShapeDtypeStruct((N_SEQ, 8, TOK_DEV // 8, WIDTH), bf16),
            jax.ShapeDtypeStruct((N_SHARD, N_SEQ + 1, 16, 128), bf16),
            jax.ShapeDtypeStruct((2, N_SHARD) + rows.shape, bf16),
        ],
        in_specs=[ANY, ANY, ANY],
        out_specs=[ANY, ANY, ANY],
        scratch_shapes=[
            pltpu.VMEM(pieces.shape, bf16),
            pltpu.VMEM((N_SEQ + 1, 16, 128), bf16),
            pltpu.SemaphoreType.DMA((12,)),
            pltpu.SemaphoreType.DMA((12,)),
            pltpu.SemaphoreType.DMA,
            pltpu.SemaphoreType.DMA((38,)),
            pltpu.SemaphoreType.DMA((38,)),
            pltpu.SemaphoreType.DMA,
            pltpu.SemaphoreType.DMA,
        ],
        compiler_params=pltpu.CompilerParams(collective_id=ident, has_side_effects=True),
        name="gather_tokens",
    )(x, pieces, rows)


def spread(rows, right):
    zeros = jnp.zeros((TOK_DEV, HEAD), rows.dtype)
    parts = [rows[:, :HEAD], rows[:, HEAD:]]
    if right:
        parts = [jnp.concatenate([zeros, part], axis=1) for part in parts]
    else:
        parts = [jnp.concatenate([part, zeros], axis=1) for part in parts]
    return jnp.concatenate(parts, axis=0)


def admitted(shape, j, first_key):
    key_pos = first_key + lax.broadcasted_iota(jnp.int32, shape, 0)
    query_pos = j * TOK_DEV + (lax.broadcasted_iota(jnp.int32, shape, 1) & (TOK_DEV - 1))
    return query_pos >= key_pos


def transfer(source, target, send, recv, axis, peer):
    return pltpu.make_async_remote_copy(
        src_ref=source,
        dst_ref=target,
        send_sem=send,
        recv_sem=recv,
        device_id={axis: peer},
        device_id_type=MESH,
    )


def everyone(seq, shard):
    return [("seq", lax.rem(seq + k, N_SEQ)) for k in range(1, N_SEQ)] + [
        ("shard", lax.rem(shard + k, N_SHARD)) for k in range(1, N_SHARD)
    ]


def attention_kernel(
    q_ref,
    kv_ref,
    cot_ref,
    slab_ref,
    wide_ref,
    lse_ref,
    att_ref,
    mem_ref,
    cot_out,
    slab_out,
    land,
    vt,
    heads,
    peak_ref,
    total_ref,
    acc_ref,
    ksend,
    krecv,
    gsend,
    grecv,
    esend,
    erecv,
    fsend,
    frecv,
    own,
    msem,
):
    seq = lax.axis_index("seq")
    me = lax.axis_index("shard")
    core = lax.rem(me, 2)
    pair = lax.rem(me // 2, 2)
    ring = me // 4

    def at(k, other_pair, other_core):
        p = 1 - pair if other_pair else pair
        c = 1 - core if other_core else core
        return (lax.rem(ring + 4 + k, 4) * 2 + p) * 2 + c

    def message(t, m, block, peer):
        return transfer(
            land.at[t, block], land.at[t, block], ksend.at[t, m], krecv.at[t, m], "shard", peer
        )

    def first(t):
        for k in (1, 2, 3):
            message(t, k - 1, me, at(k, 0, 0)).start()
        message(t, 3, me, at(0, 1, 0)).start()
        message(t, 4, me, at(0, 0, 1)).start()

    def second(t):
        block = at(0, 1, 0)
        message(t, 3, block, block).wait_recv()
        for k in (1, 2, 3):
            message(t, 4 + k, block, at(k, 0, 0)).start()
        message(t, 8, block, at(0, 0, 1)).start()
        for k in (1, 2, 3):
            block = at(-k, 0, 0)
            message(t, k - 1, block, block).wait_recv()
            message(t, 8 + k, block, at(0, 0, 1)).start()

    def third(t):
        for k in (1, 2, 3):
            block = at(-k, 1, 0)
            message(t, 4 + k, block, at(-k, 0, 0)).wait_recv()
            message(t, 11 + k, block, at(0, 0, 1)).start()

    def fourth(t):
        peer = at(0, 0, 1)
        message(t, 4, peer, peer).wait_recv()
        message(t, 8, at(0, 1, 1), peer).wait_recv()
        for k in (1, 2, 3):
            message(t, 8 + k, at(-k, 0, 1), peer).wait_recv()
            message(t, 11 + k, at(-k, 1, 1), peer).wait_recv()

    def to_expert(k):
        peer = lax.rem(me + k, N_SHARD)
        return transfer(
            cot_ref.at[peer], cot_out.at[me], esend.at[k - 1], erecv.at[k - 1], "shard", peer
        )

    def to_ring(k):
        peer = lax.rem(seq + 2 * k, N_SEQ)
        return transfer(slab_ref, slab_out.at[k], fsend.at[k - 1], frecv.at[k - 1], "seq", peer)

    def to_token(t, source):
        return transfer(
            heads.at[t], att_ref.at[source], gsend.at[t], grecv.at[source], "seq", t
        )

    greet(everyone(seq, me))

    def begin(t, carry):
        land[t, me] = kv_ref[t]
        first(t)
        peak_ref[t] = jnp.full((1, 2 * TOK_DEV), -1e30, f32)
        total_ref[t] = jnp.zeros((1, 2 * TOK_DEV), f32)
        acc_ref[t] = jnp.zeros((HEAD, 2 * TOK_DEV), f32)
        return carry

    lax.fori_loop(0, N_SEQ, begin, 0)
    second(0)
    third(0)
    second(1)
    fourth(0)
    for k in range(1, N_SHARD):
        to_expert(k).start()
    for k in (1, 2, 3):
        to_ring(k).start()
    cot_own = pltpu.make_async_copy(cot_ref.at[me], cot_out.at[me], own.at[0])
    cot_own.start()
    slab_own = pltpu.make_async_copy(slab_ref, slab_out.at[0], own.at[1])
    slab_own.start()

    def tile(t, i, masked):
        queries = spread(q_ref[i], False)
        scores = dot(land[t].reshape(SUPER, 2 * HEAD), queries, NT)
        if masked:
            scores = jnp.where(admitted(scores.shape, me, 0), scores, -1e30)
        peak = peak_ref[i]
        newest = jnp.maximum(peak, jnp.max(scores, axis=0, keepdims=True))
        weights = jnp.exp(scores - newest)
        shrink = jnp.exp(peak - newest)
        total = total_ref[i] * shrink + jnp.sum(weights, axis=0, keepdims=True)
        acc = acc_ref[i] * shrink + dot(vt[...], weights.astype(bf16), NN)
        return newest, total, acc

    def step(t, carry):
        pltpu.make_async_copy(land.at[t], mem_ref.at[t], msem.at[t]).start()

        @pl.when(t + 1 < N_SEQ)
        def _():
            third(t + 1)

        @pl.when(t + 2 < N_SEQ)
        def _():
            second(t + 2)

        for n in range(4):
            rows = land[t, 4 * n : 4 * n + 4].reshape(512, 2 * HEAD)
            vt[:, 512 * n : 512 * n + 512] = rows.T[HEAD:]
        newest, total, acc = tile(t, t, True)
        acc = acc / total
        stacked = jnp.concatenate([acc[:, :TOK_DEV], acc[:, TOK_DEV:]], axis=0)
        wide_ref[t] = stacked
        heads[t] = stacked.T.astype(bf16)
        lse_ref[t] = newest + jnp.log(total)

        @pl.when(t != seq)
        def _():
            to_token(t, seq).start()

        def rest(i, inner):
            peak_ref[i], total_ref[i], acc_ref[i] = tile(t, i, False)
            return inner

        lax.fori_loop(t + 1, N_SEQ, rest, 0)

        @pl.when(t + 1 < N_SEQ)
        def _():
            fourth(t + 1)

        return carry

    lax.fori_loop(0, N_SEQ, step, 0)
    mine = pltpu.make_async_copy(heads.at[seq], att_ref.at[seq], own.at[2])
    mine.start()
    for k in range(1, N_SEQ):
        to_token(lax.rem(seq + k, N_SEQ), seq).wait_send()
        source = lax.rem(seq + k, N_SEQ)
        to_token(source, source).wait_recv()
    mine.wait()
    cot_own.wait()
    slab_own.wait()
    for k in range(1, N_SHARD):
        to_expert(k).wait()
    for k in (1, 2, 3):
        to_ring(k).wait()

    def end(t, carry):
        for m in range(15):
            message(t, m, me, me).wait_send()
        pltpu.make_async_copy(land.at[t], mem_ref.at[t], msem.at[t]).wait()
        return carry

    lax.fori_loop(0, N_SEQ, end, 0)


def attention(queries, memory, cot_rows, slab, ident):
    dma = pltpu.SemaphoreType.DMA
    vmem = pl.BlockSpec(memory_space=pltpu.VMEM)
    return pl.pallas_call(
        attention_kernel,
        in_specs=[vmem, vmem, ANY, ANY],
        out_specs=[vmem, vmem, ANY, ANY, ANY, ANY],
        out_shape=[
            jax.ShapeDtypeStruct((N_SEQ, 2 * HEAD, TOK_DEV), f32),
            jax.ShapeDtypeStruct((N_SEQ, 1, 2 * TOK_DEV), f32),
            jax.ShapeDtypeStruct((N_SEQ, TOK_DEV, 2 * HEAD), bf16),
            jax.ShapeDtypeStruct((N_SEQ, N_SHARD, TOK_DEV, 2 * HEAD), bf16),
            jax.ShapeDtypeStruct(cot_rows.shape, bf16),
            jax.ShapeDtypeStruct((4,) + slab.shape, bf16),
        ],
        scratch_shapes=[
            pltpu.VMEM((N_SEQ, N_SHARD, TOK_DEV, 2 * HEAD), bf16),
            pltpu.VMEM((HEAD, SUPER), bf16),
            pltpu.VMEM((N_SEQ, TOK_DEV, 2 * HEAD), bf16),
            pltpu.VMEM((N_SEQ, 1, 2 * TOK_DEV), f32),
            pltpu.VMEM((N_SEQ, 1, 2 * TOK_DEV), f32),
            pltpu.VMEM((N_SEQ, HEAD, 2 * TOK_DEV), f32),
            dma((N_SEQ, 15)),
            dma((N_SEQ, 15)),
            dma((N_SEQ,)),
            dma((N_SEQ,)),
            dma((N_SHARD - 1,)),
            dma((N_SHARD - 1,)),
            dma((3,)),
            dma((3,)),
            dma((3,)),
            dma((N_SEQ,)),
        ],
        compiler_params=pltpu.CompilerParams(
            collective_id=ident, has_side_effects=True, vmem_limit_bytes=48 << 20
        ),
        name="attention_forward",
    )(queries, memory, cot_rows, slab)


def attention_back_kernel(*refs):
    (q_ref, g_ref, wide_ref, lse_ref, mem_ref, cos_ref, sin_ref, turn_ref, eo_ref) = refs[:9]
    parts = refs[9:15]
    pgq_ref, pgm_ref, tokq_ref, tokm_ref, came_ref = refs[15:20]
    parts_out = refs[20:26]
    gl, qs, gs, delta_ref, kt, acc, dq, stage, dl = refs[26:35]
    dsend, drecv, osend, orecv, jsend, jrecv, psend, precv, nsend, nrecv, own = refs[35:]
    seq = lax.axis_index("seq")
    me = lax.axis_index("shard")

    def to_head(k, source, peer):
        return transfer(
            g_ref.at[peer], gl.at[source], osend.at[k - 1], orecv.at[k - 1], "seq", peer
        )

    def to_token_expert(k):
        peer = lax.rem(me + k, N_SHARD)
        return transfer(
            eo_ref.at[:, peer], came_ref.at[:, me], jsend.at[k - 1], jrecv.at[k - 1], "shard", peer
        )

    def to_ring(n):
        peer = lax.rem(seq + 2 * (n % 3 + 1), N_SEQ)
        return transfer(parts[n], parts_out[n], psend.at[n], precv.at[n], "seq", peer)

    def to_owner(t, k, block, source, peer):
        return transfer(
            stage.at[t, block], dl.at[t, source], dsend.at[t, k - 1], drecv.at[t, k - 1], "shard", peer
        )

    def to_token(n, t, source):
        ref, out = ((pgq_ref, tokq_ref), (pgm_ref, tokm_ref))[n]
        return transfer(
            ref.at[t], out.at[source], nsend.at[n, t], nrecv.at[n, source], "seq", t
        )

    greet(everyone(seq, me))
    for k in range(1, N_SEQ):
        to_head(k, seq, lax.rem(seq + k, N_SEQ)).start()
    mine = pltpu.make_async_copy(g_ref.at[seq], gl.at[seq], own.at[0])
    mine.start()
    came_own = pltpu.make_async_copy(eo_ref.at[:, me], came_ref.at[:, me], own.at[1])
    came_own.start()
    mine.wait()
    for k in range(1, N_SEQ):
        source = lax.rem(seq + N_SEQ - k, N_SEQ)
        to_head(k, source, source).wait_recv()
    for n in range(6):
        to_ring(n).start()
    for k in range(1, N_SHARD):
        to_token_expert(k).start()

    def begin(i, carry):
        qs[i] = spread(q_ref[i], False)
        gs[i] = spread(gl[i], True)
        product = wide_ref[i] * gl[i].astype(f32).T
        delta_ref[i] = jnp.concatenate(
            [
                jnp.sum(product[:HEAD], axis=0, keepdims=True),
                jnp.sum(product[HEAD:], axis=0, keepdims=True),
            ],
            axis=1,
        )
        dq[i] = jnp.zeros((HEAD, 2 * TOK_DEV), f32)
        return carry

    lax.fori_loop(0, N_SEQ, begin, 0)

    def tile(t, i, n, masked):
        here = slice(n * BWD_TILE, (n + 1) * BWD_TILE)
        memory = mem_ref[t, 8 * n : 8 * n + 8].reshape(BWD_TILE, 2 * HEAD)
        scores = dot(memory, qs[i], NT)
        weights = jnp.exp(scores - lse_ref[i])
        if masked:
            weights = jnp.where(admitted(scores.shape, me, n * BWD_TILE), weights, 0.0)
        weight_grad = dot(memory, gs[i], NT)
        score_grad = (weights * (weight_grad - delta_ref[i])).astype(bf16)
        here_grad = dot(weights.astype(bf16), gs[i], NN) + dot(score_grad, qs[i], NN)
        if masked:
            acc[here, :] = here_grad
        else:
            acc[here, :] += here_grad
        dq[i] += dot(kt[:, here], score_grad, NN)

    def step(t, carry):
        for n in range(4):
            rows = mem_ref[t, 4 * n : 4 * n + 4].reshape(512, 2 * HEAD)
            kt[:, 512 * n : 512 * n + 512] = rows.T[:HEAD]
        tile(t, t, 0, True)
        tile(t, t, 1, True)
        grad = dq[t] * (1.0 / math.sqrt(HEAD))
        grad = jnp.concatenate([grad[:, :TOK_DEV], grad[:, TOK_DEV:]], axis=0).T.astype(bf16)
        turned = dot(grad, turn_ref[0], NT)
        grad = grad.astype(f32) * cos_ref[0, t] + turned * sin_ref[0, t]
        pgq_ref[t] = grad.astype(bf16)

        @pl.when(t != seq)
        def _():
            to_token(0, t, seq).start()

        def rest(i, inner):
            tile(t, i, 0, False)
            tile(t, i, 1, False)
            return inner

        lax.fori_loop(t + 1, N_SEQ, rest, 0)
        for n in range(4):
            rows = acc[512 * n : 512 * n + 512, :].astype(bf16)
            stage[t, 4 * n : 4 * n + 4] = rows.reshape(4, TOK_DEV, 2 * HEAD)
        dl[t, me] = stage[t, me]
        for k in range(1, N_SHARD):
            peer = lax.rem(me + k, N_SHARD)
            to_owner(t, k, peer, me, peer).start()
        return carry

    lax.fori_loop(0, N_SEQ, step, 0)

    def gathered(t, carry):
        for k in range(1, N_SHARD):
            source = lax.rem(me + N_SHARD - k, N_SHARD)
            to_owner(t, k, source, source, source).wait_recv()
        grad = jnp.sum(dl[t].astype(f32), axis=0).astype(bf16)
        turned = dot(grad, turn_ref[1], NT)
        grad = grad.astype(f32) * cos_ref[1, t] + turned * sin_ref[1, t]
        pgm_ref[t] = grad.astype(bf16)

        @pl.when(t != seq)
        def _():
            to_token(1, t, seq).start()

        return carry

    lax.fori_loop(0, N_SEQ, gathered, 0)
    mine = pltpu.make_async_copy(pgq_ref.at[seq], tokq_ref.at[seq], own.at[2])
    mine.start()
    other = pltpu.make_async_copy(pgm_ref.at[seq], tokm_ref.at[seq], own.at[3])
    other.start()
    for k in range(1, N_SEQ):
        to_head(k, seq, lax.rem(seq + k, N_SEQ)).wait_send()
    for k in range(1, N_SHARD):
        to_token_expert(k).wait()
    came_own.wait()
    for n in range(6):
        to_ring(n).wait()

    def end(t, carry):
        for k in range(1, N_SHARD):
            peer = lax.rem(me + k, N_SHARD)
            to_owner(t, k, peer, me, peer).wait_send()
        return carry

    lax.fori_loop(0, N_SEQ, end, 0)
    for n in range(2):
        for k in range(1, N_SEQ):
            peer = lax.rem(seq + k, N_SEQ)
            to_token(n, peer, seq).wait_send()
            to_token(n, peer, peer).wait_recv()
    mine.wait()
    other.wait()


def attention_back(
    queries, upstream, wide, lse, memory, cosine, sine, turn, expert_out, parts, ident
):
    dma = pltpu.SemaphoreType.DMA
    vmem = pl.BlockSpec(memory_space=pltpu.VMEM)
    chunk = jax.ShapeDtypeStruct((N_SEQ, TOK_DEV, 2 * HEAD), bf16)
    return pl.pallas_call(
        attention_back_kernel,
        in_specs=[vmem, ANY, vmem, vmem, vmem, vmem, vmem, vmem, ANY] + [ANY] * 6,
        out_specs=[vmem, vmem, ANY, ANY, ANY] + [ANY] * 6,
        out_shape=[chunk] * 4
        + [jax.ShapeDtypeStruct(expert_out.shape, bf16)]
        + [jax.ShapeDtypeStruct(part.shape, bf16) for part in parts],
        scratch_shapes=[
            pltpu.VMEM((N_SEQ, TOK_DEV, 2 * HEAD), bf16),
            pltpu.VMEM((N_SEQ, 2 * TOK_DEV, 2 * HEAD), bf16),
            pltpu.VMEM((N_SEQ, 2 * TOK_DEV, 2 * HEAD), bf16),
            pltpu.VMEM((N_SEQ, 1, 2 * TOK_DEV), f32),
            pltpu.VMEM((HEAD, SUPER), bf16),
            pltpu.VMEM((SUPER, 2 * HEAD), f32),
            pltpu.VMEM((N_SEQ, HEAD, 2 * TOK_DEV), f32),
            pltpu.VMEM((N_SEQ, N_SHARD, TOK_DEV, 2 * HEAD), bf16),
            pltpu.VMEM((N_SEQ, N_SHARD, TOK_DEV, 2 * HEAD), bf16),
            dma((N_SEQ, 15)),
            dma((N_SEQ, 15)),
            dma((N_SEQ - 1,)),
            dma((N_SEQ - 1,)),
            dma((N_SHARD - 1,)),
            dma((N_SHARD - 1,)),
            dma((6,)),
            dma((6,)),
            dma((2, N_SEQ)),
            dma((2, N_SEQ)),
            dma((4,)),
        ],
        compiler_params=pltpu.CompilerParams(
            collective_id=ident, has_side_effects=True, vmem_limit_bytes=56 << 20
        ),
        name="attention_backward",
    )(queries, upstream, wide, lse, memory, cosine, sine, turn, expert_out, *parts)


def expert_kernel(s_ref, x_ref, g_ref, w_ref, out_ref, back_ref, *refs):
    grad_refs, (gu, down, xt, ht, both) = refs[:4], refs[4:]
    gu[...] = w_ref[0, :, :128, :].reshape(WIDTH, 2 * FF)
    down[...] = w_ref[0, :, 128:, :].reshape(FF, WIDTH)

    def rows_step(t, carry):
        rows = pl.ds(pl.multiple_of(t * 128, 128), 128)
        x = x_ref[0, rows, :]
        pre = dot(x, gu[...], NN)
        gate, up = pre[:, :FF], pre[:, FF:]
        sigmoid = jax.nn.sigmoid(gate)
        act = gate * sigmoid
        hidden = (act * up).astype(bf16)
        out_ref[0, rows, :] = dot(hidden, down[...], NN).astype(bf16)
        units = dot(g_ref[0, rows, :], down[...], NT)
        gate_grad = (units * up * sigmoid * (1.0 + gate * (1.0 - sigmoid))).astype(bf16)
        up_grad = (units * act).astype(bf16)
        pair = jnp.concatenate([gate_grad, up_grad], axis=1)
        back_ref[0, rows, :] = dot(pair, gu[...], NT).astype(bf16)
        both[rows, :] = pair
        xt[:, rows] = x.T
        ht[:, rows] = hidden.T
        return carry

    lax.fori_loop(0, EXPERT_ROWS // 128, rows_step, 0)
    far = s_ref[0] % 2
    ring = s_ref[0] // 2
    for k in range(4):

        def grad_step(n, carry, k=k):
            s = (ring + k) % 4 * 2 + (far + n) % 2
            features = pl.ds(pl.multiple_of(s * 128, 128), 128)
            units = pl.ds(pl.multiple_of(s * 64, 64), 64)
            grad_refs[k][n, 0, :128, :] = dot(xt[features, :], both[...], NN).astype(bf16)
            grad_refs[k][n, 0, 128:, :] = dot(ht[units, :], g_ref[0], NN).astype(bf16)
            return carry

        lax.fori_loop(0, 2, grad_step, 0)


def experts(seq, x, g, w):
    rows = pl.BlockSpec((1, EXPERT_ROWS, WIDTH), lambda e, s: (e, 0, 0))
    shape = jax.ShapeDtypeStruct((LOCAL_EXPERTS, EXPERT_ROWS, WIDTH), bf16)
    return pl.pallas_call(
        expert_kernel,
        grid_spec=pltpu.PrefetchScalarGridSpec(
            num_scalar_prefetch=1,
            grid=(LOCAL_EXPERTS,),
            in_specs=[
                rows,
                rows,
                pl.BlockSpec((1, N_SEQ, 192, WIDTH), lambda e, s: (e, 0, 0, 0)),
            ],
            out_specs=[rows, rows]
            + [pl.BlockSpec((2, 1, 192, WIDTH), lambda e, s: (0, e, 0, 0))] * 4,
            scratch_shapes=[
                pltpu.VMEM((WIDTH, 2 * FF), bf16),
                pltpu.VMEM((FF, WIDTH), bf16),
                pltpu.VMEM((WIDTH, EXPERT_ROWS), bf16),
                pltpu.VMEM((FF, EXPERT_ROWS), bf16),
                pltpu.VMEM((EXPERT_ROWS, 2 * FF), bf16),
            ],
        ),
        out_shape=[shape, shape]
        + [jax.ShapeDtypeStruct((2, LOCAL_EXPERTS, 192, WIDTH), bf16)] * 4,
        compiler_params=pltpu.CompilerParams(vmem_limit_bytes=56 << 20),
        cost_estimate=pl.CostEstimate(
            flops=10**8, bytes_accessed=1 << 20, transcendentals=10**5
        ),
        name="experts",
    )(seq, x, g, w)


def group_columns(rows):
    lead = rows.shape[:-1]
    queries = rows[..., : HEADS * HEAD].reshape(lead + (N_SEQ, 2 * HEAD))
    keys = rows[..., HEADS * HEAD : (HEADS + KV) * HEAD].reshape(lead + (N_SEQ, HEAD))
    values = rows[..., (HEADS + KV) * HEAD :].reshape(lead + (N_SEQ, HEAD))
    return jnp.concatenate([queries, keys, values], axis=-1)


def ungroup_columns(groups):
    rows = groups.shape[0]
    return jnp.concatenate(
        [
            groups[:, :, : 2 * HEAD].reshape(rows, HEADS * HEAD),
            groups[:, :, 2 * HEAD : 3 * HEAD].reshape(rows, KV * HEAD),
            groups[:, :, 3 * HEAD :].reshape(rows, KV * HEAD),
        ],
        axis=1,
    )


def rope_pair(shard):
    half = HEAD // 2
    frequency = jnp.exp(
        jnp.arange(half, dtype=f32) * jnp.float32(-2.0 * math.log(rope_base) / HEAD)
    )
    chunk = jnp.arange(N_SEQ, dtype=jnp.int32)[:, None] * N_SHARD + shard
    position = chunk * TOK_DEV + jnp.arange(TOK_DEV, dtype=jnp.int32)[None, :]
    angles = position.reshape(HEAD_ROWS, 1).astype(f32) * frequency[None, :]
    return jnp.tile(jnp.cos(angles), (1, 6)), jnp.tile(jnp.sin(angles), (1, 6))


def turn_matrix():
    row = jnp.arange(3 * HEAD, dtype=jnp.int32)[:, None]
    col = jnp.arange(3 * HEAD, dtype=jnp.int32)[None, :]
    half = HEAD // 2
    low = col % HEAD < half
    minus = low & (row == col + half)
    plus = (~low) & (row == col - half)
    return (plus.astype(f32) - minus.astype(f32)).astype(bf16)


def after(value, *others):
    return lax.optimization_barrier((value,) + others)[0]


def routing(routes, route_weights):
    ids = jnp.arange(EXPERTS, dtype=jnp.int32)
    hit = routes[:, :, None] == ids[None, None, :]
    mask = jnp.sum(hit.astype(f32), axis=1)
    weight = jnp.sum(jnp.where(hit, route_weights[:, :, None], 0.0), axis=1)
    token = jnp.arange(TOK_DEV, dtype=jnp.int32)
    earlier = (token[:, None] > token[None, :]).astype(bf16)
    before = dot(earlier, mask.astype(bf16), NN)
    code = jnp.where(mask > 0.0, before, -1.0).astype(bf16)
    slot = jnp.arange(EXPERTS * CAP, dtype=jnp.int32)
    owner = slot // CAP % N_SHARD * LOCAL_EXPERTS + slot // (CAP * N_SHARD)
    widen = (owner[None, :] == ids[:, None]).astype(bf16)
    pick = dot(code, widen, NN) == (slot % CAP).astype(f32)[None, :]
    high = weight.astype(bf16)
    low = (weight - high.astype(f32)).astype(bf16)
    high = jnp.where(pick, dot(high, widen, NN), 0.0)
    low = jnp.where(pick, dot(low, widen, NN), 0.0)
    return pick.astype(bf16), high.astype(bf16), low.astype(bf16), jnp.sum(high + low, axis=0)


def on_device(
    layer_input,
    attn_gain,
    moe_gain,
    w_qkv,
    w_out,
    w_gate,
    w_up,
    w_down,
    routes,
    route_weights,
    cotangent,
):
    seq = lax.axis_index("seq")
    shard = lax.axis_index("shard")
    seq_array = seq.astype(jnp.int32).reshape(1)
    along_x = [(s, s + 1 - 2 * (s % 2)) for s in range(N_SEQ)]

    grouped = group_columns(w_qkv)
    pieces = grouped.reshape(8, N_SEQ, 2, 128).transpose(1, 2, 0, 3)
    gains = jnp.concatenate([attn_gain, moe_gain, jnp.zeros((112,), bf16)])
    gains = jnp.broadcast_to(gains[None, None, :], (N_SEQ, 16, 128))
    pieces = jnp.concatenate([pieces.reshape(N_SEQ, 16, 128), gains], axis=1)
    out_rows = w_out.reshape(8, 8, 128).transpose(1, 0, 2).reshape(2, 32, 128)
    tokens, columns, out_slabs = first_gather(
        layer_input.reshape(8, TOK_DEV // 8, WIDTH), pieces, out_rows, 1
    )
    out_slabs = out_slabs.reshape(2, N_SHARD, 8, 8, 128).transpose(0, 1, 3, 2, 4)
    out_slabs = out_slabs.reshape(2 * N_SHARD * 8, WIDTH)
    expert_pack = jnp.concatenate(
        [jnp.concatenate([w_gate, w_up], axis=2), w_down], axis=1
    )
    expert_weights = lax.all_gather(after(expert_pack, tokens), "seq", axis=1)
    gain_rows = columns[:, N_SEQ, :8, :16].transpose(1, 0, 2)
    gain_attn = gain_rows[:, :, :8].reshape(WIDTH).astype(f32)
    gain_moe = gain_rows[:, :, 8:].reshape(WIDTH).astype(f32)
    columns = columns[:, :N_SEQ].reshape(N_SHARD, N_SEQ, 2, 8, 128)
    columns = columns.transpose(1, 0, 3, 2, 4).reshape(WIDTH, COLS)

    wide = tokens.reshape(HEAD_ROWS, WIDTH).astype(f32)
    inverse = lax.rsqrt(jnp.mean(wide * wide, axis=1, keepdims=True) + epsilon)
    normed = (wide * inverse * gain_attn).astype(bf16)
    cosine, sine = rope_pair(shard)
    turn = turn_matrix()
    turned = dot(columns[:, : 3 * HEAD], turn, NN).astype(bf16)
    projected = dot(normed, jnp.concatenate([columns, turned], axis=1), NN)
    rotated = projected[:, : 3 * HEAD] * cosine + projected[:, COLS:] * sine
    queries = rotated[:, : 2 * HEAD].astype(bf16) * jnp.bfloat16(1.0 / math.sqrt(HEAD))
    queries = queries.reshape(N_SEQ, TOK_DEV, 2 * HEAD)
    memory = jnp.concatenate(
        [rotated[:, 2 * HEAD :], projected[:, 3 * HEAD : COLS]], axis=1
    ).astype(bf16)
    memory = memory.reshape(N_SEQ, TOK_DEV, 2 * HEAD)

    pick, scale_high, scale_low, slot_scale = routing(routes, route_weights)
    out_grad = cotangent.astype(f32)
    slots = (LOCAL_EXPERTS, N_SHARD, CAP, WIDTH)
    grad_send = (slot_scale[:, None] * dot(pick, cotangent, TN)).astype(bf16).reshape(slots)
    qkv_rows = jnp.broadcast_to(grouped.reshape(1, 16, WIDTH), (N_SHARD, 16, WIDTH))
    grad_send = jnp.concatenate([grad_send[0], grad_send[1], qkv_rows], axis=1)
    attended_wide, lse, attended_full, memory, grad_rows, out_slabs = attention(
        queries, memory, grad_send, out_slabs, 2
    )
    qkv_rows = grad_rows[:, 2 * CAP :].reshape(N_SHARD * 8, 2 * WIDTH)
    grad_rows = jnp.stack([grad_rows[:, :CAP], grad_rows[:, CAP : 2 * CAP]])
    grad_rows = grad_rows.reshape(LOCAL_EXPERTS, EXPERT_ROWS, WIDTH)

    order = jnp.stack(
        [(seq // 2 + 4 - k) % 4 * 2 + half for k in range(4) for half in range(2)]
    )
    attended_full = attended_full[order].transpose(1, 0, 2).reshape(TOK_DEV, WIDTH)
    x_wide = layer_input.astype(f32)
    out_weight = out_slabs.reshape(WIDTH, WIDTH)
    residual = x_wide + dot(attended_full, out_weight, NN)
    inverse_two = lax.rsqrt(jnp.mean(residual * residual, axis=1, keepdims=True) + epsilon)
    normed_moe = (residual * inverse_two * gain_moe).astype(bf16)

    send_rows = dot(pick, normed_moe, TN).astype(bf16).reshape(slots)
    expert_rows = exchange(send_rows, "shard", N_SHARD, 4, dim=1)
    expert_rows = expert_rows.reshape(LOCAL_EXPERTS, EXPERT_ROWS, WIDTH)
    expert_out, rows_grad, *expert_grads = experts(
        seq_array, expert_rows, grad_rows, expert_weights
    )
    returned = exchange(rows_grad.reshape(slots), "shard", N_SHARD, 5, dim=1)
    qkv_all = lax.all_gather(qkv_rows, "seq", axis=0, tiled=True)

    moe_in_grad = dot(pick, returned.reshape(EXPERTS * CAP, WIDTH), NN)
    scaled = moe_in_grad * gain_moe
    moe_part = inverse_two * scaled - residual * inverse_two**3 * jnp.mean(
        residual * scaled, axis=1, keepdims=True
    )
    residual_grad = out_grad + moe_part
    branch_grad = residual_grad.astype(bf16)
    attended_grad = dot(branch_grad, out_weight, NT).astype(bf16)
    attended_grad = attended_grad.reshape(TOK_DEV, N_SEQ, 2 * HEAD).transpose(1, 0, 2)
    back_order = jnp.stack(
        [(seq // 2 + 4 - z) % 4 * 2 + half for z in range(4) for half in range(2)]
    )
    attended_grad = attended_grad[back_order]

    out_parts = []
    for k in range(4):
        back = (4 - k) % 4 * COLS
        block = dot(attended_full[:, back : back + COLS], branch_grad, TN)
        out_parts.append(block.astype(bf16))
    tables = [
        (cosine[:, : 2 * HEAD], sine[:, : 2 * HEAD]),
        (
            jnp.concatenate([cosine[:, :HEAD], jnp.ones((HEAD_ROWS, HEAD), f32)], axis=1),
            jnp.concatenate([sine[:, :HEAD], jnp.zeros((HEAD_ROWS, HEAD), f32)], axis=1),
        ),
    ]
    tables = [
        jnp.stack(table).reshape(2, N_SEQ, TOK_DEV, 2 * HEAD) for table in zip(*tables)
    ]
    left = jnp.arange(2 * HEAD, dtype=jnp.int32) < HEAD
    turns = turn[: 2 * HEAD, : 2 * HEAD]
    turns = jnp.stack([turns, jnp.where(left[:, None] & left[None, :], turns, 0)])
    query_grad, memory_grad, token_query, token_memory, came_back, *sent = attention_back(
        queries,
        attended_grad,
        attended_wide,
        lse,
        memory,
        *tables,
        turns,
        expert_out.reshape(slots),
        expert_grads[1:] + out_parts[1:],
        6,
    )
    came_back = came_back.reshape(EXPERTS * CAP, WIDTH)
    expert_sums = sum(grad.astype(f32) for grad in [expert_grads[0]] + sent[:3])
    out_sums = sum(grad.astype(f32) for grad in [out_parts[0]] + sent[3:])
    out_sums = out_sums.reshape(2, 2 * HEAD, WIDTH)
    far = seq % 2
    out_mine = lax.dynamic_index_in_dim(out_sums, far, 0, keepdims=False)
    out_other = lax.dynamic_index_in_dim(out_sums, 1 - far, 0, keepdims=False)
    other = jnp.concatenate(
        [expert_sums[1].reshape(LOCAL_EXPERTS * 192, WIDTH), out_other], axis=0
    ).astype(bf16)
    other = lax.ppermute(other, "seq", along_x).astype(f32)
    expert_sums = expert_sums[0] + other[: LOCAL_EXPERTS * 192].reshape(
        LOCAL_EXPERTS, 192, WIDTH
    )
    out_part = out_mine + other[LOCAL_EXPERTS * 192 :]
    moe_sum = dot(scale_high, came_back, NN) + dot(scale_low, came_back, NN)
    block_out = (residual + moe_sum).astype(bf16)

    projected_grad = jnp.concatenate(
        [query_grad.reshape(HEAD_ROWS, 2 * HEAD), memory_grad.reshape(HEAD_ROWS, 2 * HEAD)], axis=1
    )

    qkv_part = dot(normed, projected_grad, TN)
    qkv_part = qkv_part.reshape(N_SEQ, N_SHARD, 8, COLS).transpose(1, 0, 2, 3)
    out_part = out_part.reshape(N_SHARD, 8, WIDTH)
    pack = expert_pack.astype(f32)
    moe_gain_part = jnp.sum(
        pack[:, :128] * expert_sums[:, :128], axis=(0, 2)
    ) / lax.dynamic_slice_in_dim(gain_moe, seq * 128, 128)
    moe_gain_part = moe_gain_part.reshape(N_SHARD, 1, 8)
    moe_gain_high = moe_gain_part.astype(bf16)
    moe_gain_low = (moe_gain_part - moe_gain_high.astype(f32)).astype(bf16)
    gain_part = jnp.concatenate([moe_gain_high, moe_gain_low], axis=1)
    gain_part = jnp.pad(gain_part, ((0, 0), (0, 14), (0, COLS - 8)))
    sums = jnp.concatenate(
        [
            qkv_part.reshape(N_SHARD, 64, COLS).astype(bf16),
            out_part.reshape(N_SHARD, 32, COLS).astype(bf16),
            gain_part,
        ],
        axis=1,
    )
    sums = jnp.sum(exchange(sums, "shard", N_SHARD, 7).astype(f32), axis=0)
    out_weight_grad = sums[64:96].reshape(8, WIDTH)
    moe_gain_grad = sums[96, :8] + sums[97, :8]
    qkv_groups = lax.all_to_all(sums[:64].reshape(N_SEQ, 8, COLS), "seq", 0, 0)
    qkv_groups = qkv_groups.transpose(1, 0, 2)
    attn_gain_grad = jnp.sum(grouped.astype(f32) * qkv_groups, axis=(1, 2)) / attn_gain.astype(f32)
    qkv_weight_grad = ungroup_columns(qkv_groups)

    token_grad = jnp.concatenate([token_query, token_memory], axis=2)
    token_grad = token_grad.transpose(1, 0, 2).reshape(TOK_DEV, N_SEQ * COLS)
    normed_grad = dot(token_grad, qkv_all, NT)
    inverse_one = lax.rsqrt(jnp.mean(x_wide * x_wide, axis=1, keepdims=True) + epsilon)
    scaled = normed_grad * gain_attn
    attn_part = inverse_one * scaled - x_wide * inverse_one**3 * jnp.mean(
        x_wide * scaled, axis=1, keepdims=True
    )
    input_grad = (residual_grad + attn_part).astype(bf16)
    return (
        block_out,
        input_grad,
        attn_gain_grad,
        moe_gain_grad,
        qkv_weight_grad,
        out_weight_grad,
        expert_sums[:, :128, :FF],
        expert_sums[:, :128, FF:],
        expert_sums[:, 128:],
    )


def solution(mesh):
    token = P(("seq", "shard"), None)
    vector = P(("seq", "shard"))
    expert = P("shard", "seq", None)
    return jax.shard_map(
        on_device,
        mesh=mesh,
        in_specs=(
            token,
            vector,
            vector,
            token,
            token,
            expert,
            expert,
            expert,
            token,
            token,
            token,
        ),
        out_specs=(token, token, vector, vector, token, token, expert, expert, expert),
        check_vma=False,
    )
```

time: 760 us -> 532 us (0.70)
  Pallas kernels: 522 us -> 389 us
  blocking collectives: 68.3 us -> 0 us
  starting transfers between devices: 31.6 us -> 9.73 us
  other arithmetic: 39.7 us -> 31.7 us
    pallas_call x8 -> x3, Pallas kernels: 271 us -> 93.6 us  [exchange(): pl.pallas_call(functools.partial(exchange_kernel, axis, count, dim), out_...]
    pallas_call x4 -> x3, Pallas kernels: 174 us -> 251 us  [the longest x1 117 us: attention_back(): pl.pallas_call(attention_back_kernel, in_specs=[vmem, ANY, vmem, vmem, vm...]
    all_to_all x1 -> x0, blocking collectives: 34.3 us -> none  [on_device(): lax.all_to_all(jnp.broadcast_to(branch_grad[None], (N_SEQ, TOK_DEV, WIDTH...]
    all_gather x1 -> x0, blocking collectives: 34 us -> none  [on_device(): projections = lax.all_gather(projections, 'shard', axis=0, tiled=True)]
    pallas_call x1, Pallas kernels: 77.6 us -> 44 us  [first_gather(): pl.pallas_call(first_kernel, out_shape=[jax.ShapeDtypeStruct((N_SEQ, 8, T...]
    all_to_all x6 -> x1, starting transfers between devices: 31.5 us -> 5.87 us  [on_device(): qkv_groups = lax.all_to_all(sums[:64].reshape(N_SEQ, 8, COLS), 'seq', 0, 0)]
    ppermute x0 -> x1, waiting for transfers between devices: none -> 14.1 us  [on_device(): other = lax.ppermute(other, 'seq', along_x).astype(f32)]
    reduce_sum x5 -> x2, other arithmetic: 13 us -> 1.34 us  [the longest x1 1.31 us: on_device(): sums = jnp.sum(exchange(sums, 'shard', N_SHARD, 7).astype(f32), axis=0)]
  transfers between devices with their start and end apart: 8 -> 4, of which waited for: 1 -> 2; matrix products, arithmetic and copies ran while one was open for 10% -> 14% of each run, Pallas kernels for 62% -> 62%
where the time goes in v2:
time: 532 us; the launch traced here: 531 us
  Pallas kernels  389 us (73%)
  local copies, waits for them, and re-layouts  40.2 us (8%)
  other arithmetic  31.7 us (6%)
  matrix products  26.1 us (5%)
  waiting for transfers between devices  18.8 us (4%)
  between operations  15.2 us (3%)
  starting transfers between devices  9.73 us (2%)
    pallas_call x1, Pallas kernels, attention_back(): pl.pallas_call(attention_back_kernel, in_specs=[vmem, ANY, vmem, vmem, vm...  117 us
    pallas_call x1, Pallas kernels, attention(): pl.pallas_call(attention_kernel, in_specs=[vmem, vmem, ANY, ANY], out_spe...  102 us
    pallas_call x3, Pallas kernels, exchange(): pl.pallas_call(functools.partial(exchange_kernel, axis, count, dim), out_...  93.6 us
    pallas_call x1, Pallas kernels, first_gather(): pl.pallas_call(first_kernel, out_shape=[jax.ShapeDtypeStruct((N_SEQ, 8, T...  44 us
    pallas_call x1, Pallas kernels, experts(): pl.pallas_call(expert_kernel, grid_spec=pltpu.PrefetchScalarGridSpec(num_...  32.6 us
    dot_general x18, matrix products, dot(): return lax.dot_general(left, right, dims, preferred_element_type=f32)  26.1 us
    ppermute x1, waiting for transfers between devices, on_device(): other = lax.ppermute(other, 'seq', along_x).astype(f32)  14.1 us
  transfers between devices with their start and end apart: 4, of which 2 were waited for; matrix products, arithmetic and copies ran while one was open for 14% of the time, Pallas kernels for 62%

profile of v2, /device:TPU:1, one launch (start us, length us, event | category | flops | bytes accessed | tf_op | source)
XLA Modules:
  0.0 530.6 jit_solution(5767804956960837327)
XLA Ops:
  12.3 2.1 pad_maximum_fusion.6
  14.4 44.0 %gather_tokens.1 = (bf16[8,8,16,1024]{3,2,1,0:T(8,128)(2,1)}, bf16[16,9,16,128]{3,2,1,0:T(8,128)(2,1)}, bf16[2,16,2,32,128]{4,3,2,1,0:T(8,128)(2,1)}) custom-call(bf16[8,16,1024]{2,1,0:T(8,128)(2,1)} %bitcast.168, bf16[8,32,128]{2,1,0:T(8,128)(2,1)} %pad_maximum_fusion.8.w_ref, bf16[2,32,128]{2,1,0:T(8,128)(2,1)} %bitcast.202), custom_call_target="tpu_custom_call" | custom-call | tf_op jit(solution)/shard_map/gather_tokens/pallas_call | solution.py:219
  60.1 2.1 multiply_reduce_fusion
  62.5 1.1 convolution_convert_fusion.6
  63.6 1.2 copy.122
  65.4 1.2 fusion.13
  69.4 1.0 add_reduce_fusion
  71.7 2.1 pad_maximum_fusion.cot_ref
  73.7 102.0 %attention_forward.1 = (f32[8,128,128]{2,1,0:T(8,128)S(1)}, f32[8,1,256]{2,1,0:T(1,128)S(1)}, bf16[8,128,128]{2,1,0:T(8,128)(2,1)S(1)}, bf16[8,16,128,128]{3,2,1...) custom-call(bf16[8,128,128]{2,1,0:T(8,128)(2,1)S(1)} %bitcast.153, ...), custom_call_target="tpu_custom_call" | custom-call | tf_op jit(solution)/shard_map/attention_forward/pallas_call | solution.py:468
  177.1 1.9 slice.159
  179.1 2.0 reshape.774
  185.0 1.5 multiply_reduce_fusion.2
  187.1 3.4 convolution_convert_fusion
  190.4 41.8 %exchange_shard.3 = bf16[2,16,40,1024]{3,2,1,0:T(8,128)(2,1)} custom-call(bf16[2,16,40,1024]{3,2,1,0:T(8,128)(2,1)} %bitcast.159), custom_call_target="tpu_custom_call" | custom-call | tf_op jit(solution)/shard_map/exchange_shard/pallas_call | solution.py:86
  232.5 2.1 fusion.83
  234.5 2.0 copy.129
  236.6 2.0 copy.130
  238.6 2.0 copy.131
  240.6 2.0 copy.132
  242.7 3.9 copy.134
  247.5 2.4 pad_maximum_fusion.2.refs_5_
  249.9 1.1 pad_maximum_fusion.3.refs_6_
  251.3 1.7 pad_maximum_fusion.1.g_ref
  253.1 32.6 %experts.1 = (bf16[2,640,1024]{2,1,0:T(8,128)(2,1)}, bf16[2,640,1024]{2,1,0:T(8,128)(2,1)}, bf16[2,2,192,1024]{3,2,1,0:T(8,128)(2,1)}, bf16[2,2,192,1024]{3,2,1,...) custom-call(s32[1]{0:T(128)} %bitcast.37.s_ref, bf16[2,640,1024]{2,1,0:T(8,128)(2,1)} %bitcast.160, ...), custom_call_target="tpu_custom_call" | custom-call | flops 100000000 | bytes 1048576 | tf_op jit(solution)/shard_map/experts/pallas_call | solution.py:751
  285.6 34.5 %exchange_shard.4 = bf16[2,16,40,1024]{3,2,1,0:T(8,128)(2,1)} custom-call(bf16[2,16,40,1024]{3,2,1,0:T(8,128)(2,1)} %bitcast.173), custom_call_target="tpu_custom_call" | custom-call | tf_op jit(solution)/shard_map/exchange_shard/pallas_call | solution.py:86
  320.2 2.4 multiply_reduce_fusion.1
  322.7 1.0 fusion.79
  324.6 1.5 gather_fusion.1
  326.1 1.9 convolution_convert_fusion.3.refs_14_
  328.1 1.9 convolution_convert_fusion.4.refs_13_
  330.0 1.1 convolution_convert_fusion.5.refs_12_
  331.1 116.7 %attention_backward.1 = (bf16[8,128,128]{2,1,0:T(8,128)(2,1)}, bf16[8,128,128]{2,1,0:T(8,128)(2,1)}, bf16[8,128,128]{2,1,0:T(8,128)(2,1)}, bf16[8,128,128]{2,1,0...) custom-call(bf16[8,128,128]{2,1,0:T(8,128)(2,1)} %bitcast.154, ...), custom_call_target="tpu_custom_call" | custom-call | tf_op jit(solution)/shard_map/attention_backward/pallas_call | solution.py:672
  447.8 1.9 fusion.7
  450.6 3.4 convert_add_fusion
  454.5 1.0 copy-done.5
  456.5 1.1 pad_maximum_fusion.4
  457.7 3.8 collective-permute-start
  461.5 1.0 copy.133
  462.5 4.1 fusion.19
  468.1 1.3 fusion.9
  469.4 14.1 %collective-permute-done = bf16[512,1024]{1,0:T(8,128)(2,1)S(1)} collective-permute-done((bf16[512,1024]{1,0:T(8,128)(2,1)}, bf16[512,1024]{1,0:T(8,128)(2,1)S(1)}, u32[]{:S(2)}, u32[]{:S(2)}) %collective-permute-start) | collective-permute-done | bytes 1048608 | tf_op jit(solution)/shard_map/ppermute | solution.py:986
  485.7 1.1 fusion.82
  487.0 1.0 copy-done.18
  489.3 1.0 pad_maximum_fusion.5.x_ref
  490.4 17.2 %exchange_shard.5 = bf16[16,112,256]{2,1,0:T(8,128)(2,1)} custom-call(bf16[16,112,256]{2,1,0:T(8,128)(2,1)} %pad_maximum_fusion.5.x_ref), custom_call_target="tpu_custom_call" | custom-call | tf_op jit(solution)/shard_map/exchange_shard/pallas_call | solution.py:86
  507.5 1.3 convert_reduce_fusion
  509.5 5.9 %all-to-all-start = ((f32[8,8,256]{2,1,0:T(8,128)}), f32[8,8,256]{2,1,0:T(8,128)S(1)}, u32[]{:S(2)}, u32[]{:S(2)}) async-start(f32[8,8,256]{2,1,0:T(8,128)} %slice_bitcast_fusion.2), calls=%async_computation | async-start | bytes 131072 | tf_op jit(solution)/shard_map/all_to_all | solution.py:1021
  517.3 4.7 all-to-all-done
  (228 shorter events, 31.2 us)
Async XLA Ops:
  7.2 245.9 %all-gather.6.cloned.1.call-start = ((), (), s32[]{:S(2)}) async-start(), calls=%async_computation.2 | async-start | bytes 7077888 | tf_op jit(solution)/shard_map/all_gather | solution.py:878
  8.8 59.2 %copy-start.39 = (bf16[8,8,64]{2,1,0:T(8,128)(2,1)}, bf16[8,8,64]{2,1,0:T(8,128)(2,1)S(1)}, u32[]{:S(2)}) copy-start(bf16[8,8,64]{2,1,0:T(8,128)(2,1)S(1)} %reshape.753) | copy-start | bytes 24580
  8.9 59.2 %copy-start.41 = (bf16[1,8,8,128]{3,2,1,0:T(8,128)(2,1)}, bf16[1,8,8,128]{3,2,1,0:T(8,128)(2,1)S(1)}, u32[]{:S(2)}) copy-start(bf16[1,8,8,128]{3,2,1,0:T(8,128)(2,1)S(1)} %copy.158) | copy-start | bytes 49156
  12.3 49.9 %copy-start.15 = (bf16[2,128,1024]{2,1,0:T(8,128)(2,1)}, bf16[2,128,1024]{2,1,0:T(8,128)(2,1)S(1)}, u32[]{:S(2)}) copy-start(bf16[2,128,1024]{2,1,0:T(8,128)(2,1)S(1)} %constant_dynamic-update-slice_fusion) | copy-start | bytes 1572868
  58.4 3.9 copy-start.35
  58.4 404.1 %all-gather.4.cloned.1.call-start = ((), (), s32[]{:S(2)}) async-start(), calls=%async_computation.1 | async-start | bytes 4718592 | tf_op jit(solution)/shard_map/all_gather | solution.py:930
  60.1 4.7 copy-start.47
  62.2 2.6 copy-start.8
  62.4 2.9 copy-start.57
  62.4 2.9 copy-start.59
  62.5 2.9 copy-start.49
  62.5 2.9 copy-start.51
  68.4 5.3 %copy-start = (bf16[1024,128]{1,0:T(8,128)(2,1)}, bf16[1024,128]{1,0:T(8,128)(2,1)S(1)}, u32[]{:S(2)}) copy-start(bf16[1024,128]{1,0:T(8,128)(2,1)S(1)} %copy.123) | copy-start | bytes 786436
  177.1 7.9 %copy-start.11 = (bf16[128,1024]{1,0:T(8,128)(2,1)S(1)}, bf16[128,1024]{1,0:T(8,128)(2,1)}, u32[]{:S(2)}) copy-start(bf16[128,1024]{1,0:T(8,128)(2,1)} %param.11) | copy-start | bytes 786436
  187.1 3.4 copy-start.55
  190.4 41.9 %copy-start.32 = (f32[1024,32]{0,1:T(8,128)S(1)}, f32[1024,32]{0,1:T(8,128)}, u32[]{:S(2)}) copy-start(f32[1024,32]{0,1:T(8,128)} %copy-done.31) | copy-start | bytes 393220
  190.4 42.0 %copy-start.30 = (f32[1024,32]{0,1:T(8,128)S(1)}, f32[1024,32]{0,1:T(8,128)}, u32[]{:S(2)}) copy-start(f32[1024,32]{0,1:T(8,128)} %copy-done.29) | copy-start | bytes 393220
  242.7 4.0 copy-start.50
  242.7 4.0 copy-start.52
  242.7 4.0 copy-start.58
  242.7 4.0 copy-start.60
  246.6 3.3 copy-start.24
  246.6 3.3 copy-start.25
  247.5 3.5 copy-start.19
  285.6 34.6 %copy-start.14 = (pred[128,1280]{1,0:T(32,128)(4,1)S(1)}, pred[128,1280]{1,0:T(32,128)(4,1)}, u32[]{:S(2)}) copy-start(pred[128,1280]{1,0:T(32,128)(4,1)} %copy-done.13) | copy-start | bytes 491524
  285.6 34.6 %copy-start.46 = (f32[1024]{0:T(1024)S(1)}, f32[1024]{0:T(1024)}, u32[]{:S(2)}) copy-start(f32[1024]{0:T(1024)} %reshape.787) | copy-start | bytes 12292
  320.2 2.5 copy-start.34
  324.5 5.5 %copy-start.20 = (bf16[128,8,128]{0,2,1:T(8,128)(2,1)S(1)}, bf16[128,8,128]{0,2,1:T(8,128)(2,1)}, u32[]{:S(2)}) copy-start(bf16[128,8,128]{0,2,1:T(8,128)(2,1)} %copy.126) | copy-start | bytes 786436
  331.1 116.7 %copy-start.22 = (bf16[1024,1024]{1,0:T(8,128)(2,1)S(1)}, bf16[1024,1024]{1,0:T(8,128)(2,1)}, u32[]{:S(2)}) copy-start(bf16[1024,1024]{1,0:T(8,128)(2,1)} %copy.134) | copy-start | bytes 6291460
  447.8 2.8 copy-start.26
  447.8 2.7 copy-start.27
  450.6 3.5 copy-start.36
  450.6 3.5 copy-start.37
  450.6 3.5 copy-start.38
  454.1 7.3 %copy-start.43 = (bf16[8,128,128]{2,1,0:T(8,128)(2,1)S(1)}, bf16[8,128,128]{2,1,0:T(8,128)(2,1)}, u32[]{:S(2)}) copy-start(bf16[8,128,128]{2,1,0:T(8,128)(2,1)} %get-tuple-element.52) | copy-start | bytes 786436
  454.1 7.3 %copy-start.44 = (bf16[8,128,128]{2,1,0:T(8,128)(2,1)S(1)}, bf16[8,128,128]{2,1,0:T(8,128)(2,1)}, u32[]{:S(2)}) copy-start(bf16[8,128,128]{2,1,0:T(8,128)(2,1)} %get-tuple-element.53) | copy-start | bytes 786436
  456.5 6.0 %copy-start.12 = (bf16[128,1024]{1,0:T(8,128)(2,1)S(1)}, bf16[128,1024]{1,0:T(8,128)(2,1)}, u32[]{:S(2)}) copy-start(bf16[128,1024]{1,0:T(8,128)(2,1)} %param.11) | copy-start | bytes 786436
  456.5 6.0 %copy-start.48 = (f32[1024]{0:T(1024)S(1)}, f32[1024]{0:T(1024)}, u32[]{:S(2)}) copy-start(f32[1024]{0:T(1024)} %copy-done.47) | copy-start | bytes 12292
  457.7 25.8 %collective-permute-start = (bf16[512,1024]{1,0:T(8,128)(2,1)}, bf16[512,1024]{1,0:T(8,128)(2,1)S(1)}, u32[]{:S(2)}, u32[]{:S(2)}) collective-permute-start(bf16[512,1024]{1,0:T(8,128)(2,1)} %pad_maximum_fusion.4), channel_id=1, source_target_pairs={{0,16},{16,0},{32,48},{48,32},{64,80},{80,64},{96,112},{112,96},{1... | collective-permute-start | bytes 3145736 | tf_op jit(solution)/shard_map/ppermute | solution.py:986
  462.5 4.1 copy-start.23
  462.5 5.1 copy-start.4
  462.5 5.1 copy-start.28
  469.4 15.0 %copy-start.6 = (f32[2,2,192,1024]{3,2,1,0:T(8,128)S(1)}, f32[2,2,192,1024]{3,2,1,0:T(8,128)}, u32[]{:S(2)}) copy-start(f32[2,2,192,1024]{3,2,1,0:T(8,128)} %copy-done.5) | copy-start | bytes 9437188
  486.8 2.6 copy-start.21
  490.3 32.0 %copy-start.40 = (bf16[8,8,64]{2,1,0:T(8,128)(2,1)S(1)}, bf16[8,8,64]{2,1,0:T(8,128)(2,1)}, u32[]{:S(2)}) copy-start(bf16[8,8,64]{2,1,0:T(8,128)(2,1)} %copy-done.39) | copy-start | bytes 24580
  490.3 32.0 %copy-start.42 = (bf16[1,8,8,128]{3,2,1,0:T(8,128)(2,1)S(1)}, bf16[1,8,8,128]{3,2,1,0:T(8,128)(2,1)}, u32[]{:S(2)}) copy-start(bf16[1,8,8,128]{3,2,1,0:T(8,128)(2,1)} %copy-done.41) | copy-start | bytes 49156
  490.4 32.2 %copy-start.62 = (bf16[8]{0:T(256)(128)(2,1)S(1)}, bf16[8]{0:T(256)(128)(2,1)}, u32[]{:S(2)}) copy-start(bf16[8]{0:T(256)(128)(2,1)} %param.12) | copy-start | bytes 52
  509.5 12.6 %all-to-all-start = ((f32[8,8,256]{2,1,0:T(8,128)}), f32[8,8,256]{2,1,0:T(8,128)S(1)}, u32[]{:S(2)}, u32[]{:S(2)}) async-start(f32[8,8,256]{2,1,0:T(8,128)} %slice_bitcast_fusion.2), calls=%async_computation | async-start | bytes 131072 | tf_op jit(solution)/shard_map/all_to_all | solution.py:1021
  (19 other events, 27.1 us)
Sparse Core Ops, SparseCore 0:
  58.6 122.7 all-gather.5
  183.7 81.7 all-gather.3

commit v3 on v2

--- a/solution.py
+++ b/solution.py
@@ -278,12 +278,14 @@
     q_ref,
     kv_ref,
     cot_ref,
+    qkv_ref,
     slab_ref,
     wide_ref,
     lse_ref,
     att_ref,
     mem_ref,
     cot_out,
+    qkv_out,
     slab_out,
     land,
     vt,
@@ -297,6 +299,8 @@
     grecv,
     esend,
     erecv,
+    vsend,
+    vrecv,
     fsend,
     frecv,
     own,
@@ -355,6 +359,12 @@
             cot_ref.at[peer], cot_out.at[me], esend.at[k - 1], erecv.at[k - 1], "shard", peer
         )
 
+    def to_shard(k):
+        peer = lax.rem(me + k, N_SHARD)
+        return transfer(
+            qkv_ref, qkv_out.at[me], vsend.at[k - 1], vrecv.at[k - 1], "shard", peer
+        )
+
     def to_ring(k):
         peer = lax.rem(seq + 2 * k, N_SEQ)
         return transfer(slab_ref, slab_out.at[k], fsend.at[k - 1], frecv.at[k - 1], "seq", peer)
@@ -381,8 +391,11 @@
     fourth(0)
     for k in range(1, N_SHARD):
         to_expert(k).start()
+        to_shard(k).start()
     for k in (1, 2, 3):
         to_ring(k).start()
+    qkv_own = pltpu.make_async_copy(qkv_ref, qkv_out.at[me], own.at[3])
+    qkv_own.start()
     cot_own = pltpu.make_async_copy(cot_ref.at[me], cot_out.at[me], own.at[0])
     cot_own.start()
     slab_own = pltpu.make_async_copy(slab_ref, slab_out.at[0], own.at[1])
@@ -447,9 +460,11 @@
         to_token(source, source).wait_recv()
     mine.wait()
     cot_own.wait()
+    qkv_own.wait()
     slab_own.wait()
     for k in range(1, N_SHARD):
         to_expert(k).wait()
+        to_shard(k).wait()
     for k in (1, 2, 3):
         to_ring(k).wait()
 
@@ -462,19 +477,20 @@
     lax.fori_loop(0, N_SEQ, end, 0)
 
 
-def attention(queries, memory, cot_rows, slab, ident):
+def attention(queries, memory, cot_rows, qkv_rows, slab, ident):
     dma = pltpu.SemaphoreType.DMA
     vmem = pl.BlockSpec(memory_space=pltpu.VMEM)
     return pl.pallas_call(
         attention_kernel,
-        in_specs=[vmem, vmem, ANY, ANY],
-        out_specs=[vmem, vmem, ANY, ANY, ANY, ANY],
+        in_specs=[vmem, vmem, ANY, ANY, ANY],
+        out_specs=[vmem, vmem, ANY, ANY, ANY, ANY, ANY],
         out_shape=[
             jax.ShapeDtypeStruct((N_SEQ, 2 * HEAD, TOK_DEV), f32),
             jax.ShapeDtypeStruct((N_SEQ, 1, 2 * TOK_DEV), f32),
             jax.ShapeDtypeStruct((N_SEQ, TOK_DEV, 2 * HEAD), bf16),
             jax.ShapeDtypeStruct((N_SEQ, N_SHARD, TOK_DEV, 2 * HEAD), bf16),
             jax.ShapeDtypeStruct(cot_rows.shape, bf16),
+            jax.ShapeDtypeStruct((N_SHARD,) + qkv_rows.shape, bf16),
             jax.ShapeDtypeStruct((4,) + slab.shape, bf16),
         ],
         scratch_shapes=[
@@ -490,46 +506,107 @@
             dma((N_SEQ,)),
             dma((N_SHARD - 1,)),
             dma((N_SHARD - 1,)),
+            dma((N_SHARD - 1,)),
+            dma((N_SHARD - 1,)),
             dma((3,)),
             dma((3,)),
-            dma((3,)),
+            dma((4,)),
             dma((N_SEQ,)),
         ],
         compiler_params=pltpu.CompilerParams(
             collective_id=ident, has_side_effects=True, vmem_limit_bytes=48 << 20
         ),
         name="attention_forward",
-    )(queries, memory, cot_rows, slab)
-
-
-def attention_back_kernel(*refs):
-    (q_ref, g_ref, wide_ref, lse_ref, mem_ref, cos_ref, sin_ref, turn_ref, eo_ref) = refs[:9]
-    parts = refs[9:15]
-    pgq_ref, pgm_ref, tokq_ref, tokm_ref, came_ref = refs[15:20]
-    parts_out = refs[20:26]
-    gl, qs, gs, delta_ref, kt, acc, dq, stage, dl = refs[26:35]
-    dsend, drecv, osend, orecv, jsend, jrecv, psend, precv, nsend, nrecv, own = refs[35:]
+    )(queries, memory, cot_rows, qkv_rows, slab)
+
+
+def late_kernel(*refs):
+    (att_ref, ow_ref, x_ref, cot_ref, gain_ref, pick_ref, pickt_ref, gr_ref, w_ref) = refs[:9]
+    (q_ref, wide_ref, lse_ref, mem_ref, cos_ref, sin_ref, turn_ref) = refs[9:16]
+    (res_ref, resg_ref, pgq_ref, pgm_ref, tokq_ref, tokm_ref, came_ref) = refs[16:23]
+    (dw_ref, kz_ref, po_ref, oz_ref) = refs[23:27]
+    (gu, dn, land, rows, returned, xt, ht, hg, gm, mixed, dw, attp, ags, po) = refs[27:41]
+    (gl, qs, gs, delta_ref, kt, acc, dq, stage, dl) = refs[41:50]
+    (wsem, hsend, hrecv, isend, irecv, ksend, krecv, psend, precv) = refs[50:59]
+    (dsend, drecv, osend, orecv, jsend, jrecv, nsend, nrecv, own) = refs[59:]
     seq = lax.axis_index("seq")
     me = lax.axis_index("shard")
-
-    def to_head(k, source, peer):
+    ring = seq // 2
+    far = lax.rem(seq, 2)
+
+    def weights(e, s):
+        return (
+            pltpu.make_async_copy(
+                w_ref.at[e, s, :128], gu.at[e, 128 * s : 128 * s + 128], wsem.at[e, s, 0]
+            ),
+            pltpu.make_async_copy(
+                w_ref.at[e, s, 128:], dn.at[e, 64 * s : 64 * s + 64], wsem.at[e, s, 1]
+            ),
+        )
+
+    pieces = ((0, 48), (48, 80))
+
+    def to_expert(part, k, block, source, peer):
+        low, high = pieces[part]
         return transfer(
-            g_ref.at[peer], gl.at[source], osend.at[k - 1], orecv.at[k - 1], "seq", peer
+            rows.at[block, low:high],
+            land.at[source, low:high],
+            hsend.at[part, k - 1],
+            hrecv.at[part, k - 1],
+            "shard",
+            peer,
+        )
+
+    back_pieces = ((0, 32), (32, 80))
+
+    def to_source(part, k, block, source, peer):
+        low, high = back_pieces[part]
+        return transfer(
+            rows.at[block, low:high],
+            returned.at[source, low:high],
+            isend.at[part, k - 1],
+            irecv.at[part, k - 1],
+            "shard",
+            peer,
         )
 
     def to_token_expert(k):
         peer = lax.rem(me + k, N_SHARD)
         return transfer(
-            eo_ref.at[:, peer], came_ref.at[:, me], jsend.at[k - 1], jrecv.at[k - 1], "shard", peer
-        )
-
-    def to_ring(n):
-        peer = lax.rem(seq + 2 * (n % 3 + 1), N_SEQ)
-        return transfer(parts[n], parts_out[n], psend.at[n], precv.at[n], "seq", peer)
+            land.at[peer], came_ref.at[me], jsend.at[k - 1], jrecv.at[k - 1], "shard", peer
+        )
+
+    def to_ring(e, k):
+        peer = lax.rem(seq + 2 * k, N_SEQ)
+        return transfer(
+            dw.at[e, k], kz_ref.at[k - 1, e], ksend.at[e, k - 1], krecv.at[e, k - 1], "seq", peer
+        )
+
+    def out_to_ring(k):
+        peer = lax.rem(seq + 2 * k, N_SEQ)
+        return transfer(
+            po.at[k], oz_ref.at[k - 1], psend.at[k - 1], precv.at[k - 1], "seq", peer
+        )
+
+    def head_of(p):
+        return lax.rem(ring + 4 - p // 2, 4) * 2 + p % 2
+
+    def to_head(p):
+        return transfer(
+            ags.at[p], gl.at[seq], osend.at[p], orecv.at[seq], "seq", head_of(p)
+        )
+
+    def from_head(source):
+        return transfer(gl.at[source], gl.at[source], osend.at[0], orecv.at[source], "seq", source)
 
     def to_owner(t, k, block, source, peer):
         return transfer(
-            stage.at[t, block], dl.at[t, source], dsend.at[t, k - 1], drecv.at[t, k - 1], "shard", peer
+            stage.at[t, block],
+            dl.at[t, source],
+            dsend.at[t, k - 1],
+            drecv.at[t, k - 1],
+            "shard",
+            peer,
         )
 
     def to_token(n, t, source):
@@ -539,20 +616,171 @@
         )
 
     greet(everyone(seq, me))
+    for e in range(LOCAL_EXPERTS):
+        for s in range(N_SEQ):
+            for copy in weights(e, s):
+                copy.start()
+
+    for p in range(N_SEQ):
+        attp[:, 128 * p : 128 * p + 128] = att_ref[head_of(p)]
+    residual = x_ref[...].astype(f32) + dot(attp[...], ow_ref[...], NN)
+    res_ref[...] = residual
+    inverse = lax.rsqrt(jnp.mean(residual * residual, axis=1, keepdims=True) + epsilon)
+    normed = (residual * inverse * gain_ref[...]).astype(bf16)
+
+    for k in range(N_SHARD):
+        peer = lax.rem(me + k, N_SHARD)
+        here = pl.ds(pl.multiple_of(peer * 80, 16), 80)
+        block = dot(pickt_ref[here, :], normed, NN).astype(bf16)
+        rows[peer] = block
+        if k:
+            to_expert(0, k, peer, me, peer).start()
+        else:
+            land[me] = block
+    for k in range(1, N_SHARD):
+        peer = lax.rem(me + k, N_SHARD)
+        to_expert(1, k, peer, me, peer).start()
+
+    def split(block, e):
+        return (
+            block.astype(f32)
+            .reshape(N_SHARD, LOCAL_EXPERTS, 8, WIDTH)[:, e]
+            .reshape(128, WIDTH)
+            .astype(bf16)
+        )
+
+    def join(first, second):
+        halves = [half.astype(f32).reshape(N_SHARD, 1, 8, WIDTH) for half in (first, second)]
+        return jnp.concatenate(halves, axis=1).reshape(N_SHARD, 16, WIDTH).astype(bf16)
+
+    def expert(e, x, g, here):
+        pre = dot(x, gu[e], NN)
+        gate, up = pre[:, :FF], pre[:, FF:]
+        sigmoid = jax.nn.sigmoid(gate)
+        act = gate * sigmoid
+        hidden = (act * up).astype(bf16)
+        units = dot(g, dn[e], NT)
+        gate_grad = (units * up * sigmoid * (1.0 + gate * (1.0 - sigmoid))).astype(bf16)
+        up_grad = (units * act).astype(bf16)
+        both = jnp.concatenate([gate_grad, up_grad], axis=1)
+        hg[e, here, :] = both
+        xt[e, :, here] = x.T
+        ht[e, :, here] = hidden.T
+        return dot(hidden, dn[e], NN).astype(bf16), dot(both, gu[e], NT).astype(bf16)
+
+    def run_expert(e, low):
+        def aligned(n, carry):
+            group = pl.ds(n * 8, 8)
+            here = pl.ds(pl.multiple_of(n * 256, 256), 256)
+            x = land[group, low : low + 32].reshape(256, WIDTH)
+            g = gr_ref[group, low : low + 32].reshape(256, WIDTH)
+            out, back = expert(e, x, g, here)
+            land[group, low : low + 32] = out.reshape(8, 32, WIDTH)
+            rows[group, low : low + 32] = back.reshape(8, 32, WIDTH)
+            return carry
+
+        lax.fori_loop(0, 2, aligned, 0)
+        g = split(gr_ref[:, 32:48], e)
+        gm[e] = g
+        out, back = expert(e, split(land[:, 32:48], e), g, slice(512, 640))
+        mixed[0, e] = out
+        mixed[1, e] = back
+
+    def expert_grads(e):
+        for k in (1, 3, 2, 0):
+
+            def block(n, carry, k=k):
+                s = lax.rem(ring + k, 4) * 2 + lax.rem(far + n, 2)
+                features = pl.ds(pl.multiple_of(s * 128, 128), 128)
+                units = pl.ds(pl.multiple_of(s * 64, 64), 64)
+                dw[e, k, n, :128, :] = dot(xt[e, features, :], hg[e], NN).astype(bf16)
+                low = 48 * e
+                part = dot(
+                    ht[e, units, :512], gr_ref[:, low : low + 32].reshape(512, WIDTH), NN
+                )
+                part += dot(ht[e, units, 512:], gm[e], NN)
+                dw[e, k, n, 128:, :] = part.astype(bf16)
+                return carry
+
+            lax.fori_loop(0, 2, block, 0)
+
+    def arrived(part):
+        for k in range(1, N_SHARD):
+            source = lax.rem(me + N_SHARD - k, N_SHARD)
+            to_expert(part, k, source, source, source).wait_recv()
+
+    for e in range(LOCAL_EXPERTS):
+        for s in range(N_SEQ):
+            for copy in weights(e, s):
+                copy.wait()
+    arrived(0)
+    for part in range(2):
+        for k in range(1, N_SHARD):
+            peer = lax.rem(me + k, N_SHARD)
+            to_expert(part, k, peer, me, peer).wait_send()
+    run_expert(0, 0)
+    for k in range(1, N_SHARD):
+        peer = lax.rem(me + k, N_SHARD)
+        to_source(0, k, peer, me, peer).start()
+    arrived(1)
+    run_expert(1, 48)
+    land[:, 32:48] = join(mixed[0, 0], mixed[0, 1])
+    rows[:, 32:48] = join(mixed[1, 0], mixed[1, 1])
+    for k in range(1, N_SHARD):
+        peer = lax.rem(me + k, N_SHARD)
+        to_source(1, k, peer, me, peer).start()
+    returned[me] = rows[me]
+    expert_grads(0)
+    for k in (1, 3):
+        to_ring(0, k).start()
+    expert_grads(1)
+
+    for part in range(2):
+        for k in range(1, N_SHARD):
+            source = lax.rem(me + N_SHARD - k, N_SHARD)
+            to_source(part, k, source, source, source).wait_recv()
+    moe_in_grad = dot(pick_ref[...], returned[...].reshape(N_SHARD * 80, WIDTH), NN)
+    residual = res_ref[...]
+    inverse = lax.rsqrt(jnp.mean(residual * residual, axis=1, keepdims=True) + epsilon)
+    scaled = moe_in_grad * gain_ref[...]
+    moe_part = inverse * scaled - residual * (inverse * inverse * inverse) * jnp.mean(
+        residual * scaled, axis=1, keepdims=True
+    )
+    residual_grad = cot_ref[...].astype(f32) + moe_part
+    resg_ref[...] = residual_grad
+    branch = residual_grad.astype(bf16)
+    attended_grad = dot(branch, ow_ref[...], NT).astype(bf16)
+    for p in range(N_SEQ):
+        ags[p] = attended_grad[:, 128 * p : 128 * p + 128]
+        if p > 1:
+            to_head(p).start()
+        else:
+
+            @pl.when(far != p)
+            def _(p=p):
+                to_head(p).start()
+
+    gl[seq] = ags[far]
+    for p in range(N_SEQ):
+        po[(4 - p // 2) % 4, p % 2] = dot(attp[:, 128 * p : 128 * p + 128].T, branch, NN).astype(
+            bf16
+        )
     for k in range(1, N_SEQ):
-        to_head(k, seq, lax.rem(seq + k, N_SEQ)).start()
-    mine = pltpu.make_async_copy(g_ref.at[seq], gl.at[seq], own.at[0])
-    mine.start()
-    came_own = pltpu.make_async_copy(eo_ref.at[:, me], came_ref.at[:, me], own.at[1])
-    came_own.start()
-    mine.wait()
-    for k in range(1, N_SEQ):
-        source = lax.rem(seq + N_SEQ - k, N_SEQ)
-        to_head(k, source, source).wait_recv()
-    for n in range(6):
-        to_ring(n).start()
+        from_head(lax.rem(seq + k, N_SEQ)).wait_recv()
+    for k in (1, 3, 2):
+        to_ring(1, k).start()
+    to_ring(0, 2).start()
+    for k in (1, 2, 3):
+        out_to_ring(k).start()
     for k in range(1, N_SHARD):
         to_token_expert(k).start()
+    came_own = pltpu.make_async_copy(land.at[me], came_ref.at[me], own.at[0])
+    came_own.start()
+    dw_own = [pltpu.make_async_copy(dw.at[e, 0], dw_ref.at[e], own.at[1 + e]) for e in range(2)]
+    for copy in dw_own:
+        copy.start()
+    po_own = pltpu.make_async_copy(po.at[0], po_ref, own.at[3])
+    po_own.start()
 
     def begin(i, carry):
         qs[i] = spread(q_ref[i], False)
@@ -574,29 +802,36 @@
         here = slice(n * BWD_TILE, (n + 1) * BWD_TILE)
         memory = mem_ref[t, 8 * n : 8 * n + 8].reshape(BWD_TILE, 2 * HEAD)
         scores = dot(memory, qs[i], NT)
-        weights = jnp.exp(scores - lse_ref[i])
+        weight = jnp.exp(scores - lse_ref[i])
         if masked:
-            weights = jnp.where(admitted(scores.shape, me, n * BWD_TILE), weights, 0.0)
+            weight = jnp.where(admitted(scores.shape, me, n * BWD_TILE), weight, 0.0)
         weight_grad = dot(memory, gs[i], NT)
-        score_grad = (weights * (weight_grad - delta_ref[i])).astype(bf16)
-        here_grad = dot(weights.astype(bf16), gs[i], NN) + dot(score_grad, qs[i], NN)
+        score_grad = (weight * (weight_grad - delta_ref[i])).astype(bf16)
+        here_grad = dot(weight.astype(bf16), gs[i], NN) + dot(score_grad, qs[i], NN)
         if masked:
             acc[here, :] = here_grad
         else:
             acc[here, :] += here_grad
         dq[i] += dot(kt[:, here], score_grad, NN)
 
+    def turned(grad, n, t):
+        cosine, sine = cos_ref[t], sin_ref[t]
+        if n:
+            key = lax.broadcasted_iota(jnp.int32, cosine.shape, 1) < HEAD
+            cosine = jnp.where(key, cosine, 1.0)
+            sine = jnp.where(key, sine, 0.0)
+        other = dot(grad, turn_ref[n], NT)
+        return (grad.astype(f32) * cosine + other * sine).astype(bf16)
+
     def step(t, carry):
         for n in range(4):
-            rows = mem_ref[t, 4 * n : 4 * n + 4].reshape(512, 2 * HEAD)
-            kt[:, 512 * n : 512 * n + 512] = rows.T[:HEAD]
+            block = mem_ref[t, 4 * n : 4 * n + 4].reshape(512, 2 * HEAD)
+            kt[:, 512 * n : 512 * n + 512] = block.T[:HEAD]
         tile(t, t, 0, True)
         tile(t, t, 1, True)
         grad = dq[t] * (1.0 / math.sqrt(HEAD))
         grad = jnp.concatenate([grad[:, :TOK_DEV], grad[:, TOK_DEV:]], axis=0).T.astype(bf16)
-        turned = dot(grad, turn_ref[0], NT)
-        grad = grad.astype(f32) * cos_ref[0, t] + turned * sin_ref[0, t]
-        pgq_ref[t] = grad.astype(bf16)
+        pgq_ref[t] = turned(grad, 0, t)
 
         @pl.when(t != seq)
         def _():
@@ -609,8 +844,8 @@
 
         lax.fori_loop(t + 1, N_SEQ, rest, 0)
         for n in range(4):
-            rows = acc[512 * n : 512 * n + 512, :].astype(bf16)
-            stage[t, 4 * n : 4 * n + 4] = rows.reshape(4, TOK_DEV, 2 * HEAD)
+            block = acc[512 * n : 512 * n + 512, :].astype(bf16)
+            stage[t, 4 * n : 4 * n + 4] = block.reshape(4, TOK_DEV, 2 * HEAD)
         dl[t, me] = stage[t, me]
         for k in range(1, N_SHARD):
             peer = lax.rem(me + k, N_SHARD)
@@ -624,9 +859,7 @@
             source = lax.rem(me + N_SHARD - k, N_SHARD)
             to_owner(t, k, source, source, source).wait_recv()
         grad = jnp.sum(dl[t].astype(f32), axis=0).astype(bf16)
-        turned = dot(grad, turn_ref[1], NT)
-        grad = grad.astype(f32) * cos_ref[1, t] + turned * sin_ref[1, t]
-        pgm_ref[t] = grad.astype(bf16)
+        pgm_ref[t] = turned(grad, 1, t)
 
         @pl.when(t != seq)
         def _():
@@ -635,17 +868,33 @@
         return carry
 
     lax.fori_loop(0, N_SEQ, gathered, 0)
-    mine = pltpu.make_async_copy(pgq_ref.at[seq], tokq_ref.at[seq], own.at[2])
-    mine.start()
-    other = pltpu.make_async_copy(pgm_ref.at[seq], tokm_ref.at[seq], own.at[3])
-    other.start()
-    for k in range(1, N_SEQ):
-        to_head(k, seq, lax.rem(seq + k, N_SEQ)).wait_send()
+    mine = [
+        pltpu.make_async_copy(pgq_ref.at[seq], tokq_ref.at[seq], own.at[4]),
+        pltpu.make_async_copy(pgm_ref.at[seq], tokm_ref.at[seq], own.at[5]),
+    ]
+    for copy in mine:
+        copy.start()
+
+    for part in range(2):
+        for k in range(1, N_SHARD):
+            peer = lax.rem(me + k, N_SHARD)
+            to_source(part, k, peer, me, peer).wait_send()
+    for p in range(N_SEQ):
+        if p > 1:
+            to_head(p).wait_send()
+        else:
+
+            @pl.when(far != p)
+            def _(p=p):
+                to_head(p).wait_send()
+
     for k in range(1, N_SHARD):
         to_token_expert(k).wait()
-    came_own.wait()
-    for n in range(6):
-        to_ring(n).wait()
+    for e in range(LOCAL_EXPERTS):
+        for k in (1, 2, 3):
+            to_ring(e, k).wait()
+    for k in (1, 2, 3):
+        out_to_ring(k).wait()
 
     def end(t, carry):
         for k in range(1, N_SHARD):
@@ -659,24 +908,49 @@
             peer = lax.rem(seq + k, N_SEQ)
             to_token(n, peer, seq).wait_send()
             to_token(n, peer, peer).wait_recv()
-    mine.wait()
-    other.wait()
-
-
-def attention_back(
-    queries, upstream, wide, lse, memory, cosine, sine, turn, expert_out, parts, ident
-):
+    for copy in mine + dw_own + [came_own, po_own]:
+        copy.wait()
+
+
+def late(operands, ident):
     dma = pltpu.SemaphoreType.DMA
     vmem = pl.BlockSpec(memory_space=pltpu.VMEM)
     chunk = jax.ShapeDtypeStruct((N_SEQ, TOK_DEV, 2 * HEAD), bf16)
+    wide = jax.ShapeDtypeStruct((TOK_DEV, WIDTH), f32)
+    routed = (N_SHARD, 80, WIDTH)
+    grads = (LOCAL_EXPERTS, 2, 192, WIDTH)
     return pl.pallas_call(
-        attention_back_kernel,
-        in_specs=[vmem, ANY, vmem, vmem, vmem, vmem, vmem, vmem, ANY] + [ANY] * 6,
-        out_specs=[vmem, vmem, ANY, ANY, ANY] + [ANY] * 6,
-        out_shape=[chunk] * 4
-        + [jax.ShapeDtypeStruct(expert_out.shape, bf16)]
-        + [jax.ShapeDtypeStruct(part.shape, bf16) for part in parts],
+        late_kernel,
+        in_specs=[vmem] * 8 + [ANY] + [vmem] * 7,
+        out_specs=[vmem] * 4 + [ANY] * 7,
+        out_shape=[
+            wide,
+            wide,
+            chunk,
+            chunk,
+            chunk,
+            chunk,
+            jax.ShapeDtypeStruct(routed, bf16),
+            jax.ShapeDtypeStruct(grads, bf16),
+            jax.ShapeDtypeStruct((3,) + grads, bf16),
+            jax.ShapeDtypeStruct((2, 128, WIDTH), bf16),
+            jax.ShapeDtypeStruct((3, 2, 128, WIDTH), bf16),
+        ],
         scratch_shapes=[
+            pltpu.VMEM((LOCAL_EXPERTS, WIDTH, 2 * FF), bf16),
+            pltpu.VMEM((LOCAL_EXPERTS, FF, WIDTH), bf16),
+            pltpu.VMEM(routed, bf16),
+            pltpu.VMEM(routed, bf16),
+            pltpu.VMEM(routed, bf16),
+            pltpu.VMEM((LOCAL_EXPERTS, WIDTH, EXPERT_ROWS), bf16),
+            pltpu.VMEM((LOCAL_EXPERTS, FF, EXPERT_ROWS), bf16),
+            pltpu.VMEM((LOCAL_EXPERTS, EXPERT_ROWS, 2 * FF), bf16),
+            pltpu.VMEM((LOCAL_EXPERTS, 128, WIDTH), bf16),
+            pltpu.VMEM((2, LOCAL_EXPERTS, 128, WIDTH), bf16),
+            pltpu.VMEM((LOCAL_EXPERTS, 4, 2, 192, WIDTH), bf16),
+            pltpu.VMEM((TOK_DEV, WIDTH), bf16),
+            pltpu.VMEM((N_SEQ, TOK_DEV, 128), bf16),
+            pltpu.VMEM((4, 2, 128, WIDTH), bf16),
             pltpu.VMEM((N_SEQ, TOK_DEV, 2 * HEAD), bf16),
             pltpu.VMEM((N_SEQ, 2 * TOK_DEV, 2 * HEAD), bf16),
             pltpu.VMEM((N_SEQ, 2 * TOK_DEV, 2 * HEAD), bf16),
@@ -686,96 +960,30 @@
             pltpu.VMEM((N_SEQ, HEAD, 2 * TOK_DEV), f32),
             pltpu.VMEM((N_SEQ, N_SHARD, TOK_DEV, 2 * HEAD), bf16),
             pltpu.VMEM((N_SEQ, N_SHARD, TOK_DEV, 2 * HEAD), bf16),
-            dma((N_SEQ, 15)),
-            dma((N_SEQ, 15)),
-            dma((N_SEQ - 1,)),
-            dma((N_SEQ - 1,)),
+            dma((LOCAL_EXPERTS, N_SEQ, 2)),
+            dma((2, N_SHARD - 1)),
+            dma((2, N_SHARD - 1)),
+            dma((2, N_SHARD - 1)),
+            dma((2, N_SHARD - 1)),
+            dma((LOCAL_EXPERTS, 3)),
+            dma((LOCAL_EXPERTS, 3)),
+            dma((3,)),
+            dma((3,)),
+            dma((N_SEQ, N_SHARD - 1)),
+            dma((N_SEQ, N_SHARD - 1)),
+            dma((N_SEQ,)),
+            dma((N_SEQ,)),
             dma((N_SHARD - 1,)),
             dma((N_SHARD - 1,)),
-            dma((6,)),
-            dma((6,)),
             dma((2, N_SEQ)),
             dma((2, N_SEQ)),
-            dma((4,)),
+            dma((6,)),
         ],
         compiler_params=pltpu.CompilerParams(
-            collective_id=ident, has_side_effects=True, vmem_limit_bytes=56 << 20
+            collective_id=ident, has_side_effects=True, vmem_limit_bytes=63 << 20
         ),
-        name="attention_backward",
-    )(queries, upstream, wide, lse, memory, cosine, sine, turn, expert_out, *parts)
-
-
-def expert_kernel(s_ref, x_ref, g_ref, w_ref, out_ref, back_ref, *refs):
-    grad_refs, (gu, down, xt, ht, both) = refs[:4], refs[4:]
-    gu[...] = w_ref[0, :, :128, :].reshape(WIDTH, 2 * FF)
-    down[...] = w_ref[0, :, 128:, :].reshape(FF, WIDTH)
-
-    def rows_step(t, carry):
-        rows = pl.ds(pl.multiple_of(t * 128, 128), 128)
-        x = x_ref[0, rows, :]
-        pre = dot(x, gu[...], NN)
-        gate, up = pre[:, :FF], pre[:, FF:]
-        sigmoid = jax.nn.sigmoid(gate)
-        act = gate * sigmoid
-        hidden = (act * up).astype(bf16)
-        out_ref[0, rows, :] = dot(hidden, down[...], NN).astype(bf16)
-        units = dot(g_ref[0, rows, :], down[...], NT)
-        gate_grad = (units * up * sigmoid * (1.0 + gate * (1.0 - sigmoid))).astype(bf16)
-        up_grad = (units * act).astype(bf16)
-        pair = jnp.concatenate([gate_grad, up_grad], axis=1)
-        back_ref[0, rows, :] = dot(pair, gu[...], NT).astype(bf16)
-        both[rows, :] = pair
-        xt[:, rows] = x.T
-        ht[:, rows] = hidden.T
-        return carry
-
-    lax.fori_loop(0, EXPERT_ROWS // 128, rows_step, 0)
-    far = s_ref[0] % 2
-    ring = s_ref[0] // 2
-    for k in range(4):
-
-        def grad_step(n, carry, k=k):
-            s = (ring + k) % 4 * 2 + (far + n) % 2
-            features = pl.ds(pl.multiple_of(s * 128, 128), 128)
-            units = pl.ds(pl.multiple_of(s * 64, 64), 64)
-            grad_refs[k][n, 0, :128, :] = dot(xt[features, :], both[...], NN).astype(bf16)
-            grad_refs[k][n, 0, 128:, :] = dot(ht[units, :], g_ref[0], NN).astype(bf16)
-            return carry
-
-        lax.fori_loop(0, 2, grad_step, 0)
-
-
-def experts(seq, x, g, w):
-    rows = pl.BlockSpec((1, EXPERT_ROWS, WIDTH), lambda e, s: (e, 0, 0))
-    shape = jax.ShapeDtypeStruct((LOCAL_EXPERTS, EXPERT_ROWS, WIDTH), bf16)
-    return pl.pallas_call(
-        expert_kernel,
-        grid_spec=pltpu.PrefetchScalarGridSpec(
-            num_scalar_prefetch=1,
-            grid=(LOCAL_EXPERTS,),
-            in_specs=[
-                rows,
-                rows,
-                pl.BlockSpec((1, N_SEQ, 192, WIDTH), lambda e, s: (e, 0, 0, 0)),
-            ],
-            out_specs=[rows, rows]
-            + [pl.BlockSpec((2, 1, 192, WIDTH), lambda e, s: (0, e, 0, 0))] * 4,
-            scratch_shapes=[
-                pltpu.VMEM((WIDTH, 2 * FF), bf16),
-                pltpu.VMEM((FF, WIDTH), bf16),
-                pltpu.VMEM((WIDTH, EXPERT_ROWS), bf16),
-                pltpu.VMEM((FF, EXPERT_ROWS), bf16),
-                pltpu.VMEM((EXPERT_ROWS, 2 * FF), bf16),
-            ],
-        ),
-        out_shape=[shape, shape]
-        + [jax.ShapeDtypeStruct((2, LOCAL_EXPERTS, 192, WIDTH), bf16)] * 4,
-        compiler_params=pltpu.CompilerParams(vmem_limit_bytes=56 << 20),
-        cost_estimate=pl.CostEstimate(
-            flops=10**8, bytes_accessed=1 << 20, transcendentals=10**5
-        ),
-        name="experts",
-    )(seq, x, g, w)
+        name="experts_attention_backward",
+    )(*operands)
 
 
 def group_columns(rows):
@@ -832,10 +1040,12 @@
     earlier = (token[:, None] > token[None, :]).astype(bf16)
     before = dot(earlier, mask.astype(bf16), NN)
     code = jnp.where(mask > 0.0, before, -1.0).astype(bf16)
-    slot = jnp.arange(EXPERTS * CAP, dtype=jnp.int32)
-    owner = slot // CAP % N_SHARD * LOCAL_EXPERTS + slot // (CAP * N_SHARD)
+    place = jnp.arange(N_SHARD * 80, dtype=jnp.int32)
+    row = place % 80
+    slot = jnp.where(row < 40, row, jnp.where(row < 48, row - 8, row - 48))
+    owner = place // 80 * LOCAL_EXPERTS + (row >= 40).astype(jnp.int32)
     widen = (owner[None, :] == ids[:, None]).astype(bf16)
-    pick = dot(code, widen, NN) == (slot % CAP).astype(f32)[None, :]
+    pick = dot(code, widen, NN) == slot.astype(f32)[None, :]
     high = weight.astype(bf16)
     low = (weight - high.astype(f32)).astype(bf16)
     high = jnp.where(pick, dot(high, widen, NN), 0.0)
@@ -858,7 +1068,6 @@
 ):
     seq = lax.axis_index("seq")
     shard = lax.axis_index("shard")
-    seq_array = seq.astype(jnp.int32).reshape(1)
     along_x = [(s, s + 1 - 2 * (s % 2)) for s in range(N_SEQ)]
 
     grouped = group_columns(w_qkv)
@@ -898,96 +1107,69 @@
     memory = memory.reshape(N_SEQ, TOK_DEV, 2 * HEAD)
 
     pick, scale_high, scale_low, slot_scale = routing(routes, route_weights)
-    out_grad = cotangent.astype(f32)
-    slots = (LOCAL_EXPERTS, N_SHARD, CAP, WIDTH)
-    grad_send = (slot_scale[:, None] * dot(pick, cotangent, TN)).astype(bf16).reshape(slots)
-    qkv_rows = jnp.broadcast_to(grouped.reshape(1, 16, WIDTH), (N_SHARD, 16, WIDTH))
-    grad_send = jnp.concatenate([grad_send[0], grad_send[1], qkv_rows], axis=1)
-    attended_wide, lse, attended_full, memory, grad_rows, out_slabs = attention(
-        queries, memory, grad_send, out_slabs, 2
-    )
-    qkv_rows = grad_rows[:, 2 * CAP :].reshape(N_SHARD * 8, 2 * WIDTH)
-    grad_rows = jnp.stack([grad_rows[:, :CAP], grad_rows[:, CAP : 2 * CAP]])
-    grad_rows = grad_rows.reshape(LOCAL_EXPERTS, EXPERT_ROWS, WIDTH)
-
-    order = jnp.stack(
-        [(seq // 2 + 4 - k) % 4 * 2 + half for k in range(4) for half in range(2)]
-    )
-    attended_full = attended_full[order].transpose(1, 0, 2).reshape(TOK_DEV, WIDTH)
-    x_wide = layer_input.astype(f32)
-    out_weight = out_slabs.reshape(WIDTH, WIDTH)
-    residual = x_wide + dot(attended_full, out_weight, NN)
-    inverse_two = lax.rsqrt(jnp.mean(residual * residual, axis=1, keepdims=True) + epsilon)
-    normed_moe = (residual * inverse_two * gain_moe).astype(bf16)
-
-    send_rows = dot(pick, normed_moe, TN).astype(bf16).reshape(slots)
-    expert_rows = exchange(send_rows, "shard", N_SHARD, 4, dim=1)
-    expert_rows = expert_rows.reshape(LOCAL_EXPERTS, EXPERT_ROWS, WIDTH)
-    expert_out, rows_grad, *expert_grads = experts(
-        seq_array, expert_rows, grad_rows, expert_weights
-    )
-    returned = exchange(rows_grad.reshape(slots), "shard", N_SHARD, 5, dim=1)
+    pick_turned = pick.T
+    grad_send = (slot_scale[:, None] * dot(pick_turned, cotangent, NN)).astype(bf16)
+    attended_wide, lse, attended, memory, grad_rows, qkv_rows, out_slabs = attention(
+        queries,
+        memory,
+        grad_send.reshape(N_SHARD, 80, WIDTH),
+        grouped.reshape(16, WIDTH),
+        out_slabs,
+        2,
+    )
+    qkv_rows = qkv_rows.reshape(N_SHARD * 8, 2 * WIDTH)
     qkv_all = lax.all_gather(qkv_rows, "seq", axis=0, tiled=True)
-
-    moe_in_grad = dot(pick, returned.reshape(EXPERTS * CAP, WIDTH), NN)
-    scaled = moe_in_grad * gain_moe
-    moe_part = inverse_two * scaled - residual * inverse_two**3 * jnp.mean(
-        residual * scaled, axis=1, keepdims=True
-    )
-    residual_grad = out_grad + moe_part
-    branch_grad = residual_grad.astype(bf16)
-    attended_grad = dot(branch_grad, out_weight, NT).astype(bf16)
-    attended_grad = attended_grad.reshape(TOK_DEV, N_SEQ, 2 * HEAD).transpose(1, 0, 2)
-    back_order = jnp.stack(
-        [(seq // 2 + 4 - z) % 4 * 2 + half for z in range(4) for half in range(2)]
-    )
-    attended_grad = attended_grad[back_order]
-
-    out_parts = []
-    for k in range(4):
-        back = (4 - k) % 4 * COLS
-        block = dot(attended_full[:, back : back + COLS], branch_grad, TN)
-        out_parts.append(block.astype(bf16))
-    tables = [
-        (cosine[:, : 2 * HEAD], sine[:, : 2 * HEAD]),
-        (
-            jnp.concatenate([cosine[:, :HEAD], jnp.ones((HEAD_ROWS, HEAD), f32)], axis=1),
-            jnp.concatenate([sine[:, :HEAD], jnp.zeros((HEAD_ROWS, HEAD), f32)], axis=1),
-        ),
-    ]
-    tables = [
-        jnp.stack(table).reshape(2, N_SEQ, TOK_DEV, 2 * HEAD) for table in zip(*tables)
-    ]
     left = jnp.arange(2 * HEAD, dtype=jnp.int32) < HEAD
     turns = turn[: 2 * HEAD, : 2 * HEAD]
     turns = jnp.stack([turns, jnp.where(left[:, None] & left[None, :], turns, 0)])
-    query_grad, memory_grad, token_query, token_memory, came_back, *sent = attention_back(
-        queries,
-        attended_grad,
-        attended_wide,
-        lse,
-        memory,
-        *tables,
-        turns,
-        expert_out.reshape(slots),
-        expert_grads[1:] + out_parts[1:],
-        6,
-    )
-    came_back = came_back.reshape(EXPERTS * CAP, WIDTH)
-    expert_sums = sum(grad.astype(f32) for grad in [expert_grads[0]] + sent[:3])
-    out_sums = sum(grad.astype(f32) for grad in [out_parts[0]] + sent[3:])
-    out_sums = out_sums.reshape(2, 2 * HEAD, WIDTH)
+    (
+        residual,
+        residual_grad,
+        query_grad,
+        memory_grad,
+        token_query,
+        token_memory,
+        came_back,
+        expert_mine,
+        expert_sent,
+        out_own,
+        out_sent,
+    ) = late(
+        (
+            attended,
+            out_slabs.reshape(WIDTH, WIDTH),
+            layer_input,
+            cotangent,
+            gain_moe[None, :],
+            pick,
+            pick_turned,
+            grad_rows,
+            expert_weights,
+            queries,
+            attended_wide,
+            lse,
+            memory,
+            cosine[:, : 2 * HEAD].reshape(N_SEQ, TOK_DEV, 2 * HEAD),
+            sine[:, : 2 * HEAD].reshape(N_SEQ, TOK_DEV, 2 * HEAD),
+            turns,
+        ),
+        3,
+    )
+    came_back = came_back.reshape(N_SHARD * 80, WIDTH)
+    expert_sums = expert_mine.astype(f32) + jnp.sum(expert_sent.astype(f32), axis=0)
+    out_sums = out_own.astype(f32) + jnp.sum(out_sent.astype(f32), axis=0)
     far = seq % 2
     out_mine = lax.dynamic_index_in_dim(out_sums, far, 0, keepdims=False)
     out_other = lax.dynamic_index_in_dim(out_sums, 1 - far, 0, keepdims=False)
     other = jnp.concatenate(
-        [expert_sums[1].reshape(LOCAL_EXPERTS * 192, WIDTH), out_other], axis=0
+        [expert_sums[:, 1].reshape(LOCAL_EXPERTS * 192, WIDTH), out_other], axis=0
     ).astype(bf16)
     other = lax.ppermute(other, "seq", along_x).astype(f32)
-    expert_sums = expert_sums[0] + other[: LOCAL_EXPERTS * 192].reshape(
+    expert_sums = expert_sums[:, 0] + other[: LOCAL_EXPERTS * 192].reshape(
         LOCAL_EXPERTS, 192, WIDTH
     )
     out_part = out_mine + other[LOCAL_EXPERTS * 192 :]
+    x_wide = layer_input.astype(f32)
     moe_sum = dot(scale_high, came_back, NN) + dot(scale_low, came_back, NN)
     block_out = (residual + moe_sum).astype(bf16)
 
@@ -1015,7 +1197,7 @@
         ],
         axis=1,
     )
-    sums = jnp.sum(exchange(sums, "shard", N_SHARD, 7).astype(f32), axis=0)
+    sums = jnp.sum(exchange(sums, "shard", N_SHARD, 4).astype(f32), axis=0)
     out_weight_grad = sums[64:96].reshape(8, WIDTH)
     moe_gain_grad = sums[96, :8] + sums[97, :8]
     qkv_groups = lax.all_to_all(sums[:64].reshape(N_SEQ, 8, COLS), "seq", 0, 0)

time: 532 us -> 471 us (0.89)
  Pallas kernels: 389 us -> 352 us
  other arithmetic: 31.7 us -> 17.6 us
  matrix products: 26.1 us -> 14.8 us
  local copies, waits for them, and re-layouts: 40.2 us -> 29.4 us
  waiting for transfers between devices: 18.8 us -> 26 us
    pallas_call x3 -> x1, Pallas kernels: 93.6 us -> 16.3 us  [exchange(): pl.pallas_call(functools.partial(exchange_kernel, axis, count, dim), out_...]
    pallas_call x3 -> x2, Pallas kernels: 251 us -> 292 us  [the longest x1 189 us: late(): pl.pallas_call(late_kernel, in_specs=[vmem] * 8 + [ANY] + [vmem] * 7, out...]
    dot_general x18 -> x10, matrix products: 26.1 us -> 14.8 us  [dot(): return lax.dot_general(left, right, dims, preferred_element_type=f32)]
    ppermute x1, waiting for transfers between devices: 14.1 us -> 20.9 us  [on_device(): other = lax.ppermute(other, 'seq', along_x).astype(f32)]
  transfers between devices with their start and end apart: 4 -> 4, of which waited for: 2 -> 2; matrix products, arithmetic and copies ran while one was open for 14% -> 7% of each run, Pallas kernels for 62% -> 63%
where the time goes in v3:
time: 471 us; the launch traced here: 465 us
  Pallas kernels  352 us (75%)
  local copies, waits for them, and re-layouts  29.4 us (6%)
  waiting for transfers between devices  26 us (6%)
  other arithmetic  17.6 us (4%)
  between operations  15.2 us (3%)
  matrix products  14.8 us (3%)
  starting transfers between devices  9.44 us (2%)
    pallas_call x1, Pallas kernels, late(): pl.pallas_call(late_kernel, in_specs=[vmem] * 8 + [ANY] + [vmem] * 7, out...  189 us
    pallas_call x1, Pallas kernels, attention(): pl.pallas_call(attention_kernel, in_specs=[vmem, vmem, ANY, ANY, ANY], ou...  102 us
    pallas_call x1, Pallas kernels, first_gather(): pl.pallas_call(first_kernel, out_shape=[jax.ShapeDtypeStruct((N_SEQ, 8, T...  44 us
    ppermute x1, waiting for transfers between devices, on_device(): other = lax.ppermute(other, 'seq', along_x).astype(f32)  20.9 us
    pallas_call x1, Pallas kernels, exchange(): pl.pallas_call(functools.partial(exchange_kernel, axis, count, dim), out_...  16.3 us
    dot_general x10, matrix products, dot(): return lax.dot_general(left, right, dims, preferred_element_type=f32)  14.8 us
    unnamed x73, local copies, waits for them, and re-layouts  10.1 us
  transfers between devices with their start and end apart: 4, of which 2 were waited for; matrix products, arithmetic and copies ran while one was open for 7% of the time, Pallas kernels for 63%

profile of v3, /device:TPU:1, one launch (start us, length us, event | category | flops | bytes accessed | tf_op | source)
XLA Modules:
  0.0 464.8 jit_solution(17248700461786451681)
XLA Ops:
  7.2 0.7 slice_bitcast_fusion.6
  7.9 0.7 fusion.71
  8.9 1.0 constant_dynamic-update-slice_fusion.1
  9.9 0.8 pad_maximum_fusion.8
  11.3 1.0 constant_dynamic-update-slice_fusion
  12.3 0.8 copy-done.11
  13.1 1.9 pad_maximum_fusion.2
  15.0 44.0 %gather_tokens.1 = (bf16[8,8,16,1024]{3,2,1,0:T(8,128)(2,1)}, bf16[16,9,16,128]{3,2,1,0:T(8,128)(2,1)}, bf16[2,16,2,32,128]{4,3,2,1,0:T(8,128)(2,1)}) custom-call(bf16[8,16,1024]{2,1,0:T(8,128)(2,1)} %bitcast.112, bf16[8,32,128]{2,1,0:T(8,128)(2,1)} %pad_maximum_fusion.4.w_ref, bf16[2,32,128]{2,1,0:T(8,128)(2,1)} %bitcast.128), custom_call_target="tpu_custom_call" | custom-call | tf_op jit(solution)/shard_map/gather_tokens/pallas_call | solution.py:219
  59.2 1.2 slice_bitcast_fusion.1
  61.3 0.8 slice_bitcast_fusion.4
  62.1 0.7 slice_convert_fusion.2
  62.9 1.1 convolution_convert_fusion.1
  64.0 1.2 copy.138
  65.8 1.2 fusion.8
  70.1 1.1 add_reduce_fusion
  71.3 2.4 multiply_convert_fusion
  73.7 102.5 %attention_forward.1 = (f32[8,128,128]{2,1,0:T(8,128)S(1)}, f32[8,1,256]{2,1,0:T(1,128)S(1)}, bf16[8,128,128]{2,1,0:T(8,128)(2,1)S(1)}, bf16[8,16,128,128]{3,2,1...) custom-call(bf16[8,128,128]{2,1,0:T(8,128)(2,1)S(1)} %bitcast.100, ...), custom_call_target="tpu_custom_call" | custom-call | tf_op jit(solution)/shard_map/attention_forward/pallas_call | solution.py:483
  176.2 1.4 copy-done.1
  177.6 0.8 copy-done.2
  178.4 0.7 copy-done.4
  179.7 1.0 reshape.398
  180.8 0.7 reshape.410.refs_4_
  181.5 0.8 convert_bitcast_fusion
  182.3 0.9 copy.149.refs_5_
  183.4 1.0 copy.147
  184.6 1.0 copy.148
  185.6 2.6 copy.151
  188.3 0.6 pad_maximum_fusion.5.refs_15_
  188.9 189.5 %experts_attention_backward.1 = (f32[128,1024]{1,0:T(8,128)}, f32[128,1024]{1,0:T(8,128)}, bf16[8,128,128]{2,1,0:T(8,128)(2,1)}, bf16[8,128,128]{2,1,0:T(8,128)(...) custom-call(bf16[8,128,128]{2,1,0:T(8,128)(2,1)} %copy-done.4, ...), custom_call_target="tpu_custom_call" | custom-call | tf_op jit(solution)/shard_map/experts_attention_backward/pallas_call | solution.py:922
  378.5 2.4 fusion.3
  380.9 0.8 copy.165
  382.2 3.9 fusion.14
  386.1 1.8 convert_reduce_fusion.1
  388.0 1.1 convert_reduce_fusion
  390.6 1.0 copy-done.13
  391.7 1.5 collective-permute-start
  393.3 0.9 fusion.18
  395.3 1.3 fusion.5
  396.5 20.9 %collective-permute-done = bf16[512,1024]{1,0:T(8,128)(2,1)S(1)} collective-permute-done((bf16[512,1024]{1,0:T(8,128)(2,1)S(1)}, bf16[512,1024]{1,0:T(8,128)(2,1)S(1)}, u32[]{:S(2)}, u32[]{:S(2)}) %collective-permute-start) | collective-permute-done | bytes 1048608 | tf_op jit(solution)/shard_map/ppermute | solution.py:1167
  417.9 0.8 copy-done.12
  418.9 1.1 fusion.69
  420.6 0.9 copy-done.14
  421.8 1.0 pad_maximum_fusion.1.x_ref
  422.8 16.3 %exchange_shard.1 = bf16[16,112,256]{2,1,0:T(8,128)(2,1)} custom-call(bf16[16,112,256]{2,1,0:T(8,128)(2,1)} %pad_maximum_fusion.1.x_ref), custom_call_target="tpu_custom_call" | custom-call | tf_op jit(solution)/shard_map/exchange_shard/pallas_call | solution.py:86
  439.2 1.3 convert_reduce_fusion.2
  441.1 7.8 %all-to-all-start = ((f32[8,8,256]{2,1,0:T(8,128)}), f32[8,8,256]{2,1,0:T(8,128)S(1)}, u32[]{:S(2)}, u32[]{:S(2)}) async-start(f32[8,8,256]{2,1,0:T(8,128)} %slice_bitcast_fusion.2), calls=%async_computation | async-start | bytes 131072 | tf_op jit(solution)/shard_map/all_to_all | solution.py:1203
  449.4 0.8 slice.160
  450.9 5.0 %all-to-all-done = f32[8,8,256]{2,1,0:T(8,128)S(1)} async-done(((f32[8,8,256]{2,1,0:T(8,128)}), f32[8,8,256]{2,1,0:T(8,128)S(1)}, u32[]{:S(2)}, u32[]{:S(2)}) %all-to-all-start) | async-done | bytes 65568 | tf_op jit(solution)/shard_map/all_to_all | solution.py:1203
  (153 shorter events, 14.8 us)
Async XLA Ops:
  7.2 181.8 %all-gather.6.cloned.1.call-start = ((), (), s32[]{:S(2)}) async-start(), calls=%async_computation.2 | async-start | bytes 7077888 | tf_op jit(solution)/shard_map/all_gather | solution.py:1087
  12.3 0.8 copy-start.11
  59.0 1.7 copy-start.9
  59.0 323.1 %all-gather.4.cloned.1.call-start = ((), (), s32[]{:S(2)}) async-start(), calls=%async_computation.1 | async-start | bytes 4718592 | tf_op jit(solution)/shard_map/all_gather | solution.py:1121
  62.9 2.9 copy-start.31
  65.8 1.3 copy-start.7
  67.4 1.7 copy-start.29
  67.4 1.7 copy-start.30
  67.9 0.7 copy-start.18
  68.0 0.7 copy-start.20
  68.8 4.8 %copy-start = (bf16[1024,128]{1,0:T(8,128)(2,1)}, bf16[1024,128]{1,0:T(8,128)(2,1)S(1)}, u32[]{:S(2)}) copy-start(bf16[1024,128]{1,0:T(8,128)(2,1)S(1)} %copy.139) | copy-start | bytes 786436
  69.1 2.2 copy-start.22
  70.1 3.5 copy-start.3
  73.7 107.0 %copy-start.26 = (f32[8,16,8]{2,0,1:T(8,128)S(1)}, f32[8,16,8]{2,0,1:T(8,128)}, u32[]{:S(2)}) copy-start(f32[8,16,8]{2,0,1:T(8,128)} %get-tuple-element.65) | copy-start | bytes 12292
  176.2 1.4 copy-start.1
  177.6 0.8 copy-start.2
  178.4 0.7 copy-start.4
  179.1 0.6 copy-start.5
  179.7 3.6 copy-start.21
  181.5 2.9 copy-start.19
  183.4 2.1 copy-start.8
  185.6 2.6 copy-start.32
  378.4 3.3 copy-start.27
  378.4 3.3 copy-start.28
  380.9 1.3 copy-start.10
  381.8 6.1 %slice-start = ((s8[4718592]{0:T(1024)(128)(4,1)}), s8[524288]{0:T(1024)(128)(4,1)S(1)}, s32[]{:S(2)}) async-start(s8[4718592]{0:T(1024)(128)(4,1)} %bitcast.110), calls=%async_computation.3 | async-start | bytes 1048576
  382.2 5.8 %slice-start.1 = ((s8[4718592]{0:T(1024)(128)(4,1)}), s8[4194304]{0:T(1024)(128)(4,1)S(1)}, s32[]{:S(2)}) async-start(s8[4718592]{0:T(1024)(128)(4,1)} %bitcast.110), calls=%async_computation.4 | async-start | bytes 8388608
  388.0 1.4 copy-start.16
  389.4 1.0 copy-start.25
  390.4 2.9 copy-start.24
  390.6 1.0 copy-start.13
  391.6 2.6 copy-start.6
  391.6 2.6 copy-start.17
  391.7 25.7 %collective-permute-start = (bf16[512,1024]{1,0:T(8,128)(2,1)S(1)}, bf16[512,1024]{1,0:T(8,128)(2,1)S(1)}, u32[]{:S(2)}, u32[]{:S(2)}) collective-permute-start(bf16[512,1024]{1,0:T(8,128)(2,1)S(1)} %pad_maximum_fusion), channel_id=1, source_target_pairs={{0,16},{16,0},{32,48},{48,32},{64,80},{80,64},{96,112},{112,96},{1... | collective-permute-start | bytes 3145736 | tf_op jit(solution)/shard_map/ppermute | solution.py:1167
  394.2 1.0 copy-start.23
  417.6 1.0 copy-start.12
  420.3 1.2 copy-start.14
  420.4 1.4 copy-start.15
  422.8 33.4 %copy-start.33 = (bf16[8]{0:T(256)(128)(2,1)S(1)}, bf16[8]{0:T(256)(128)(2,1)}, u32[]{:S(2)}) copy-start(bf16[8]{0:T(256)(128)(2,1)} %param.12) | copy-start | bytes 52
  441.1 14.8 %all-to-all-start = ((f32[8,8,256]{2,1,0:T(8,128)}), f32[8,8,256]{2,1,0:T(8,128)S(1)}, u32[]{:S(2)}, u32[]{:S(2)}) async-start(f32[8,8,256]{2,1,0:T(8,128)} %slice_bitcast_fusion.2), calls=%async_computation | async-start | bytes 131072 | tf_op jit(solution)/shard_map/all_to_all | solution.py:1203
Sparse Core Ops, SparseCore 0:
  59.2 122.2 all-gather.5
  183.8 93.5 all-gather.3

commit v4 on v3

v4 whole, which is shorter than its diff:
```python
import functools
import math

import jax
import jax.numpy as jnp
from jax import lax
from jax.experimental import pallas as pl
from jax.experimental.pallas import tpu as pltpu
from jax.sharding import PartitionSpec as P

HEADS = 16
KV = 8
HEAD = 64
EXPERTS = 32
TOPK = 8
TOK_DEV = 128
CAP = 40
WIDTH = 1024
FF = 512
N_SEQ = 8
N_SHARD = 16
HEAD_ROWS = TOK_DEV * N_SEQ
TOKENS = TOK_DEV * N_SEQ * N_SHARD
LOCAL_EXPERTS = EXPERTS // N_SHARD
EXPERT_ROWS = N_SHARD * CAP
COLS = 256
SUPER = TOK_DEV * N_SHARD
BWD_TILE = 1024
LIMIT = 63

epsilon = 1e-06
rope_base = 10000.0

f32 = jnp.float32
bf16 = jnp.bfloat16
MESH = pl.DeviceIdType.MESH
ANY = pl.BlockSpec(memory_space=pl.ANY)
NT = (((1,), (1,)), ((), ()))
NN = (((1,), (0,)), ((), ()))
TN = (((0,), (0,)), ((), ()))


def dot(left, right, dims):
    return lax.dot_general(left, right, dims, preferred_element_type=f32)


def greet(peers):
    barrier = pltpu.get_barrier_semaphore()
    for axis, peer in peers:
        pl.semaphore_signal(barrier, inc=1, device_id={axis: peer}, device_id_type=MESH)
    pl.semaphore_wait(barrier, len(peers))


def remote(source, target, send, recv, axis, peer):
    copy = pltpu.make_async_remote_copy(
        src_ref=source,
        dst_ref=target,
        send_sem=send,
        recv_sem=recv,
        device_id={axis: peer},
        device_id_type=MESH,
    )
    copy.start()
    return copy


def staged(axis, units, share, x_ref, place, sem_send, sem_recv, own):
    me = lax.axis_index(axis)
    cores = 2 if axis == "shard" else 1
    core = lax.rem(me, cores)
    pair = lax.rem(me // cores, 2)
    ring = me // (2 * cores)

    def at(r, p, c):
        return (r * 2 + p) * cores + c

    ring_peer = [at(lax.rem(ring + k, 4), pair, core) for k in (1, 2, 3)]
    ring_from = [lax.rem(ring + 4 - k, 4) for k in (1, 2, 3)]
    pair_peer = at(ring, 1 - pair, core)
    core_peer = at(ring, pair, 1 - core)
    mine = pltpu.make_async_copy(x_ref, place(me, 0, units), own)
    mine.start()
    sends = []

    def go(source, index, low, high, peer):
        n = len(sends)
        sends.append(
            remote(source, place(index, low, high), sem_send.at[n], sem_recv.at[n], axis, peer)
        )
        return sends[-1]

    to_pair = go(x_ref, me, 0, units, pair_peer)
    to_ring = [go(x_ref, me, 0, units, peer) for peer in ring_peer]
    landed = []
    if cores == 2:
        landed.append(go(x_ref, me, 0, units, core_peer))

    def pass_core(index, low, high):
        if cores == 2:
            landed.append(go(place(index, low, high), index, low, high, core_peer))

    to_pair.wait_recv()
    fwd_ring = [
        go(place(pair_peer, 0, share), pair_peer, 0, share, peer) for peer in ring_peer
    ]
    pass_core(pair_peer, 0, units)
    fwd_pair = []
    for k in (0, 2, 1):
        to_ring[k].wait_recv()
        source = at(ring_from[k], pair, core)
        if share < units:
            fwd_pair.append((k, go(place(source, share, units), source, share, units, pair_peer)))
        pass_core(source, 0, units)
    for k in (0, 2, 1):
        fwd_ring[k].wait_recv()
        pass_core(at(ring_from[k], 1 - pair, core), 0, share)
    for k, copy in fwd_pair:
        copy.wait_recv()
        pass_core(at(ring_from[k], 1 - pair, core), share, units)
    for copy in landed:
        copy.wait_recv()
    mine.wait()
    for copy in sends:
        copy.wait_send()


def first_kernel(
    x_ref, w_ref, v_ref, xo_ref, wo_ref, vo_ref, w_mid, w_pack, send, recv, own, wsend, wrecv, wown, vown
):
    seq = lax.axis_index("seq")
    shard = lax.axis_index("shard")
    greet(
        [("seq", lax.rem(seq + k, N_SEQ)) for k in range(1, N_SEQ)]
        + [("shard", lax.rem(shard + k, N_SHARD)) for k in range(1, N_SHARD)]
    )
    mine = pltpu.make_async_copy(w_ref.at[seq], w_mid.at[seq], wown)
    mine.start()
    slab = pltpu.make_async_copy(v_ref, vo_ref.at[shard], vown)
    slab.start()
    pieces = []
    for k in range(1, N_SEQ):
        peer = lax.rem(seq + k, N_SEQ)
        pieces.append(
            remote(w_ref.at[peer], w_mid.at[seq], wsend.at[k - 1], wrecv.at[k - 1], "seq", peer)
        )
    rows = []
    for k in range(1, N_SHARD):
        peer = lax.rem(shard + k, N_SHARD)
        n = 21 + k
        rows.append(
            remote(v_ref, vo_ref.at[shard], wsend.at[n], wrecv.at[n], "shard", peer)
        )
    mine.wait()
    for piece in pieces:
        piece.wait()
    packed = jnp.zeros((16, 128), f32)
    row = lax.broadcasted_iota(jnp.int32, (16, 128), 0)
    for s in range(N_SEQ):
        packed = jnp.where(row == s, w_mid[s, 16:].astype(f32), packed)
        w_pack[s] = w_mid[s, :16]
    w_pack[N_SEQ] = packed.astype(bf16)
    mine = pltpu.make_async_copy(w_pack, wo_ref.at[shard], wown)
    mine.start()
    pieces = []
    for k in range(1, N_SHARD):
        peer = lax.rem(shard + k, N_SHARD)
        n = 6 + k
        pieces.append(
            remote(w_pack, wo_ref.at[shard], wsend.at[n], wrecv.at[n], "shard", peer)
        )
    staged("seq", 8, 4, x_ref, lambda s, low, high: xo_ref.at[s, low:high], send, recv, own)
    slab.wait()
    for row in rows:
        row.wait()
    mine.wait()
    for piece in pieces:
        piece.wait()


def first_gather(x, pieces, rows, ident):
    return pl.pallas_call(
        first_kernel,
        out_shape=[
            jax.ShapeDtypeStruct((N_SEQ, 8, TOK_DEV // 8, WIDTH), bf16),
            jax.ShapeDtypeStruct((N_SHARD, N_SEQ + 1, 16, 128), bf16),
            jax.ShapeDtypeStruct((N_SHARD,) + rows.shape, bf16),
        ],
        in_specs=[ANY, ANY, ANY],
        out_specs=[ANY, ANY, ANY],
        scratch_shapes=[
            pltpu.VMEM(pieces.shape, bf16),
            pltpu.VMEM((N_SEQ + 1, 16, 128), bf16),
            pltpu.SemaphoreType.DMA((12,)),
            pltpu.SemaphoreType.DMA((12,)),
            pltpu.SemaphoreType.DMA,
            pltpu.SemaphoreType.DMA((38,)),
            pltpu.SemaphoreType.DMA((38,)),
            pltpu.SemaphoreType.DMA,
            pltpu.SemaphoreType.DMA,
        ],
        compiler_params=pltpu.CompilerParams(collective_id=ident, has_side_effects=True),
        name="gather_tokens",
    )(x, pieces, rows)


def spread(rows, right):
    zeros = jnp.zeros((TOK_DEV, HEAD), rows.dtype)
    parts = [rows[:, :HEAD], rows[:, HEAD:]]
    if right:
        parts = [jnp.concatenate([zeros, part], axis=1) for part in parts]
    else:
        parts = [jnp.concatenate([part, zeros], axis=1) for part in parts]
    return jnp.concatenate(parts, axis=0)


def admitted(shape, j, first_key):
    key_pos = first_key + lax.broadcasted_iota(jnp.int32, shape, 0)
    query_pos = j * TOK_DEV + (lax.broadcasted_iota(jnp.int32, shape, 1) & (TOK_DEV - 1))
    return query_pos >= key_pos


def transfer(source, target, send, recv, axis, peer):
    return pltpu.make_async_remote_copy(
        src_ref=source,
        dst_ref=target,
        send_sem=send,
        recv_sem=recv,
        device_id={axis: peer},
        device_id_type=MESH,
    )


def everyone(seq, shard):
    return [("seq", lax.rem(seq + k, N_SEQ)) for k in range(1, N_SEQ)] + [
        ("shard", lax.rem(shard + k, N_SHARD)) for k in range(1, N_SHARD)
    ]


def attention_kernel(*refs):
    (x_ref, cols_ref, gain_ref, cos_ref, sin_ref, turn_ref, slab_ref, rows_ref) = refs[:8]
    (own_ref, gain2_ref, pickt_ref, cot_ref) = refs[8:12]
    (q_ref, wide_ref, lse_ref, attp_ref, res_ref) = refs[12:17]
    (norm_ref, mem_ref, rows_out, ow_ref, land_ref, cot_out) = refs[17:23]
    (land, vt, heads, peak_ref, total_ref, acc_ref, att, ow, weights_ref, norm, rows) = refs[23:34]
    (ksend, krecv, gsend, grecv, esend, erecv, fsend, frecv, hsend, hrecv, own, msem) = refs[34:46]
    dsend, drecv = refs[46:]
    seq = lax.axis_index("seq")
    me = lax.axis_index("shard")
    core = lax.rem(me, 2)
    pair = lax.rem(me // 2, 2)
    ring = me // 4
    far = lax.rem(seq, 2)
    partner = seq + 1 - 2 * far

    def at(k, other_pair, other_core):
        p = 1 - pair if other_pair else pair
        c = 1 - core if other_core else core
        return (lax.rem(ring + 4 + k, 4) * 2 + p) * 2 + c

    def message(t, m, block, peer):
        return transfer(
            land.at[t, block], land.at[t, block], ksend.at[t, m], krecv.at[t, m], "shard", peer
        )

    def first(t):
        for k in (1, 2, 3):
            message(t, k - 1, me, at(k, 0, 0)).start()
        message(t, 3, me, at(0, 1, 0)).start()
        message(t, 4, me, at(0, 0, 1)).start()

    def second(t):
        block = at(0, 1, 0)
        message(t, 3, block, block).wait_recv()
        for k in (1, 2, 3):
            message(t, 4 + k, block, at(k, 0, 0)).start()
        message(t, 8, block, at(0, 0, 1)).start()
        for k in (1, 2, 3):
            block = at(-k, 0, 0)
            message(t, k - 1, block, block).wait_recv()
            message(t, 8 + k, block, at(0, 0, 1)).start()

    def third(t):
        for k in (1, 2, 3):
            block = at(-k, 1, 0)
            message(t, 4 + k, block, at(-k, 0, 0)).wait_recv()
            message(t, 11 + k, block, at(0, 0, 1)).start()

    def fourth(t):
        peer = at(0, 0, 1)
        message(t, 4, peer, peer).wait_recv()
        message(t, 8, at(0, 1, 1), peer).wait_recv()
        for k in (1, 2, 3):
            message(t, 8 + k, at(-k, 0, 1), peer).wait_recv()
            message(t, 11 + k, at(-k, 1, 1), peer).wait_recv()

    def to_shard(k):
        peer = lax.rem(me + k, N_SHARD)
        return transfer(
            rows_ref, rows_out.at[me], esend.at[k - 1], erecv.at[k - 1], "shard", peer
        )

    def slab_to_ring(n, k, block, peer):
        source = slab_ref if n == 0 else ow.at[block]
        return transfer(source, ow.at[block], fsend.at[n, k], frecv.at[n, k], "seq", peer)

    def grads_to_expert(k):
        peer = lax.rem(me + k, N_SHARD)
        return transfer(
            cot_ref.at[peer], cot_out.at[me], dsend.at[k - 1], drecv.at[k - 1], "shard", peer
        )

    def to_expert(k):
        peer = lax.rem(me + k, N_SHARD)
        here = pl.ds(pl.multiple_of(peer * 80, 16), 80)
        return transfer(
            rows.at[here], land_ref.at[me], hsend.at[k - 1], hrecv.at[k - 1], "shard", peer
        )

    def to_token(t, source):
        return transfer(
            heads.at[t], att.at[source], gsend.at[t], grecv.at[source], "seq", t
        )

    greet(everyone(seq, me))

    for half in range(2):
        block = cols_ref[...].astype(f32).reshape(N_SHARD, N_SEQ, 2, 8, 128)[:, :, half]
        block = jnp.swapaxes(block, 0, 1).reshape(WIDTH, 128).astype(bf16)
        weights_ref[:, 128 * half : 128 * half + 128] = block
    weights_ref[:, COLS:] = dot(weights_ref[:, :COLS], turn_ref[...], NN).astype(bf16)
    key = lax.broadcasted_iota(jnp.int32, (TOK_DEV, 2 * HEAD), 1) < HEAD

    def project(n, carry):
        here = pl.ds(pl.multiple_of(n * 512, 512), 512)
        x = x_ref[here, :].astype(f32)
        inverse = lax.rsqrt(jnp.mean(x * x, axis=1, keepdims=True) + epsilon)
        normed = (x * inverse * gain_ref[...]).astype(bf16)
        norm[here, :] = normed
        wide = dot(normed, weights_ref[...], NN).reshape(4, TOK_DEV, 2 * COLS)
        for m in range(4):
            t = 4 * n + m
            cosine, sine = cos_ref[t], sin_ref[t]
            query = wide[m, :, :128] * cosine + wide[m, :, 256:384] * sine
            q_ref[t] = query.astype(bf16) * jnp.bfloat16(1.0 / math.sqrt(HEAD))
            cosine, sine = jnp.where(key, cosine, 1.0), jnp.where(key, sine, 0.0)
            memory = wide[m, :, 128:256] * cosine + wide[m, :, 384:] * sine
            land[t, me] = memory.astype(bf16)
        return carry

    lax.fori_loop(0, 2, project, 0)
    norm_own = pltpu.make_async_copy(norm, norm_ref, own.at[3])
    norm_own.start()
    cot_own = pltpu.make_async_copy(cot_ref.at[me], cot_out.at[me], own.at[4])
    cot_own.start()

    def begin(t, carry):
        first(t)
        peak_ref[t] = jnp.full((1, 2 * TOK_DEV), -1e30, f32)
        total_ref[t] = jnp.zeros((1, 2 * TOK_DEV), f32)
        acc_ref[t] = jnp.zeros((HEAD, 2 * TOK_DEV), f32)
        return carry

    lax.fori_loop(0, N_SEQ, begin, 0)
    second(0)
    third(0)
    second(1)
    fourth(0)
    for k in range(1, N_SHARD):
        to_shard(k).start()
    slab_to_ring(0, 0, seq, partner).start()
    for k in (1, 2, 3):
        slab_to_ring(0, k, seq, lax.rem(seq + 2 * k, N_SEQ)).start()
    rows_own = pltpu.make_async_copy(rows_ref, rows_out.at[me], own.at[0])
    rows_own.start()
    slab_own = pltpu.make_async_copy(slab_ref, ow.at[seq], own.at[1])
    slab_own.start()

    def tile(t, i, masked):
        queries = spread(q_ref[i], False)
        scores = dot(land[t].reshape(SUPER, 2 * HEAD), queries, NT)
        if masked:
            scores = jnp.where(admitted(scores.shape, me, 0), scores, -1e30)
        peak = peak_ref[i]
        newest = jnp.maximum(peak, jnp.max(scores, axis=0, keepdims=True))
        weights = jnp.exp(scores - newest)
        shrink = jnp.exp(peak - newest)
        total = total_ref[i] * shrink + jnp.sum(weights, axis=0, keepdims=True)
        acc = acc_ref[i] * shrink + dot(vt[...], weights.astype(bf16), NN)
        return newest, total, acc

    def step(t, carry):
        pltpu.make_async_copy(land.at[t], mem_ref.at[t], msem.at[t]).start()

        for n in range(5):

            @pl.when(t == n)
            def _(n=n):
                for k in range(1, 4):
                    grads_to_expert(3 * n + k).start()

        @pl.when(t == 2)
        def _():
            slab_to_ring(0, 0, partner, partner).wait_recv()
            for k in (1, 2, 3):
                slab_to_ring(1, k, partner, lax.rem(seq + 2 * k, N_SEQ)).start()

        @pl.when(t + 1 < N_SEQ)
        def _():
            third(t + 1)

        @pl.when(t + 2 < N_SEQ)
        def _():
            second(t + 2)

        for n in range(4):
            rows = land[t, 4 * n : 4 * n + 4].reshape(512, 2 * HEAD)
            vt[:, 512 * n : 512 * n + 512] = rows.T[HEAD:]
        newest, total, acc = tile(t, t, True)
        acc = acc / total
        stacked = jnp.concatenate([acc[:, :TOK_DEV], acc[:, TOK_DEV:]], axis=0)
        wide_ref[t] = stacked
        heads[t] = stacked.T.astype(bf16)
        lse_ref[t] = newest + jnp.log(total)

        @pl.when(t != seq)
        def _():
            to_token(t, seq).start()

        def rest(i, inner):
            peak_ref[i], total_ref[i], acc_ref[i] = tile(t, i, False)
            return inner

        lax.fori_loop(t + 1, N_SEQ, rest, 0)

        @pl.when(t + 1 < N_SEQ)
        def _():
            fourth(t + 1)

        return carry

    lax.fori_loop(0, N_SEQ, step, 0)
    slab_own.wait()
    for k in (1, 2, 3):
        for n, block in enumerate((seq, partner)):
            slab_to_ring(n, k, block, lax.rem(seq + 2 * k, N_SEQ)).wait_send()
            source = lax.rem(block + N_SEQ - 2 * k, N_SEQ)
            slab_to_ring(n, k, source, lax.rem(seq + N_SEQ - 2 * k, N_SEQ)).wait_recv()
    slab_to_ring(0, 0, seq, partner).wait_send()
    ow_own = pltpu.make_async_copy(ow, ow_ref, own.at[1])
    ow_own.start()
    att[seq] = heads[seq]
    for k in range(1, N_SEQ):
        source = lax.rem(seq + k, N_SEQ)
        to_token(source, source).wait_recv()

    for s in range(N_SEQ):
        attp_ref[:, 128 * s : 128 * s + 128] = att[s]
    residual = own_ref[...].astype(f32) + dot(
        attp_ref[...], ow[...].reshape(WIDTH, WIDTH), NN
    )
    res_ref[...] = residual
    inverse = lax.rsqrt(jnp.mean(residual * residual, axis=1, keepdims=True) + epsilon)
    normed = (residual * inverse * gain2_ref[...]).astype(bf16)
    for k in range(N_SHARD):
        peer = lax.rem(me + k, N_SHARD)
        here = pl.ds(pl.multiple_of(peer * 80, 16), 80)
        rows[here, :] = dot(pickt_ref[here, :], normed, NN).astype(bf16)
        if k:
            to_expert(k).start()
    here = pl.ds(pl.multiple_of(me * 80, 16), 80)
    mine = pltpu.make_async_copy(rows.at[here], land_ref.at[me], own.at[2])
    mine.start()
    for k in range(1, N_SEQ):
        to_token(lax.rem(seq + k, N_SEQ), seq).wait_send()
    rows_own.wait()
    norm_own.wait()
    ow_own.wait()
    for k in range(1, N_SHARD):
        to_shard(k).wait()
    for k in range(1, N_SHARD):
        grads_to_expert(k).wait()
        to_expert(k).wait()
    mine.wait()
    cot_own.wait()

    def end(t, carry):
        for m in range(15):
            message(t, m, me, me).wait_send()
        pltpu.make_async_copy(land.at[t], mem_ref.at[t], msem.at[t]).wait()
        return carry

    lax.fori_loop(0, N_SEQ, end, 0)


def attention(operands, ident):
    dma = pltpu.SemaphoreType.DMA
    vmem = pl.BlockSpec(memory_space=pltpu.VMEM)
    shards = (N_SHARD - 1,)
    return pl.pallas_call(
        attention_kernel,
        in_specs=[vmem] * 6 + [ANY] * 2 + [vmem] * 3 + [ANY],
        out_specs=[vmem] * 5 + [ANY] * 6,
        out_shape=[
            jax.ShapeDtypeStruct((N_SEQ, TOK_DEV, 2 * HEAD), bf16),
            jax.ShapeDtypeStruct((N_SEQ, 2 * HEAD, TOK_DEV), f32),
            jax.ShapeDtypeStruct((N_SEQ, 1, 2 * TOK_DEV), f32),
            jax.ShapeDtypeStruct((TOK_DEV, WIDTH), bf16),
            jax.ShapeDtypeStruct((TOK_DEV, WIDTH), f32),
            jax.ShapeDtypeStruct((HEAD_ROWS, WIDTH), bf16),
            jax.ShapeDtypeStruct((N_SEQ, N_SHARD, TOK_DEV, 2 * HEAD), bf16),
            jax.ShapeDtypeStruct((N_SHARD, 8, 2 * WIDTH), bf16),
            jax.ShapeDtypeStruct((N_SEQ, 128, WIDTH), bf16),
            jax.ShapeDtypeStruct((N_SHARD, 80, WIDTH), bf16),
            jax.ShapeDtypeStruct((N_SHARD, 80, WIDTH), bf16),
        ],
        scratch_shapes=[
            pltpu.VMEM((N_SEQ, N_SHARD, TOK_DEV, 2 * HEAD), bf16),
            pltpu.VMEM((HEAD, SUPER), bf16),
            pltpu.VMEM((N_SEQ, TOK_DEV, 2 * HEAD), bf16),
            pltpu.VMEM((N_SEQ, 1, 2 * TOK_DEV), f32),
            pltpu.VMEM((N_SEQ, 1, 2 * TOK_DEV), f32),
            pltpu.VMEM((N_SEQ, HEAD, 2 * TOK_DEV), f32),
            pltpu.VMEM((N_SEQ, TOK_DEV, 128), bf16),
            pltpu.VMEM((N_SEQ, 128, WIDTH), bf16),
            pltpu.VMEM((WIDTH, 2 * COLS), bf16),
            pltpu.VMEM((HEAD_ROWS, WIDTH), bf16),
            pltpu.VMEM((N_SHARD * 80, WIDTH), bf16),
            dma((N_SEQ, 15)),
            dma((N_SEQ, 15)),
            dma((N_SEQ,)),
            dma((N_SEQ,)),
            dma(shards),
            dma(shards),
            dma((2, 4)),
            dma((2, 4)),
            dma(shards),
            dma(shards),
            dma((5,)),
            dma((N_SEQ,)),
            dma(shards),
            dma(shards),
        ],
        compiler_params=pltpu.CompilerParams(
            collective_id=ident, has_side_effects=True, vmem_limit_bytes=56 << 20
        ),
        name="attention_forward",
    )(*operands)


def late_kernel(*refs):
    (attp, ow_ref, res_ref, cot_ref, gain_ref, pick_ref, land_ref, gr_ref, w_ref) = refs[:9]
    (q_ref, wide_ref, lse_ref, mem_ref, cos_ref, sin_ref, turn_ref) = refs[9:16]
    (normed_ref, slab_ref, pack_ref, gcol_ref) = refs[16:20]
    (resg_ref, tok_ref, came_ref, sums_ref, qkv_ref, wout_ref, mgain_ref, kz_ref) = refs[20:28]
    qall_ref = refs[28]
    (gu, dn, land, rows, returned, xt, ht, hg, gm, mixed, dw, ags, xstage) = refs[29:42]
    (gl, qs, gs, delta_ref, kt, acc, dq, stage, dl) = refs[42:51]
    (mbuf, pg, qp, qstage, qland, qsum, osum, xland, oland, mstage, mland) = refs[51:62]
    cland, cstage, oseq = refs[62:65]
    (wsem, isend, irecv, ksend, krecv, psend, precv) = refs[65:72]
    (dsend, drecv, osend, orecv, jsend, jrecv, nsend, nrecv, own) = refs[72:81]
    (msem, asend, arecv, bsend, brecv, xsend, xrecv, csend, crecv, tsend, trecv) = refs[81:92]
    (usend, urecv, fsend, frecv) = refs[92:]
    seq = lax.axis_index("seq")
    me = lax.axis_index("shard")
    ring = seq // 2
    far = lax.rem(seq, 2)

    def weights(e, s):
        return (
            pltpu.make_async_copy(
                w_ref.at[e, s, :128], gu.at[e, 128 * s : 128 * s + 128], wsem.at[e, s, 0]
            ),
            pltpu.make_async_copy(
                w_ref.at[e, s, 128:], dn.at[e, 64 * s : 64 * s + 64], wsem.at[e, s, 1]
            ),
        )

    def flat(block, low, high):
        return pl.ds(pl.multiple_of(block * 80 + low, 16), high - low)

    back_pieces = ((0, 32), (32, 80))

    def to_source(part, k, block, source, peer):
        low, high = back_pieces[part]
        return transfer(
            rows.at[flat(block, low, high)],
            returned.at[flat(source, low, high)],
            isend.at[part, k - 1],
            irecv.at[part, k - 1],
            "shard",
            peer,
        )

    def to_token_expert(k):
        peer = lax.rem(me + k, N_SHARD)
        return transfer(
            land.at[peer], came_ref.at[me], jsend.at[k - 1], jrecv.at[k - 1], "shard", peer
        )

    def to_ring(e, k):
        peer = lax.rem(seq + 2 * k, N_SEQ)
        return transfer(
            dw.at[e, k], kz_ref.at[e, k - 1], ksend.at[e, k - 1], krecv.at[e, k - 1], "seq", peer
        )

    def out_to_shard(k, block, source, peer):
        return transfer(
            rows.at[flat(block, 0, 64)], oland.at[source], psend.at[k - 1], precv.at[k - 1], "shard", peer
        )

    def to_head(p):
        return transfer(
            ags.at[p], gl.at[seq], osend.at[p], orecv.at[seq], "seq", p
        )

    def from_head(source):
        return transfer(gl.at[source], gl.at[source], osend.at[0], orecv.at[source], "seq", source)

    core = lax.rem(me, 2)
    chip = me // 2

    def to_core(t):
        return transfer(
            stage.at[lax.rem(t, 4), :, 1 - core],
            cland.at[lax.rem(t, 4)],
            tsend.at[t],
            trecv.at[t],
            "shard",
            me + 1 - 2 * core,
        )

    def to_owner(t, k, block, source, peer):
        return transfer(
            cstage.at[lax.rem(t, 4), block],
            dl.at[t, source],
            dsend.at[t, k - 1],
            drecv.at[t, k - 1],
            "shard",
            peer * 2 + core,
        )

    def to_token(t, source):
        return transfer(pg.at[t], tok_ref.at[source], nsend.at[t], nrecv.at[source], "seq", t)

    def out_to_seq(p):
        return transfer(
            osum.at[p], oseq.at[seq], usend.at[p], urecv.at[seq], "seq", p
        )

    def out_from_seq(source):
        return transfer(
            oseq.at[source], oseq.at[source], usend.at[0], urecv.at[source], "seq", source
        )

    def slab_to_ring(n, k, block, peer):
        source = slab_ref if n == 0 else qall_ref.at[block]
        return transfer(
            source, qall_ref.at[block], fsend.at[n, k], frecv.at[n, k], "seq", peer
        )

    def fetch(t):
        slot = lax.rem(t, 2)
        return pltpu.make_async_copy(mem_ref.at[t], mbuf.at[slot], msem.at[slot])

    def qkv_to_shard(k, block, source, peer):
        return transfer(
            qstage.at[block], qland.at[source], asend.at[k - 1], arecv.at[k - 1], "shard", peer
        )

    def qkv_to_seq(k, block, source, peer):
        return transfer(
            qsum.at[block], qkv_ref.at[source], bsend.at[k - 1], brecv.at[k - 1], "seq", peer
        )

    def gain_to_shard(k, block, source, peer):
        return transfer(
            mstage.at[block], mland.at[source], csend.at[k - 1], crecv.at[k - 1], "shard", peer
        )

    partner = seq + 1 - 2 * far
    to_pair = transfer(xstage, xland, xsend, xrecv, "seq", partner)

    greet(everyone(seq, me))
    for e in range(LOCAL_EXPERTS):
        for s in range(N_SEQ):
            for copy in weights(e, s):
                copy.start()
    slab_to_ring(0, 0, seq, partner).start()
    for k in (1, 2, 3):
        slab_to_ring(0, k, seq, lax.rem(seq + 2 * k, N_SEQ)).start()
    slab_own = pltpu.make_async_copy(slab_ref, qall_ref.at[seq], own.at[3])
    slab_own.start()

    land_copy = pltpu.make_async_copy(land_ref, land, own.at[4])
    land_copy.start()

    def split(block, e):
        return (
            block.astype(f32)
            .reshape(N_SHARD, LOCAL_EXPERTS, 8, WIDTH)[:, e]
            .reshape(128, WIDTH)
            .astype(bf16)
        )

    def join(first, second):
        halves = [half.astype(f32).reshape(N_SHARD, 1, 8, WIDTH) for half in (first, second)]
        return jnp.concatenate(halves, axis=1).reshape(N_SHARD, 16, WIDTH).astype(bf16)

    def expert(e, x, g, here):
        pre = dot(x, gu[e], NN)
        gate, up = pre[:, :FF], pre[:, FF:]
        sigmoid = jax.nn.sigmoid(gate)
        act = gate * sigmoid
        hidden = (act * up).astype(bf16)
        units = dot(g, dn[e], NT)
        gate_grad = (units * up * sigmoid * (1.0 + gate * (1.0 - sigmoid))).astype(bf16)
        up_grad = (units * act).astype(bf16)
        both = jnp.concatenate([gate_grad, up_grad], axis=1)
        hg[e, here, :] = both
        xt[e, :, here] = x.T
        ht[e, :, here] = hidden.T
        return dot(hidden, dn[e], NN).astype(bf16), dot(both, gu[e], NT).astype(bf16)

    def run_expert(e, low):
        def aligned(n, carry):
            group = pl.ds(n * 8, 8)
            here = pl.ds(pl.multiple_of(n * 256, 256), 256)
            x = land[group, low : low + 32].reshape(256, WIDTH)
            g = gr_ref[group, low : low + 32].reshape(256, WIDTH)
            out, back = expert(e, x, g, here)
            land[group, low : low + 32] = out.reshape(8, 32, WIDTH)
            for m in range(8):
                rows[flat(n * 8 + m, low, low + 32), :] = back[32 * m : 32 * m + 32]
            return carry

        lax.fori_loop(0, 2, aligned, 0)
        g = split(gr_ref[:, 32:48], e)
        gm[e] = g
        out, back = expert(e, split(land[:, 32:48], e), g, slice(512, 640))
        mixed[0, e] = out
        mixed[1, e] = back

    def expert_grads(e):
        low = 48 * e

        def block(h, carry):
            features = pl.ds(pl.multiple_of(h * 512, 512), 512)
            units = pl.ds(pl.multiple_of(h * 256, 256), 256)
            grad = dot(xt[e, features, :], hg[e], NN).astype(bf16)
            part = dot(ht[e, units, :512], gr_ref[:, low : low + 32].reshape(512, WIDTH), NN)
            part = (part + dot(ht[e, units, 512:], gm[e], NN)).astype(bf16)
            for m in range(4):
                k = lax.rem(2 * h + m // 2 + 4 - ring, 4)
                n = lax.rem(m + far, 2)
                dw[e, k, n, :128, :] = grad[128 * m : 128 * m + 128]
                dw[e, k, n, 128:, :] = part[64 * m : 64 * m + 64]
            return carry

        lax.fori_loop(0, 2, block, 0)

    for e in range(LOCAL_EXPERTS):
        for s in range(N_SEQ):
            for copy in weights(e, s):
                copy.wait()
    land_copy.wait()
    run_expert(0, 0)
    for k in range(1, N_SHARD):
        peer = lax.rem(me + k, N_SHARD)
        to_source(0, k, peer, me, peer).start()
    slab_to_ring(0, 0, partner, partner).wait_recv()
    for k in (1, 2, 3):
        slab_to_ring(1, k, partner, lax.rem(seq + 2 * k, N_SEQ)).start()
    run_expert(1, 48)
    land[:, 32:48] = join(mixed[0, 0], mixed[0, 1])
    joined = join(mixed[1, 0], mixed[1, 1])
    for n in range(N_SHARD):
        rows[80 * n + 32 : 80 * n + 48, :] = joined[n]
    for k in range(1, N_SHARD):
        peer = lax.rem(me + k, N_SHARD)
        to_source(1, k, peer, me, peer).start()
    returned[flat(me, 0, 80), :] = rows[flat(me, 0, 80), :]
    normed_copy = pltpu.make_async_copy(normed_ref, gu.at[0], own.at[4])
    normed_copy.start()
    ow_copy = pltpu.make_async_copy(ow_ref, gu.at[1], own.at[0])
    ow_copy.start()
    expert_grads(0)
    for k in (1, 3):
        to_ring(0, k).start()
    expert_grads(1)

    for part in range(2):
        for k in range(1, N_SHARD):
            source = lax.rem(me + N_SHARD - k, N_SHARD)
            to_source(part, k, source, source, source).wait_recv()
    moe_in_grad = dot(pick_ref[...], returned[...], NN)
    residual = res_ref[...]
    inverse = lax.rsqrt(jnp.mean(residual * residual, axis=1, keepdims=True) + epsilon)
    scaled = moe_in_grad * gain_ref[...]
    moe_part = inverse * scaled - residual * (inverse * inverse * inverse) * jnp.mean(
        residual * scaled, axis=1, keepdims=True
    )
    residual_grad = cot_ref[...].astype(f32) + moe_part
    resg_ref[...] = residual_grad
    branch = residual_grad.astype(bf16)
    ow_copy.wait()
    attended_grad = dot(branch, gu[1], NT).astype(bf16)
    for p in range(N_SEQ):
        ags[p] = attended_grad[:, 128 * p : 128 * p + 128]

        @pl.when(seq != p)
        def _(p=p):
            to_head(p).start()

    gl[seq] = ags[seq]
    for part in range(2):
        for k in range(1, N_SHARD):
            peer = lax.rem(me + k, N_SHARD)
            to_source(part, k, peer, me, peer).wait_send()
    for k in range(4):
        block = dot(attp[:, 256 * k : 256 * k + 256].T, branch, NN).reshape(2, N_SHARD, 8, WIDTH)
        for j in range(N_SHARD):
            rows[80 * j + 16 * k : 80 * j + 16 * k + 16, :] = jnp.concatenate(
                [block[0, j], block[1, j]], axis=0
            ).astype(bf16)
    for k in range(1, N_SEQ):
        from_head(lax.rem(seq + k, N_SEQ)).wait_recv()
    for k in (1, 3, 2):
        to_ring(1, k).start()
    to_ring(0, 2).start()
    for k in range(1, N_SHARD):
        peer = lax.rem(me + k, N_SHARD)
        out_to_shard(k, peer, me, peer).start()
    oland[me] = rows[flat(me, 0, 64), :]
    came_own = pltpu.make_async_copy(land.at[me], came_ref.at[me], own.at[0])
    came_own.start()
    fetch(0).start()
    normed_copy.wait()
    qp[...] = jnp.zeros((WIDTH, COLS), f32)

    def begin(i, carry):
        qs[i] = spread(q_ref[i], False)
        gs[i] = spread(gl[i], True)
        product = wide_ref[i] * gl[i].astype(f32).T
        delta_ref[i] = jnp.concatenate(
            [
                jnp.sum(product[:HEAD], axis=0, keepdims=True),
                jnp.sum(product[HEAD:], axis=0, keepdims=True),
            ],
            axis=1,
        )
        dq[i] = jnp.zeros((HEAD, 2 * TOK_DEV), f32)
        return carry

    lax.fori_loop(0, N_SEQ, begin, 0)

    def tile(t, i, n, masked):
        here = slice(n * BWD_TILE, (n + 1) * BWD_TILE)
        memory = mbuf[lax.rem(t, 2), 8 * n : 8 * n + 8].reshape(BWD_TILE, 2 * HEAD)
        scores = dot(memory, qs[i], NT)
        weight = jnp.exp(scores - lse_ref[i])
        if masked:
            weight = jnp.where(admitted(scores.shape, me, n * BWD_TILE), weight, 0.0)
        weight_grad = dot(memory, gs[i], NT)
        score_grad = (weight * (weight_grad - delta_ref[i])).astype(bf16)
        here_grad = dot(weight.astype(bf16), gs[i], NN) + dot(score_grad, qs[i], NN)
        if masked:
            acc[here, :] = here_grad
        else:
            acc[here, :] += here_grad
        dq[i] += dot(kt[:, here], score_grad, NN)

    def turned(grad, n, t):
        cosine, sine = cos_ref[t], sin_ref[t]
        if n:
            key = lax.broadcasted_iota(jnp.int32, cosine.shape, 1) < HEAD
            cosine = jnp.where(key, cosine, 1.0)
            sine = jnp.where(key, sine, 0.0)
        other = dot(grad, turn_ref[n], NT)
        return (grad.astype(f32) * cosine + other * sine).astype(bf16)

    def chip_sum(t):
        slot = lax.rem(t, 4)

        @pl.when(t >= 4)
        def _():
            for k in range(1, N_SHARD // 2):
                peer = lax.rem(chip + k, N_SHARD // 2)
                to_owner(t - 4, k, peer, chip, peer).wait_send()

        to_core(t).wait_recv()
        total = stage[slot, :, core].astype(f32) + cland[slot].astype(f32)
        cstage[slot] = total.astype(bf16)
        dl[t, chip] = cstage[slot, chip]
        for k in range(1, N_SHARD // 2):
            peer = lax.rem(chip + k, N_SHARD // 2)
            to_owner(t, k, peer, chip, peer).start()

    def token_gradient(t):
        for k in range(1, N_SHARD // 2):
            source = lax.rem(chip + N_SHARD // 2 - k, N_SHARD // 2)
            to_owner(t, k, source, source, source).wait_recv()
        grad = jnp.sum(dl[t].astype(f32), axis=0).astype(bf16)
        pg[t, :, 2 * HEAD :] = turned(grad, 1, t)
        grad = pg[t]

        @pl.when(t != seq)
        def _():
            to_token(t, seq).start()

        tokens = pl.ds(pl.multiple_of(t * 128, 128), 128)
        qp[...] += dot(gu[0, tokens, :].T, grad, NN)

    def sum_weights():
        for k in range(1, N_SHARD):
            peer = lax.rem(me + k, N_SHARD)
            out_to_shard(k, peer, me, peer).wait_send()
        for e in range(LOCAL_EXPERTS):
            for k in (1, 2, 3):
                to_ring(e, k).wait()
        back = []
        for e, buffer in enumerate((rows, returned)):
            for k in range(3):
                for n in range(2):
                    index = 2 * k + n
                    back.append(
                        pltpu.make_async_copy(
                            kz_ref.at[e, k, n],
                            buffer.at[192 * index : 192 * index + 192],
                            wsem.at[e, index, 0],
                        )
                    )
                    back[-1].start()
        for copy in back:
            copy.wait()
        for e, buffer in enumerate((rows, returned)):
            for n in range(2):
                total = dw[e, 0, n].astype(f32)
                for k in range(3):
                    index = 2 * k + n
                    total += buffer[192 * index : 192 * index + 192, :].astype(f32)
                if n == 0:
                    sums_ref[e] = total
                else:
                    xstage[e] = total.astype(bf16)
        to_pair.start()
        for k in range(1, N_SHARD):
            source = lax.rem(me + N_SHARD - k, N_SHARD)
            out_to_shard(k, source, source, source).wait_recv()
        osum[...] = jnp.sum(oland[...].astype(f32), axis=0).reshape(N_SEQ, 8, WIDTH)
        for p in range(N_SEQ):

            @pl.when(seq != p)
            def _(p=p):
                out_to_seq(p).start()

        oseq[seq] = osum[seq]

    def step(t, carry):
        fetch(t).wait()

        @pl.when(t + 1 < N_SEQ)
        def _():
            fetch(t + 1).start()

        @pl.when(t >= 1)
        def _():
            chip_sum(t - 1)

        @pl.when(t >= 3)
        def _():
            token_gradient(t - 3)

        for n in range(5):

            @pl.when(t == n + 1)
            def _(n=n):
                for k in range(1, 4):
                    to_token_expert(3 * n + k).start()

        @pl.when(t == N_SEQ - 2)
        def _():
            sum_weights()

        for n in range(4):
            block = mbuf[lax.rem(t, 2), 4 * n : 4 * n + 4].reshape(512, 2 * HEAD)
            kt[:, 512 * n : 512 * n + 512] = block.T[:HEAD]
        tile(t, t, 0, True)
        tile(t, t, 1, True)
        grad = dq[t] * (1.0 / math.sqrt(HEAD))
        grad = jnp.concatenate([grad[:, :TOK_DEV], grad[:, TOK_DEV:]], axis=0).T.astype(bf16)
        pg[t, :, : 2 * HEAD] = turned(grad, 0, t)

        def rest(i, inner):
            tile(t, i, 0, False)
            tile(t, i, 1, False)
            return inner

        lax.fori_loop(t + 1, N_SEQ, rest, 0)

        @pl.when(t >= 4)
        def _():
            to_core(t - 4).wait_send()

        slot = lax.rem(t, 4)
        for n in range(4):
            block = acc[512 * n : 512 * n + 512, :].astype(bf16)
            stage[slot, 2 * n : 2 * n + 2] = block.reshape(2, 2, TOK_DEV, 2 * HEAD)
        to_core(t).start()
        return carry

    lax.fori_loop(0, N_SEQ, step, 0)

    chip_sum(N_SEQ - 1)
    for t in (3, 2, 1):
        token_gradient(N_SEQ - t)
    own_token = pltpu.make_async_copy(pg.at[seq], tok_ref.at[seq], own.at[1])
    own_token.start()
    split_rows = qp[...].reshape(N_SEQ, N_SHARD, 8, COLS)
    for j in range(N_SHARD):
        qstage[j] = split_rows[:, j].reshape(64, COLS).astype(bf16)
    for k in range(1, N_SHARD):
        peer = lax.rem(me + k, N_SHARD)
        qkv_to_shard(k, peer, me, peer).start()
    qland[me] = qstage[me]
    for k in range(1, N_SHARD):
        source = lax.rem(me + N_SHARD - k, N_SHARD)
        qkv_to_shard(k, source, source, source).wait_recv()
    qsum[...] = jnp.sum(qland[...].astype(f32), axis=0).reshape(N_SEQ, 8, COLS)
    for k in range(1, N_SEQ):
        peer = lax.rem(seq + k, N_SEQ)
        qkv_to_seq(k, peer, seq, peer).start()
    own_qkv = pltpu.make_async_copy(qsum.at[seq], qkv_ref.at[seq], own.at[2])
    own_qkv.start()

    to_pair.wait()
    gain = jnp.zeros((128, 128), f32)
    for e in range(LOCAL_EXPERTS):
        sums_ref[e] += xland[e].astype(f32)
        product = pack_ref[e, :128].astype(f32) * sums_ref[e, :128]
        for c in range(8):
            gain += product[:, 128 * c : 128 * c + 128]
    gain = jnp.sum(gain, axis=1, keepdims=True) / gcol_ref[...]
    mstage[...] = gain.reshape(N_SHARD, 8, 128)
    for k in range(1, N_SHARD):
        peer = lax.rem(me + k, N_SHARD)
        gain_to_shard(k, peer, me, peer).start()
    mland[me] = mstage[me]
    for k in range(1, N_SEQ):
        out_from_seq(lax.rem(seq + k, N_SEQ)).wait_recv()
    wout_ref[...] = jnp.sum(oseq[...], axis=0)
    for k in range(1, N_SHARD):
        source = lax.rem(me + N_SHARD - k, N_SHARD)
        gain_to_shard(k, source, source, source).wait_recv()
    mgain_ref[...] = jnp.sum(mland[...], axis=0)

    for p in range(N_SEQ):

        @pl.when(seq != p)
        def _(p=p):
            to_head(p).wait_send()
            out_to_seq(p).wait_send()

    for k in range(1, N_SHARD):
        to_token_expert(k).wait()
        peer = lax.rem(me + k, N_SHARD)
        qkv_to_shard(k, peer, me, peer).wait_send()
        gain_to_shard(k, peer, me, peer).wait_send()

    def end(t, carry):
        for k in range(1, N_SHARD // 2):
            peer = lax.rem(chip + k, N_SHARD // 2)
            to_owner(t, k, peer, chip, peer).wait_send()
        to_core(t).wait_send()
        return carry

    lax.fori_loop(4, N_SEQ, end, 0)
    for k in range(1, N_SEQ):
        peer = lax.rem(seq + k, N_SEQ)
        to_token(peer, seq).wait_send()
        to_token(peer, peer).wait_recv()
        qkv_to_seq(k, peer, seq, peer).wait_send()
        source = lax.rem(seq + N_SEQ - k, N_SEQ)
        qkv_to_seq(k, source, source, source).wait_recv()
    slab_to_ring(0, 0, seq, partner).wait_send()
    for k in (1, 2, 3):
        for n, block in enumerate((seq, partner)):
            slab_to_ring(n, k, block, lax.rem(seq + 2 * k, N_SEQ)).wait_send()
            source = lax.rem(block + N_SEQ - 2 * k, N_SEQ)
            slab_to_ring(n, k, source, lax.rem(seq + N_SEQ - 2 * k, N_SEQ)).wait_recv()
    for copy in (own_token, own_qkv, came_own, slab_own):
        copy.wait()


def late(operands, ident):
    dma = pltpu.SemaphoreType.DMA
    vmem = pl.BlockSpec(memory_space=pltpu.VMEM)
    wide = jax.ShapeDtypeStruct((TOK_DEV, WIDTH), f32)
    routed = (N_SHARD, 80, WIDTH)
    grads = (LOCAL_EXPERTS, 2, 192, WIDTH)
    shapes = [
        ((LOCAL_EXPERTS, WIDTH, 2 * FF), bf16),
        ((LOCAL_EXPERTS, FF, WIDTH), bf16),
        (routed, bf16),
        ((N_SHARD * 80, WIDTH), bf16),
        ((N_SHARD * 80, WIDTH), bf16),
        ((LOCAL_EXPERTS, WIDTH, EXPERT_ROWS), bf16),
        ((LOCAL_EXPERTS, FF, EXPERT_ROWS), bf16),
        ((LOCAL_EXPERTS, EXPERT_ROWS, 2 * FF), bf16),
        ((LOCAL_EXPERTS, 128, WIDTH), bf16),
        ((2, LOCAL_EXPERTS, 128, WIDTH), bf16),
        ((LOCAL_EXPERTS, 4, 2, 192, WIDTH), bf16),
        ((N_SEQ, TOK_DEV, 128), bf16),
        ((LOCAL_EXPERTS, 192, WIDTH), bf16),
        ((N_SEQ, TOK_DEV, 2 * HEAD), bf16),
        ((N_SEQ, 2 * TOK_DEV, 2 * HEAD), bf16),
        ((N_SEQ, 2 * TOK_DEV, 2 * HEAD), bf16),
        ((N_SEQ, 1, 2 * TOK_DEV), f32),
        ((HEAD, SUPER), bf16),
        ((SUPER, 2 * HEAD), f32),
        ((N_SEQ, HEAD, 2 * TOK_DEV), f32),
        ((4, N_SHARD // 2, 2, TOK_DEV, 2 * HEAD), bf16),
        ((N_SEQ, N_SHARD // 2, TOK_DEV, 2 * HEAD), bf16),
        ((2, N_SHARD, TOK_DEV, 2 * HEAD), bf16),
        ((N_SEQ, TOK_DEV, COLS), bf16),
        ((WIDTH, COLS), f32),
        ((N_SHARD, 64, COLS), bf16),
        ((N_SHARD, 64, COLS), bf16),
        ((N_SEQ, 8, COLS), f32),
        ((N_SEQ, 8, WIDTH), f32),
        ((LOCAL_EXPERTS, 192, WIDTH), bf16),
        ((N_SHARD, 64, WIDTH), bf16),
        ((N_SHARD, 8, 128), f32),
        ((N_SHARD, 8, 128), f32),
        ((4, N_SHARD // 2, TOK_DEV, 2 * HEAD), bf16),
        ((4, N_SHARD // 2, TOK_DEV, 2 * HEAD), bf16),
        ((N_SEQ, 8, WIDTH), f32),
    ]
    shards = (N_SHARD - 1,)
    counts = [(LOCAL_EXPERTS, N_SEQ, 2)]
    counts += [(2,) + shards] * 2
    counts += [(LOCAL_EXPERTS, 3)] * 2 + [shards] * 2
    counts += [(N_SEQ, N_SHARD // 2 - 1)] * 2 + [(N_SEQ,)] * 2 + [shards] * 2 + [(N_SEQ,)] * 2
    counts += [(5,), (2,)] + [shards] * 2 + [(N_SEQ - 1,)] * 2
    semaphores = [dma(count) for count in counts] + [dma, dma]
    semaphores += [dma(shards)] * 2 + [dma((N_SEQ,))] * 4 + [dma((2, 4))] * 2
    return pl.pallas_call(
        late_kernel,
        in_specs=[vmem, ANY] + [vmem] * 4 + [ANY, vmem, ANY] + [vmem] * 3 + [ANY] + [vmem] * 3 + [ANY] * 2 + [vmem] * 2,
        out_specs=[vmem, ANY, ANY, vmem, ANY, vmem, vmem, ANY, ANY],
        out_shape=[
            wide,
            jax.ShapeDtypeStruct((N_SEQ, TOK_DEV, COLS), bf16),
            jax.ShapeDtypeStruct(routed, bf16),
            jax.ShapeDtypeStruct((LOCAL_EXPERTS, 192, WIDTH), f32),
            jax.ShapeDtypeStruct((N_SEQ, 8, COLS), f32),
            jax.ShapeDtypeStruct((8, WIDTH), f32),
            jax.ShapeDtypeStruct((8, 128), f32),
            jax.ShapeDtypeStruct((LOCAL_EXPERTS, 3, 2, 192, WIDTH), bf16),
            jax.ShapeDtypeStruct((N_SEQ, 128, 2 * WIDTH), bf16),
        ],
        scratch_shapes=[pltpu.VMEM(*shape) for shape in shapes] + semaphores,
        compiler_params=pltpu.CompilerParams(
            collective_id=ident, has_side_effects=True, vmem_limit_bytes=LIMIT << 20
        ),
        name="experts_attention_backward",
    )(*operands)


def group_columns(rows):
    lead = rows.shape[:-1]
    queries = rows[..., : HEADS * HEAD].reshape(lead + (N_SEQ, 2 * HEAD))
    keys = rows[..., HEADS * HEAD : (HEADS + KV) * HEAD].reshape(lead + (N_SEQ, HEAD))
    values = rows[..., (HEADS + KV) * HEAD :].reshape(lead + (N_SEQ, HEAD))
    return jnp.concatenate([queries, keys, values], axis=-1)


def ungroup_columns(groups):
    rows = groups.shape[0]
    return jnp.concatenate(
        [
            groups[:, :, : 2 * HEAD].reshape(rows, HEADS * HEAD),
            groups[:, :, 2 * HEAD : 3 * HEAD].reshape(rows, KV * HEAD),
            groups[:, :, 3 * HEAD :].reshape(rows, KV * HEAD),
        ],
        axis=1,
    )


def rope_pair(shard):
    half = HEAD // 2
    frequency = jnp.exp(
        jnp.arange(half, dtype=f32) * jnp.float32(-2.0 * math.log(rope_base) / HEAD)
    )
    chunk = jnp.arange(N_SEQ, dtype=jnp.int32)[:, None] * N_SHARD + shard
    position = chunk * TOK_DEV + jnp.arange(TOK_DEV, dtype=jnp.int32)[None, :]
    angles = position[:, :, None].astype(f32) * frequency[None, None, :]
    cosine, sine = lax.optimization_barrier((jnp.cos(angles), jnp.sin(angles)))
    return jnp.tile(cosine, (1, 1, 4)), jnp.tile(sine, (1, 1, 4))


def turn_matrix():
    row = jnp.arange(COLS, dtype=jnp.int32)[:, None]
    col = jnp.arange(COLS, dtype=jnp.int32)[None, :]
    half = HEAD // 2
    low = col % HEAD < half
    minus = low & (row == col + half) & (col < 3 * HEAD)
    plus = (~low) & (row == col - half) & (col < 3 * HEAD)
    return (plus.astype(f32) - minus.astype(f32)).astype(bf16)


def routing(routes, route_weights):
    ids = jnp.arange(EXPERTS, dtype=jnp.int32)
    hit = routes[:, :, None] == ids[None, None, :]
    mask = jnp.sum(hit.astype(f32), axis=1)
    weight = jnp.sum(jnp.where(hit, route_weights[:, :, None], 0.0), axis=1)
    token = jnp.arange(TOK_DEV, dtype=jnp.int32)
    earlier = (token[:, None] > token[None, :]).astype(bf16)
    before = dot(earlier, mask.astype(bf16), NN)
    code = jnp.where(mask > 0.0, before, -1.0).astype(bf16)
    place = jnp.arange(N_SHARD * 80, dtype=jnp.int32)
    row = place % 80
    slot = jnp.where(row < 40, row, jnp.where(row < 48, row - 8, row - 48))
    owner = place // 80 * LOCAL_EXPERTS + (row >= 40).astype(jnp.int32)
    widen = (owner[None, :] == ids[:, None]).astype(bf16)
    pick = dot(code, widen, NN) == slot.astype(f32)[None, :]
    high = weight.astype(bf16)
    low = (weight - high.astype(f32)).astype(bf16)
    high = jnp.where(pick, dot(high, widen, NN), 0.0)
    low = jnp.where(pick, dot(low, widen, NN), 0.0)
    return pick.astype(bf16), high.astype(bf16), low.astype(bf16), jnp.sum(high + low, axis=0)


def on_device(
    layer_input,
    attn_gain,
    moe_gain,
    w_qkv,
    w_out,
    w_gate,
    w_up,
    w_down,
    routes,
    route_weights,
    cotangent,
):
    seq = lax.axis_index("seq")
    shard = lax.axis_index("shard")

    pick, scale_high, scale_low, slot_scale = routing(routes, route_weights)
    pick_turned = pick.T
    grad_send = (slot_scale[:, None] * dot(pick_turned, cotangent, NN)).astype(bf16)

    grouped = group_columns(w_qkv)
    pieces = grouped.reshape(8, N_SEQ, 2, 128).transpose(1, 2, 0, 3)
    gains = jnp.concatenate([attn_gain, moe_gain, jnp.zeros((112,), bf16)])
    gains = jnp.broadcast_to(gains[None, None, :], (N_SEQ, 16, 128))
    pieces = jnp.concatenate([pieces.reshape(N_SEQ, 16, 128), gains], axis=1)
    tokens, columns, out_slabs = first_gather(
        layer_input.reshape(8, TOK_DEV // 8, WIDTH), pieces, w_out, 1
    )
    expert_pack = jnp.concatenate(
        [jnp.concatenate([w_gate, w_up], axis=2), w_down], axis=1
    )
    expert_weights = lax.all_gather(
        lax.optimization_barrier((expert_pack, tokens))[0], "seq", axis=1
    )
    gain_rows = columns[:, N_SEQ, :8, :16].transpose(1, 0, 2)
    gain_attn = gain_rows[:, :, :8].reshape(WIDTH).astype(f32)
    gain_moe = gain_rows[:, :, 8:].reshape(WIDTH).astype(f32)
    cosine, sine = rope_pair(shard)
    turn = turn_matrix()
    (
        queries,
        attended_wide,
        lse,
        attended,
        residual,
        normed,
        memory,
        qkv_slab,
        out_weight,
        expert_rows,
        grad_rows,
    ) = attention(
        (
            tokens.reshape(HEAD_ROWS, WIDTH),
            columns[:, :N_SEQ],
            gain_attn[None, :],
            cosine,
            sine,
            turn,
            out_slabs.reshape(128, WIDTH),
            grouped.reshape(8, 2 * WIDTH),
            layer_input,
            gain_moe[None, :],
            pick_turned,
            grad_send.reshape(N_SHARD, 80, WIDTH),
        ),
        2,
    )
    left = jnp.arange(2 * HEAD, dtype=jnp.int32) < HEAD
    turns = turn[:128, :128]
    turns = jnp.stack([turns, jnp.where(left[:, None] & left[None, :], turns, 0)])
    gain_here = lax.dynamic_slice_in_dim(gain_moe, seq * 128, 128)
    (
        residual_grad,
        token_grad,
        came_back,
        expert_sums,
        qkv_groups,
        out_weight_grad,
        moe_gain_grad,
        _,
        qkv_all,
    ) = late(
        (
            attended,
            out_weight.reshape(WIDTH, WIDTH),
            residual,
            cotangent,
            gain_moe[None, :],
            pick,
            expert_rows,
            grad_rows,
            expert_weights,
            queries,
            attended_wide,
            lse,
            memory,
            cosine,
            sine,
            turns,
            normed,
            qkv_slab.reshape(128, 2 * WIDTH),
            expert_pack,
            jnp.broadcast_to(gain_here[:, None], (128, 128)),
        ),
        3,
    )
    came_back = came_back.reshape(N_SHARD * 80, WIDTH)
    x_wide = layer_input.astype(f32)
    moe_sum = dot(scale_high, came_back, NN) + dot(scale_low, came_back, NN)
    block_out = (residual + moe_sum).astype(bf16)

    qkv_groups = qkv_groups.transpose(1, 0, 2)
    attn_gain_grad = jnp.sum(grouped.astype(f32) * qkv_groups, axis=(1, 2)) / attn_gain.astype(f32)
    qkv_weight_grad = ungroup_columns(qkv_groups)

    token_grad = token_grad.transpose(1, 0, 2).reshape(TOK_DEV, 2 * WIDTH)
    normed_grad = dot(token_grad, qkv_all.reshape(WIDTH, 2 * WIDTH), NT)
    inverse_one = lax.rsqrt(jnp.mean(x_wide * x_wide, axis=1, keepdims=True) + epsilon)
    scaled = normed_grad * gain_attn
    attn_part = inverse_one * scaled - x_wide * inverse_one**3 * jnp.mean(
        x_wide * scaled, axis=1, keepdims=True
    )
    input_grad = (residual_grad + attn_part).astype(bf16)
    return (
        block_out,
        input_grad,
        attn_gain_grad,
        moe_gain_grad[:, 0],
        qkv_weight_grad,
        out_weight_grad,
        expert_sums[:, :128, :FF],
        expert_sums[:, :128, FF:],
        expert_sums[:, 128:],
    )


def solution(mesh):
    token = P(("seq", "shard"), None)
    vector = P(("seq", "shard"))
    expert = P("shard", "seq", None)
    return jax.shard_map(
        on_device,
        mesh=mesh,
        in_specs=(
            token,
            vector,
            vector,
            token,
            token,
            expert,
            expert,
            expert,
            token,
            token,
            token,
        ),
        out_specs=(token, token, vector, vector, token, token, expert, expert, expert),
        check_vma=False,
    )
```

time: 471 us -> 429 us (0.911); the launches traced: 465 us -> 428 us
  waiting for transfers between devices: 26 us -> 0.02 us
  Pallas kernels: 352 us -> 372 us
  starting transfers between devices: 9.44 us -> 0.04 us
  local copies, waits for them, and re-layouts: 29.4 us -> 20.1 us
  other arithmetic: 17.6 us -> 11.4 us
    pallas_call x3 -> x2, Pallas kernels: 308 us -> 335 us  [the longest x1 201 us: late(): pl.pallas_call(late_kernel, in_specs=[vmem, ANY] + [vmem] * 4 + [ANY, vme...]
    ppermute x1 -> x0, waiting for transfers between devices: 20.9 us -> none  [on_device(): other = lax.ppermute(other, 'seq', along_x).astype(f32)]
    unnamed x73 -> x33, local copies, waits for them, and re-layouts: 10.1 us -> 0.69 us
    pallas_call x1, Pallas kernels: 44 us -> 36.1 us  [first_gather(): pl.pallas_call(first_kernel, out_shape=[jax.ShapeDtypeStruct((N_SEQ, 8, T...]
    all_to_all x1 -> x0, starting transfers between devices: 7.82 us -> none  [on_device(): qkv_groups = lax.all_to_all(sums[:64].reshape(N_SEQ, 8, COLS), 'seq', 0, 0)]
    all_to_all x1 -> x0, waiting for transfers between devices: 5 us -> none  [on_device(): qkv_groups = lax.all_to_all(sums[:64].reshape(N_SEQ, 8, COLS), 'seq', 0, 0)]
    reduce_sum x5 -> x0, other arithmetic: 4.93 us -> none  [the longest x1 1.82 us: on_device(): out_sums = out_own.astype(f32) + jnp.sum(out_sent.astype(f32), axis=0)]
    dot_general x10 -> x7, matrix products: 14.8 us -> 10.7 us  [dot(): return lax.dot_general(left, right, dims, preferred_element_type=f32)]
  transfers between devices with their start and end apart: 4 -> 1, of which waited for: 2 -> 0; matrix products, arithmetic and copies ran while one was open for 7% -> 4% of each run, Pallas kernels for 63% -> 31%
where the time goes in v4:
time: 429 us; the launch traced here: 428 us
  Pallas kernels  372 us (87%)
  local copies, waits for them, and re-layouts  20.1 us (5%)
  between operations  14.4 us (3%)
  other arithmetic  11.4 us (3%)
  matrix products  10.7 us (2%)
    pallas_call x1, Pallas kernels, late(): pl.pallas_call(late_kernel, in_specs=[vmem, ANY] + [vmem] * 4 + [ANY, vme...  201 us
    pallas_call x1, Pallas kernels, attention(): pl.pallas_call(attention_kernel, in_specs=[vmem] * 6 + [ANY] * 2 + [vmem]...  135 us
    pallas_call x1, Pallas kernels, first_gather(): pl.pallas_call(first_kernel, out_shape=[jax.ShapeDtypeStruct((N_SEQ, 8, T...  36.1 us
    dot_general x7, matrix products, dot(): return lax.dot_general(left, right, dims, preferred_element_type=f32)  10.7 us
  transfers between devices with their start and end apart: 1, of which 0 were waited for; matrix products, arithmetic and copies ran while one was open for 4% of the time, Pallas kernels for 31%

profile of v4, /device:TPU:1, one launch (start us, length us, event | category | flops | bytes accessed | tf_op | source)
XLA Modules:
  0.0 428.1 jit_solution(8467520010721427775)
XLA Ops:
  7.2 0.7 slice_bitcast_fusion.3
  7.9 0.7 fusion.49
  8.7 0.1 reshape.245
  8.8 0.1 reshape.246
  8.9 0.8 pad_maximum_fusion.5
  9.6 0.1 fusion.57
  9.7 0.6 pad_maximum_fusion.1.w_ref
  10.4 2.1 pad_maximum_fusion.refs_18_
  12.5 36.1 %gather_tokens.1 = (bf16[8,8,16,1024]{3,2,1,0:T(8,128)(2,1)}, bf16[16,9,16,128]{3,2,1,0:T(8,128)(2,1)}, bf16[16,8,1024]{2,1,0:T(8,128)(2,1)}) custom-call(bf16[8,16,1024]{2,1,0:T(8,128)(2,1)} %bitcast.48, bf16[8,32,128]{2,1,0:T(8,128)(2,1)} %pad_maximum_fusion.1.w_ref, bf16[8,1024]{1,0:T(8,128)(2,1)} %v_ref.1), custom_call_target="tpu_custom_call" | custom-call | tf_op jit(solution)/shard_map/gather_tokens/pallas_call | solution.py:181
  48.6 1.9 slice.50.refs_1_
  50.5 0.8 slice_bitcast_fusion.1
  51.3 0.1 slice_convert_fusion
  51.4 0.7 reshape.262.refs_9_.refs_4_
  52.0 0.1 reshape.263
  52.2 0.7 reshape.264
  52.8 0.7 reshape.261.refs_2_
  53.6 0.5 multiply_sine_fusion
  54.2 1.0 copy.59.refs_3_.refs_13_
  55.3 1.0 copy.60.refs_4_.refs_14_
  56.4 0.4 convolution_compare_fusion
  56.8 0.8 fusion.47
  57.6 0.9 copy.61.refs_10_
  58.6 0.7 pad_maximum_fusion.4
  59.3 0.8 subtract_convert_fusion.refs_5_
  60.1 0.3 convolution_select_fusion
  60.4 1.0 add_reduce_fusion
  61.4 2.4 multiply_convert_fusion
  63.8 134.6 %attention_forward.1 = (bf16[8,128,128]{2,1,0:T(8,128)(2,1)}, f32[8,128,128]{2,1,0:T(8,128)}, f32[8,1,256]{2,1,0:T(1,128)}, bf16[128,1024]{1,0:T(8,128)(2,1)}, f...) custom-call(bf16[1024,1024]{1,0:T(8,128)(2,1)} %bitcast.52, ...), custom_call_target="tpu_custom_call" | custom-call | tf_op jit(solution)/shard_map/attention_forward/pallas_call | solution.py:499
  198.4 0.8 slice_bitcast_fusion.2
  199.2 0.6 pad_maximum_fusion.2.refs_15_
  199.9 0.7 broadcast_in_dim.38.refs_19_
  200.6 200.9 %experts_attention_backward.1 = (f32[128,1024]{1,0:T(8,128)}, bf16[8,128,256]{2,1,0:T(8,128)(2,1)}, bf16[16,80,1024]{2,1,0:T(8,128)(2,1)}, f32[2,192,1024]{2,1,0...) custom-call(bf16[128,1024]{1,0:T(8,128)(2,1)} %get-tuple-element.40., ...), custom_call_target="tpu_custom_call" | custom-call | tf_op jit(solution)/shard_map/experts_attention_backward/pallas_call | solution.py:1147
  401.5 1.2 multiply_reduce_fusion
  402.7 1.4 slice_bitcast_fusion
  404.1 0.9 fusion.48
  405.0 1.9 slice.61
  406.9 2.2 fusion.46
  409.1 0.5 convert_divide_fusion
  409.6 0.6 slice_reduce_fusion
  410.3 0.1 reshape.259
  410.4 0.7 reshape.260
  411.0 1.5 fusion.10
  412.6 1.2 fusion.1
  413.8 1.3 copy.65
  415.2 3.8 fusion.3
  419.1 0.6 pad_maximum_fusion.3
  419.7 0.9 fusion.7
  420.7 0.6 copy.74
  (57 shorter events, 0.5 us)
Async XLA Ops:
  7.2 192.7 %all-gather.3.cloned.1.call-start = ((), (), s32[]{:S(2)}) async-start(), calls=%async_computation | async-start | bytes 7077888 | tf_op jit(solution)/shard_map/all_gather | solution.py:1265
  8.8 49.9 %copy-start.5 = (bf16[8,8,64]{2,0,1:T(8,128)(2,1)}, bf16[8,8,64]{2,0,1:T(8,128)(2,1)S(1)}, u32[]{:S(2)}) copy-start(bf16[8,8,64]{2,0,1:T(8,128)(2,1)S(1)} %copy.55) | copy-start | bytes 24580
  8.9 49.8 %copy-start.7 = (bf16[8,8,64]{2,0,1:T(8,128)(2,1)}, bf16[8,8,64]{2,0,1:T(8,128)(2,1)S(1)}, u32[]{:S(2)}) copy-start(bf16[8,8,64]{2,0,1:T(8,128)(2,1)S(1)} %copy.56) | copy-start | bytes 24580
  48.6 7.7 %copy-start.12 = (f32[128,8]{0,1:T(8,128)S(1)}, f32[128,8]{0,1:T(8,128)}, u32[]{:S(2)}) copy-start(f32[128,8]{0,1:T(8,128)} %param.20) | copy-start | bytes 12292
  48.6 7.7 %copy-start.13 = (s32[128,8]{0,1:T(8,128)S(1)}, s32[128,8]{0,1:T(8,128)}, u32[]{:S(2)}) copy-start(s32[128,8]{0,1:T(8,128)} %param.19) | copy-start | bytes 12292
  56.3 5.1 %copy-start.3 = (bf16[128,1024]{1,0:T(8,128)(2,1)S(1)}, bf16[128,1024]{1,0:T(8,128)(2,1)}, u32[]{:S(2)}) copy-start(bf16[128,1024]{1,0:T(8,128)(2,1)} %refs_3_.1) | copy-start | bytes 786436
  200.6 200.9 %copy-start.6 = (bf16[8,8,64]{2,0,1:T(8,128)(2,1)S(1)}, bf16[8,8,64]{2,0,1:T(8,128)(2,1)}, u32[]{:S(2)}) copy-start(bf16[8,8,64]{2,0,1:T(8,128)(2,1)} %copy-done.5) | copy-start | bytes 24580
  200.6 200.9 %copy-start.8 = (bf16[8,8,64]{2,0,1:T(8,128)(2,1)S(1)}, bf16[8,8,64]{2,0,1:T(8,128)(2,1)}, u32[]{:S(2)}) copy-start(bf16[8,8,64]{2,0,1:T(8,128)(2,1)} %copy-done.7) | copy-start | bytes 24580
  401.5 7.7 %copy-start.15 = (bf16[8]{0:T(256)(128)(2,1)S(1)}, bf16[8]{0:T(256)(128)(2,1)}, u32[]{:S(2)}) copy-start(bf16[8]{0:T(256)(128)(2,1)} %param.12) | copy-start | bytes 52
  401.5 8.2 %copy-start.14 = (f32[8,128]{1,0:T(8,128)S(1)}, f32[8,128]{1,0:T(8,128)}, u32[]{:S(2)}) copy-start(f32[8,128]{1,0:T(8,128)} %get-tuple-element.56) | copy-start | bytes 12292
  401.5 9.6 %copy-start = (bf16[16,80,1024]{2,1,0:T(8,128)(2,1)S(1)}, bf16[16,80,1024]{2,1,0:T(8,128)(2,1)}, u32[]{:S(2)}) copy-start(bf16[16,80,1024]{2,1,0:T(8,128)(2,1)} %get-tuple-element.51) | copy-start | bytes 7864324
  411.0 1.6 copy-start.2
  412.6 2.6 copy-start.1
  415.2 3.9 copy-start.9
  415.2 3.9 copy-start.10
  415.2 4.5 %copy-start.4 = (f32[128,1024]{1,0:T(8,128)S(1)}, f32[128,1024]{1,0:T(8,128)}, u32[]{:S(2)}) copy-start(f32[128,1024]{1,0:T(8,128)} %get-tuple-element.52) | copy-start | bytes 1572868
  415.2 5.5 %copy-start.11 = (f32[8,1024]{1,0:T(8,128)S(1)}, f32[8,1024]{1,0:T(8,128)}, u32[]{:S(2)}) copy-start(f32[8,1024]{1,0:T(8,128)} %get-tuple-element.104) | copy-start | bytes 98308
Sparse Core Ops, SparseCore 0:
  48.7 121.9 all-gather.2

commit v5 on v4

--- a/solution.py
+++ b/solution.py
@@ -27,6 +27,7 @@
 SUPER = TOK_DEV * N_SHARD
 BWD_TILE = 1024
 LIMIT = 63
+STAGE = 3
 
 epsilon = 1e-06
 rope_base = 10000.0
@@ -238,12 +239,12 @@
 
 def attention_kernel(*refs):
     (x_ref, cols_ref, gain_ref, cos_ref, sin_ref, turn_ref, slab_ref, rows_ref) = refs[:8]
-    (own_ref, gain2_ref, pickt_ref, cot_ref) = refs[8:12]
-    (q_ref, wide_ref, lse_ref, attp_ref, res_ref) = refs[12:17]
-    (norm_ref, mem_ref, rows_out, ow_ref, land_ref, cot_out) = refs[17:23]
-    (land, vt, heads, peak_ref, total_ref, acc_ref, att, ow, weights_ref, norm, rows) = refs[23:34]
-    (ksend, krecv, gsend, grecv, esend, erecv, fsend, frecv, hsend, hrecv, own, msem) = refs[34:46]
-    dsend, drecv = refs[46:]
+    (own_ref, gain2_ref, pickt_ref, cot_ref, pack_ref) = refs[8:13]
+    (q_ref, wide_ref, lse_ref, attp_ref, res_ref) = refs[13:18]
+    (norm_ref, mem_ref, rows_out, ow_ref, land_ref, cot_out, pack_out) = refs[18:25]
+    (land, vt, heads, peak_ref, total_ref, acc_ref, att, ow, weights_ref, norm, rows) = refs[25:36]
+    (ksend, krecv, gsend, grecv, esend, erecv, fsend, frecv, hsend, hrecv, own, msem) = refs[36:48]
+    dsend, drecv, psend, precv = refs[48:]
     seq = lax.axis_index("seq")
     me = lax.axis_index("shard")
     core = lax.rem(me, 2)
@@ -303,6 +304,11 @@
         source = slab_ref if n == 0 else ow.at[block]
         return transfer(source, ow.at[block], fsend.at[n, k], frecv.at[n, k], "seq", peer)
 
+    def pack_to_ring(n, k, block, peer):
+        target = pack_out.at[block] if n == 0 else pack_out.at[block, n - 1]
+        source = pack_ref if n == 0 else target
+        return transfer(source, target, psend.at[n, k], precv.at[n, k], "seq", peer)
+
     def grads_to_expert(k):
         peer = lax.rem(me + k, N_SHARD)
         return transfer(
@@ -324,7 +330,7 @@
     greet(everyone(seq, me))
 
     for half in range(2):
-        block = cols_ref[...].astype(f32).reshape(N_SHARD, N_SEQ, 2, 8, 128)[:, :, half]
+        block = cols_ref[:, :N_SEQ].astype(f32).reshape(N_SHARD, N_SEQ, 2, 8, 128)[:, :, half]
         block = jnp.swapaxes(block, 0, 1).reshape(WIDTH, 128).astype(bf16)
         weights_ref[:, 128 * half : 128 * half + 128] = block
     weights_ref[:, COLS:] = dot(weights_ref[:, :COLS], turn_ref[...], NN).astype(bf16)
@@ -370,6 +376,11 @@
     slab_to_ring(0, 0, seq, partner).start()
     for k in (1, 2, 3):
         slab_to_ring(0, k, seq, lax.rem(seq + 2 * k, N_SEQ)).start()
+    pack_to_ring(0, 0, seq, partner).start()
+    for k in (1, 2, 3):
+        pack_to_ring(0, k, seq, lax.rem(seq + 2 * k, N_SEQ)).start()
+    pack_own = pltpu.make_async_copy(pack_ref, pack_out.at[seq], own.at[5])
+    pack_own.start()
     rows_own = pltpu.make_async_copy(rows_ref, rows_out.at[me], own.at[0])
     rows_own.start()
     slab_own = pltpu.make_async_copy(slab_ref, ow.at[seq], own.at[1])
@@ -404,6 +415,12 @@
             for k in (1, 2, 3):
                 slab_to_ring(1, k, partner, lax.rem(seq + 2 * k, N_SEQ)).start()
 
+        @pl.when(t == STAGE)
+        def _():
+            pack_to_ring(0, 0, partner, partner).wait_recv()
+            for k in (1, 2, 3):
+                pack_to_ring(1, k, partner, lax.rem(seq + 2 * k, N_SEQ)).start()
+
         @pl.when(t + 1 < N_SEQ)
         def _():
             third(t + 1)
@@ -426,11 +443,19 @@
         def _():
             to_token(t, seq).start()
 
-        def rest(i, inner):
-            peak_ref[i], total_ref[i], acc_ref[i] = tile(t, i, False)
+        def rest(n, inner):
+            i = t + 1 + 2 * n
+            first, other = tile(t, i, False), tile(t, i + 1, False)
+            peak_ref[i], total_ref[i], acc_ref[i] = first
+            peak_ref[i + 1], total_ref[i + 1], acc_ref[i + 1] = other
             return inner
 
-        lax.fori_loop(t + 1, N_SEQ, rest, 0)
+        lax.fori_loop(0, (N_SEQ - 1 - t) // 2, rest, 0)
+
+        @pl.when(lax.rem(t, 2) == 0)
+        def _():
+            last = N_SEQ - 1
+            peak_ref[last], total_ref[last], acc_ref[last] = tile(t, last, False)
 
         @pl.when(t + 1 < N_SEQ)
         def _():
@@ -439,6 +464,8 @@
         return carry
 
     lax.fori_loop(0, N_SEQ, step, 0)
+    for k in (1, 2, 3):
+        pack_to_ring(2, k, partner, lax.rem(seq + 2 * k, N_SEQ)).start()
     slab_own.wait()
     for k in (1, 2, 3):
         for n, block in enumerate((seq, partner)):
@@ -482,6 +509,13 @@
         to_expert(k).wait()
     mine.wait()
     cot_own.wait()
+    pack_own.wait()
+    pack_to_ring(0, 0, seq, partner).wait_send()
+    for k in (1, 2, 3):
+        for n, block in enumerate((seq, partner, partner)):
+            pack_to_ring(n, k, block, lax.rem(seq + 2 * k, N_SEQ)).wait_send()
+            source = lax.rem(block + N_SEQ - 2 * k, N_SEQ)
+            pack_to_ring(n, k, source, lax.rem(seq + N_SEQ - 2 * k, N_SEQ)).wait_recv()
 
     def end(t, carry):
         for m in range(15):
@@ -498,8 +532,8 @@
     shards = (N_SHARD - 1,)
     return pl.pallas_call(
         attention_kernel,
-        in_specs=[vmem] * 6 + [ANY] * 2 + [vmem] * 3 + [ANY],
-        out_specs=[vmem] * 5 + [ANY] * 6,
+        in_specs=[vmem] * 6 + [ANY] * 2 + [vmem] * 3 + [ANY] * 2,
+        out_specs=[vmem] * 5 + [ANY] * 7,
         out_shape=[
             jax.ShapeDtypeStruct((N_SEQ, TOK_DEV, 2 * HEAD), bf16),
             jax.ShapeDtypeStruct((N_SEQ, 2 * HEAD, TOK_DEV), f32),
@@ -512,6 +546,7 @@
             jax.ShapeDtypeStruct((N_SEQ, 128, WIDTH), bf16),
             jax.ShapeDtypeStruct((N_SHARD, 80, WIDTH), bf16),
             jax.ShapeDtypeStruct((N_SHARD, 80, WIDTH), bf16),
+            jax.ShapeDtypeStruct((N_SEQ, LOCAL_EXPERTS, 192, WIDTH), bf16),
         ],
         scratch_shapes=[
             pltpu.VMEM((N_SEQ, N_SHARD, TOK_DEV, 2 * HEAD), bf16),
@@ -535,10 +570,12 @@
             dma((2, 4)),
             dma(shards),
             dma(shards),
-            dma((5,)),
+            dma((6,)),
             dma((N_SEQ,)),
             dma(shards),
             dma(shards),
+            dma((3, 4)),
+            dma((3, 4)),
         ],
         compiler_params=pltpu.CompilerParams(
             collective_id=ident, has_side_effects=True, vmem_limit_bytes=56 << 20
@@ -556,11 +593,11 @@
     (gu, dn, land, rows, returned, xt, ht, hg, gm, mixed, dw, ags, xstage) = refs[29:42]
     (gl, qs, gs, delta_ref, kt, acc, dq, stage, dl) = refs[42:51]
     (mbuf, pg, qp, qstage, qland, qsum, osum, xland, oland, mstage, mland) = refs[51:62]
-    cland, cstage, oseq = refs[62:65]
-    (wsem, isend, irecv, ksend, krecv, psend, precv) = refs[65:72]
-    (dsend, drecv, osend, orecv, jsend, jrecv, nsend, nrecv, own) = refs[72:81]
-    (msem, asend, arecv, bsend, brecv, xsend, xrecv, csend, crecv, tsend, trecv) = refs[81:92]
-    (usend, urecv, fsend, frecv) = refs[92:]
+    cland, cstage, oseq, hid = refs[62:66]
+    (wsem, isend, irecv, ksend, krecv, psend, precv) = refs[66:73]
+    (dsend, drecv, osend, orecv, jsend, jrecv, nsend, nrecv, own) = refs[73:82]
+    (msem, asend, arecv, bsend, brecv, xsend, xrecv, csend, crecv, tsend, trecv) = refs[82:93]
+    (usend, urecv, fsend, frecv) = refs[93:]
     seq = lax.axis_index("seq")
     me = lax.axis_index("shard")
     ring = seq // 2
@@ -569,10 +606,10 @@
     def weights(e, s):
         return (
             pltpu.make_async_copy(
-                w_ref.at[e, s, :128], gu.at[e, 128 * s : 128 * s + 128], wsem.at[e, s, 0]
+                w_ref.at[s, e, :128], gu.at[e, 128 * s : 128 * s + 128], wsem.at[e, s, 0]
             ),
             pltpu.make_async_copy(
-                w_ref.at[e, s, 128:], dn.at[e, 64 * s : 64 * s + 64], wsem.at[e, s, 1]
+                w_ref.at[s, e, 128:], dn.at[e, 64 * s : 64 * s + 64], wsem.at[e, s, 1]
             ),
         )
 
@@ -592,10 +629,12 @@
             peer,
         )
 
-    def to_token_expert(k):
-        peer = lax.rem(me + k, N_SHARD)
-        return transfer(
-            land.at[peer], came_ref.at[me], jsend.at[k - 1], jrecv.at[k - 1], "shard", peer
+    def to_token_expert(n):
+        m = (n + 1) % 8
+        pair = lax.rem(me // 2 % 2 + (n + 1) // 8, 2)
+        peer = lax.rem(me // 4 + m // 2, 4) * 4 + pair * 2 + lax.rem(me + m, 2)
+        return transfer(
+            land.at[peer], came_ref.at[me], jsend.at[n], jrecv.at[n], "shard", peer
         )
 
     def to_ring(e, k):
@@ -604,9 +643,24 @@
             dw.at[e, k], kz_ref.at[e, k - 1], ksend.at[e, k - 1], krecv.at[e, k - 1], "seq", peer
         )
 
-    def out_to_shard(k, block, source, peer):
-        return transfer(
-            rows.at[flat(block, 0, 64)], oland.at[source], psend.at[k - 1], precv.at[k - 1], "shard", peer
+    def out_to_core(q):
+        return transfer(
+            rows.at[flat(2 * q + 1 - me % 2, 0, 64)],
+            oland.at[q],
+            psend.at[q],
+            precv.at[q],
+            "shard",
+            me + 1 - 2 * (me % 2),
+        )
+
+    def out_to_chip(k, block, source, peer):
+        return transfer(
+            rows.at[flat(2 * block + me % 2, 0, 64)],
+            oland.at[8 + source],
+            psend.at[7 + k],
+            precv.at[7 + k],
+            "shard",
+            2 * peer + me % 2,
         )
 
     def to_head(p):
@@ -718,9 +772,8 @@
         up_grad = (units * act).astype(bf16)
         both = jnp.concatenate([gate_grad, up_grad], axis=1)
         hg[e, here, :] = both
-        xt[e, :, here] = x.T
-        ht[e, :, here] = hidden.T
-        return dot(hidden, dn[e], NN).astype(bf16), dot(both, gu[e], NT).astype(bf16)
+        hid[e, here, :] = hidden
+        return dot(both, gu[e], NT).astype(bf16)
 
     def run_expert(e, low):
         def aligned(n, carry):
@@ -728,8 +781,7 @@
             here = pl.ds(pl.multiple_of(n * 256, 256), 256)
             x = land[group, low : low + 32].reshape(256, WIDTH)
             g = gr_ref[group, low : low + 32].reshape(256, WIDTH)
-            out, back = expert(e, x, g, here)
-            land[group, low : low + 32] = out.reshape(8, 32, WIDTH)
+            back = expert(e, x, g, here)
             for m in range(8):
                 rows[flat(n * 8 + m, low, low + 32), :] = back[32 * m : 32 * m + 32]
             return carry
@@ -737,9 +789,24 @@
         lax.fori_loop(0, 2, aligned, 0)
         g = split(gr_ref[:, 32:48], e)
         gm[e] = g
-        out, back = expert(e, split(land[:, 32:48], e), g, slice(512, 640))
-        mixed[0, e] = out
-        mixed[1, e] = back
+        mixed[1, e] = expert(e, split(land[:, 32:48], e), g, slice(512, 640))
+
+    def finish_expert(e, low):
+        def aligned(n, carry):
+            group = pl.ds(n * 8, 8)
+            here = pl.ds(pl.multiple_of(n * 256, 256), 256)
+            hidden = hid[e, here, :]
+            xt[:, here] = land[group, low : low + 32].reshape(256, WIDTH).T
+            ht[:, here] = hidden.T
+            out = dot(hidden, dn[e], NN).astype(bf16)
+            land[group, low : low + 32] = out.reshape(8, 32, WIDTH)
+            return carry
+
+        lax.fori_loop(0, 2, aligned, 0)
+        hidden = hid[e, 512:, :]
+        xt[:, 512:] = split(land[:, 32:48], e).T
+        ht[:, 512:] = hidden.T
+        mixed[0, e] = dot(hidden, dn[e], NN).astype(bf16)
 
     def expert_grads(e):
         low = 48 * e
@@ -747,9 +814,9 @@
         def block(h, carry):
             features = pl.ds(pl.multiple_of(h * 512, 512), 512)
             units = pl.ds(pl.multiple_of(h * 256, 256), 256)
-            grad = dot(xt[e, features, :], hg[e], NN).astype(bf16)
-            part = dot(ht[e, units, :512], gr_ref[:, low : low + 32].reshape(512, WIDTH), NN)
-            part = (part + dot(ht[e, units, 512:], gm[e], NN)).astype(bf16)
+            grad = dot(xt[features, :], hg[e], NN).astype(bf16)
+            part = dot(ht[units, :512], gr_ref[:, low : low + 32].reshape(512, WIDTH), NN)
+            part = (part + dot(ht[units, 512:], gm[e], NN)).astype(bf16)
             for m in range(4):
                 k = lax.rem(2 * h + m // 2 + 4 - ring, 4)
                 n = lax.rem(m + far, 2)
@@ -772,7 +839,6 @@
     for k in (1, 2, 3):
         slab_to_ring(1, k, partner, lax.rem(seq + 2 * k, N_SEQ)).start()
     run_expert(1, 48)
-    land[:, 32:48] = join(mixed[0, 0], mixed[0, 1])
     joined = join(mixed[1, 0], mixed[1, 1])
     for n in range(N_SHARD):
         rows[80 * n + 32 : 80 * n + 48, :] = joined[n]
@@ -784,15 +850,20 @@
     normed_copy.start()
     ow_copy = pltpu.make_async_copy(ow_ref, gu.at[1], own.at[0])
     ow_copy.start()
+    finish_expert(0, 0)
     expert_grads(0)
     for k in (1, 3):
         to_ring(0, k).start()
+    finish_expert(1, 48)
+    land[:, 32:48] = join(mixed[0, 0], mixed[0, 1])
     expert_grads(1)
 
     for part in range(2):
         for k in range(1, N_SHARD):
             source = lax.rem(me + N_SHARD - k, N_SHARD)
             to_source(part, k, source, source, source).wait_recv()
+    for n in range(7):
+        to_token_expert(n).start()
     moe_in_grad = dot(pick_ref[...], returned[...], NN)
     residual = res_ref[...]
     inverse = lax.rsqrt(jnp.mean(residual * residual, axis=1, keepdims=True) + epsilon)
@@ -828,10 +899,8 @@
     for k in (1, 3, 2):
         to_ring(1, k).start()
     to_ring(0, 2).start()
-    for k in range(1, N_SHARD):
-        peer = lax.rem(me + k, N_SHARD)
-        out_to_shard(k, peer, me, peer).start()
-    oland[me] = rows[flat(me, 0, 64), :]
+    for q in range(N_SHARD // 2):
+        out_to_core(q).start()
     came_own = pltpu.make_async_copy(land.at[me], came_ref.at[me], own.at[0])
     came_own.start()
     fetch(0).start()
@@ -911,10 +980,23 @@
         tokens = pl.ds(pl.multiple_of(t * 128, 128), 128)
         qp[...] += dot(gu[0, tokens, :].T, grad, NN)
 
+    def out_chips():
+        for q in range(N_SHARD // 2):
+            out_to_core(q).wait_recv()
+            here = flat(2 * q + core, 0, 64)
+            total = rows[here, :].astype(f32) + oland[q].astype(f32)
+            rows[here, :] = total.astype(bf16)
+        oland[8 + chip] = rows[flat(me, 0, 64), :]
+        for k in range(1, N_SHARD // 2):
+            peer = lax.rem(chip + k, N_SHARD // 2)
+            out_to_chip(k, peer, chip, peer).start()
+
     def sum_weights():
-        for k in range(1, N_SHARD):
-            peer = lax.rem(me + k, N_SHARD)
-            out_to_shard(k, peer, me, peer).wait_send()
+        for q in range(N_SHARD // 2):
+            out_to_core(q).wait_send()
+        for k in range(1, N_SHARD // 2):
+            peer = lax.rem(chip + k, N_SHARD // 2)
+            out_to_chip(k, peer, chip, peer).wait_send()
         for e in range(LOCAL_EXPERTS):
             for k in (1, 2, 3):
                 to_ring(e, k).wait()
@@ -944,10 +1026,10 @@
                 else:
                     xstage[e] = total.astype(bf16)
         to_pair.start()
-        for k in range(1, N_SHARD):
-            source = lax.rem(me + N_SHARD - k, N_SHARD)
-            out_to_shard(k, source, source, source).wait_recv()
-        osum[...] = jnp.sum(oland[...].astype(f32), axis=0).reshape(N_SEQ, 8, WIDTH)
+        for k in range(1, N_SHARD // 2):
+            source = lax.rem(chip + N_SHARD // 2 - k, N_SHARD // 2)
+            out_to_chip(k, source, source, source).wait_recv()
+        osum[...] = jnp.sum(oland[8:].astype(f32), axis=0).reshape(N_SEQ, 8, WIDTH)
         for p in range(N_SEQ):
 
             @pl.when(seq != p)
@@ -975,8 +1057,11 @@
 
             @pl.when(t == n + 1)
             def _(n=n):
-                for k in range(1, 4):
-                    to_token_expert(3 * n + k).start()
+                if n < 4:
+                    to_token_expert(7 + 2 * n).start()
+                    to_token_expert(8 + 2 * n).start()
+                if n == 0:
+                    out_chips()
 
         @pl.when(t == N_SEQ - 2)
         def _():
@@ -1062,7 +1147,7 @@
             out_to_seq(p).wait_send()
 
     for k in range(1, N_SHARD):
-        to_token_expert(k).wait()
+        to_token_expert(k - 1).wait()
         peer = lax.rem(me + k, N_SHARD)
         qkv_to_shard(k, peer, me, peer).wait_send()
         gain_to_shard(k, peer, me, peer).wait_send()
@@ -1104,8 +1189,8 @@
         (routed, bf16),
         ((N_SHARD * 80, WIDTH), bf16),
         ((N_SHARD * 80, WIDTH), bf16),
-        ((LOCAL_EXPERTS, WIDTH, EXPERT_ROWS), bf16),
-        ((LOCAL_EXPERTS, FF, EXPERT_ROWS), bf16),
+        ((WIDTH, EXPERT_ROWS), bf16),
+        ((FF, EXPERT_ROWS), bf16),
         ((LOCAL_EXPERTS, EXPERT_ROWS, 2 * FF), bf16),
         ((LOCAL_EXPERTS, 128, WIDTH), bf16),
         ((2, LOCAL_EXPERTS, 128, WIDTH), bf16),
@@ -1135,6 +1220,7 @@
         ((4, N_SHARD // 2, TOK_DEV, 2 * HEAD), bf16),
         ((4, N_SHARD // 2, TOK_DEV, 2 * HEAD), bf16),
         ((N_SEQ, 8, WIDTH), f32),
+        ((LOCAL_EXPERTS, EXPERT_ROWS, FF), bf16),
     ]
     shards = (N_SHARD - 1,)
     counts = [(LOCAL_EXPERTS, N_SEQ, 2)]
@@ -1262,9 +1348,6 @@
     expert_pack = jnp.concatenate(
         [jnp.concatenate([w_gate, w_up], axis=2), w_down], axis=1
     )
-    expert_weights = lax.all_gather(
-        lax.optimization_barrier((expert_pack, tokens))[0], "seq", axis=1
-    )
     gain_rows = columns[:, N_SEQ, :8, :16].transpose(1, 0, 2)
     gain_attn = gain_rows[:, :, :8].reshape(WIDTH).astype(f32)
     gain_moe = gain_rows[:, :, 8:].reshape(WIDTH).astype(f32)
@@ -1282,10 +1365,11 @@
         out_weight,
         expert_rows,
         grad_rows,
+        expert_weights,
     ) = attention(
         (
             tokens.reshape(HEAD_ROWS, WIDTH),
-            columns[:, :N_SEQ],
+            columns,
             gain_attn[None, :],
             cosine,
             sine,
@@ -1296,6 +1380,7 @@
             gain_moe[None, :],
             pick_turned,
             grad_send.reshape(N_SHARD, 80, WIDTH),
+            expert_pack,
         ),
         2,
     )

time: 429 us -> 411 us (0.958)
  between operations: 14.4 us -> 1.01 us
  local copies, waits for them, and re-layouts: 20.1 us -> 15.4 us
    pallas_call x1, Pallas kernels: 201 us -> 208 us  [late(): pl.pallas_call(late_kernel, in_specs=[vmem, ANY] + [vmem] * 4 + [ANY, vme...]
    pallas_call x1, Pallas kernels: 135 us -> 129 us  [attention(): pl.pallas_call(attention_kernel, in_specs=[vmem] * 6 + [ANY] * 2 + [vmem]...]
  transfers between devices with their start and end apart: 1 -> 0, of which waited for: 0 -> 0; matrix products, arithmetic and copies ran while one was open for 4% -> 0% of each run, Pallas kernels for 31% -> 0%
where the time goes in v5:
time: 411 us
  Pallas kernels  373 us (91%)
  local copies, waits for them, and re-layouts  15.4 us (4%)
  matrix products  11.6 us (3%)
  other arithmetic  9.58 us (2%)
    pallas_call x1, Pallas kernels, late(): pl.pallas_call(late_kernel, in_specs=[vmem, ANY] + [vmem] * 4 + [ANY, vme...  208 us
    pallas_call x1, Pallas kernels, attention(): pl.pallas_call(attention_kernel, in_specs=[vmem] * 6 + [ANY] * 2 + [vmem]...  129 us
    pallas_call x1, Pallas kernels, first_gather(): pl.pallas_call(first_kernel, out_shape=[jax.ShapeDtypeStruct((N_SEQ, 8, T...  36.1 us
    dot_general x7, matrix products, dot(): return lax.dot_general(left, right, dims, preferred_element_type=f32)  11.6 us

profile of v5, /device:TPU:1, one launch (start us, length us, event | category | flops | bytes accessed | tf_op | source)
XLA Modules:
  0.0 410.6 jit_solution(8724014825476495076)
XLA Ops:
  0.7 0.8 pad_maximum_fusion.5
  1.5 0.7 slice_bitcast_fusion.3
  2.3 0.7 fusion.49
  3.0 0.1 reshape.245
  3.1 0.1 reshape.246
  3.2 0.1 fusion.57
  3.3 0.6 pad_maximum_fusion.1.w_ref
  4.0 0.7 pad_maximum_fusion.4
  4.7 0.7 select_reduce_fusion
  5.4 0.1 subtract_convert_fusion.refs_5_
  5.5 0.1 slice_bitcast_fusion.2
  5.6 0.6 pad_maximum_fusion.2.refs_15_
  6.3 0.4 convolution_compare_fusion
  6.7 0.5 multiply_sine_fusion
  7.3 1.0 copy.59.refs_3_.refs_13_
  8.4 1.0 copy.60.refs_4_.refs_14_
  9.4 0.3 convolution_select_fusion
  9.7 1.0 add_reduce_fusion
  10.7 0.8 fusion.47
  11.5 0.9 copy.61.refs_10_
  12.4 1.0 pad_maximum_fusion.refs_12_.refs_18_
  13.4 2.4 multiply_convert_fusion
  15.8 36.1 %gather_tokens.1 = (bf16[8,8,16,1024]{3,2,1,0:T(8,128)(2,1)}, bf16[16,9,16,128]{3,2,1,0:T(8,128)(2,1)}, bf16[16,8,1024]{2,1,0:T(8,128)(2,1)}) custom-call(bf16[8,16,1024]{2,1,0:T(8,128)(2,1)} %bitcast.46, bf16[8,32,128]{2,1,0:T(8,128)(2,1)} %pad_maximum_fusion.1.w_ref, bf16[8,1024]{1,0:T(8,128)(2,1)} %v_ref.1), custom_call_target="tpu_custom_call" | custom-call | tf_op jit(solution)/shard_map/gather_tokens/pallas_call | solution.py:182
  51.9 0.8 slice_bitcast_fusion.1
  52.6 0.1 slice_convert_fusion
  52.7 0.7 reshape.262.refs_9_.refs_4_
  53.4 0.1 reshape.263
  53.5 0.1 dynamic_slice.3
  53.6 0.7 broadcast_in_dim.38.refs_19_
  54.3 0.7 reshape.264
  55.0 0.7 reshape.261.refs_2_
  55.7 128.5 %attention_forward.1 = (bf16[8,128,128]{2,1,0:T(8,128)(2,1)}, f32[8,128,128]{2,1,0:T(8,128)}, f32[8,1,256]{2,1,0:T(1,128)}, bf16[128,1024]{1,0:T(8,128)(2,1)}, f...) custom-call(bf16[1024,1024]{1,0:T(8,128)(2,1)} %bitcast.47, ...), custom_call_target="tpu_custom_call" | custom-call | tf_op jit(solution)/shard_map/attention_forward/pallas_call | solution.py:533
  184.2 208.4 %experts_attention_backward.1 = (f32[128,1024]{1,0:T(8,128)}, bf16[8,128,256]{2,1,0:T(8,128)(2,1)}, bf16[16,80,1024]{2,1,0:T(8,128)(2,1)}, f32[2,192,1024]{2,1,0...) custom-call(bf16[128,1024]{1,0:T(8,128)(2,1)} %get-tuple-element.40., ...), custom_call_target="tpu_custom_call" | custom-call | tf_op jit(solution)/shard_map/experts_attention_backward/pallas_call | solution.py:1233
  392.7 1.2 multiply_reduce_fusion
  393.9 0.5 convert_divide_fusion
  394.4 1.3 slice_reduce_fusion
  395.7 0.8 slice_bitcast_fusion
  396.5 0.9 fusion.48
  397.4 0.1 reshape.259
  397.6 0.6 pad_maximum_fusion.3
  398.2 2.4 fusion.10
  400.6 1.2 fusion.1
  401.8 1.3 copy.65
  403.2 3.9 fusion.3
  407.2 0.9 fusion.7
  408.1 0.8 slice.57
  408.9 1.1 fusion.46
  410.0 0.6 copy.74
  (55 shorter events, 0.5 us)
Async XLA Ops:
  3.1 2.5 copy-start.7
  3.2 2.4 copy-start.9
  5.5 4.1 %copy-start.5 = (bf16[256,256]{1,0:T(8,128)(2,1)}, bf16[256,256]{1,0:T(8,128)(2,1)S(1)}, u32[]{:S(2)}) copy-start(bf16[256,256]{1,0:T(8,128)(2,1)S(1)} %subtract_convert_fusion.refs_5_) | copy-start | bytes 393220
  8.3 4.1 copy-start.11
  8.3 4.1 copy-start.12
  8.3 4.1 copy-start.13
  9.4 4.0 copy-start.4
  184.2 208.5 %copy-start.8 = (bf16[8,8,64]{2,0,1:T(8,128)(2,1)S(1)}, bf16[8,8,64]{2,0,1:T(8,128)(2,1)}, u32[]{:S(2)}) copy-start(bf16[8,8,64]{2,0,1:T(8,128)(2,1)} %copy-done.7) | copy-start | bytes 24580
  184.2 208.5 %copy-start.10 = (bf16[8,8,64]{2,0,1:T(8,128)(2,1)S(1)}, bf16[8,8,64]{2,0,1:T(8,128)(2,1)}, u32[]{:S(2)}) copy-start(bf16[8,8,64]{2,0,1:T(8,128)(2,1)} %copy-done.9) | copy-start | bytes 24580
  184.2 209.7 %copy-start.16 = (bf16[8]{0:T(256)(128)(2,1)S(1)}, bf16[8]{0:T(256)(128)(2,1)}, u32[]{:S(2)}) copy-start(bf16[8]{0:T(256)(128)(2,1)} %param.12) | copy-start | bytes 52
  392.7 7.9 %copy-start = (bf16[16,80,1024]{2,1,0:T(8,128)(2,1)S(1)}, bf16[16,80,1024]{2,1,0:T(8,128)(2,1)}, u32[]{:S(2)}) copy-start(bf16[16,80,1024]{2,1,0:T(8,128)(2,1)} %get-tuple-element.51) | copy-start | bytes 7864324
  397.6 3.0 copy-start.2
  400.6 2.6 copy-start.1
  400.6 2.6 copy-start.15
  403.2 4.0 copy-start.6
  403.2 4.9 %copy-start.3 = (f32[2,192,1024]{2,1,0:T(8,128)S(1)}, f32[2,192,1024]{2,1,0:T(8,128)}, u32[]{:S(2)}) copy-start(f32[2,192,1024]{2,1,0:T(8,128)} %get-tuple-element.58) | copy-start | bytes 4718596
  407.1 2.9 copy-start.14
